TPU v7x, 128 devices: a whole 4x4x4 slice. The times are simulated.
128 devices in a mesh: heads: 4 (over x), ctx: 32 (over z, y, core).
Axes of the slice: x: 4, y: 4, z: 4, core: 2. Of those that a mesh axis runs over, the one named last changes fastest.
Arguments:
- queries: bfloat16 [16384, 1536], P('ctx', 'heads'), may hold values from -8 to 8
- key_rows: bfloat16 [16384, 1536], P('ctx', 'heads'), may hold values from -8 to 8
- value_rows: bfloat16 [16384, 1536], P('ctx', 'heads'), may hold values from -6 to 6
- out_weight: bfloat16 [1536, 3072], P('heads'), may hold values from -0.15625 to 0.15625
- tile_masks: int32 [2, 128, 128], replicated, may hold values from 0 to 1, as said below
- head_pattern: int32 [12], P('heads'), may hold values from 0 to 1
Outputs:
- mixed: bfloat16 [16384, 3072], P('ctx', 'heads')
Inputs may be any that keep to these rules, and one draw needn't show every extreme that they name: tile_masks[k, i, i] = 1 for every pattern k and tile i.
All inputs are finite; a program needn't handle non-finite values.
Results may differ from a plain program's by a relative error of at most 0.015.
Values may be sent and summed in bfloat16 or wider, within the bound.
A program may use at most 128 MiB of HBM per device.

v0:
```python
import math

import jax
import jax.numpy as jnp
from jax import lax
from jax.sharding import PartitionSpec as P

DH = 128
TILE = 128
SPATIAL = 512


def to_spatial(moved, row_count, columns):
    return moved.transpose(1, 0, 2).reshape(row_count, columns)


def body(queries, key_rows, value_rows, out_weight, tile_masks, head_pattern):
    ctx_count = lax.axis_size("ctx")
    row_count = queries.shape[0]
    columns = queries.shape[1]
    local_heads = columns // DH
    frame_count = row_count * ctx_count // SPATIAL
    local_frames = row_count // SPATIAL
    local_spots = SPATIAL // ctx_count
    local_tiles = row_count // TILE
    tile_total = tile_masks.shape[1]
    blocks = tuple(
        (field.reshape(local_frames, SPATIAL, columns) for field in (queries, key_rows, value_rows))
    )
    moved = (
        lax.all_to_all(blocks[0], "ctx", split_axis=1, concat_axis=0, tiled=True),
        lax.all_to_all(blocks[1], "ctx", split_axis=1, concat_axis=0, tiled=True),
        lax.all_to_all(blocks[2], "ctx", split_axis=1, concat_axis=0, tiled=True),
    )
    query_s = to_spatial(moved[0], row_count, columns)
    key_side = to_spatial(moved[1], row_count, columns)
    value_side = to_spatial(moved[2], row_count, columns)

    def tile_of(positions):
        return positions // TILE

    pattern_masks = jnp.where(
        (head_pattern == 0)[:, None, None], tile_masks[0][None], tile_masks[1][None]
    )
    first_tile = lax.axis_index("ctx") * local_tiles
    own_masks = lax.dynamic_slice_in_dim(pattern_masks, first_tile, local_tiles, 1).astype(
        jnp.float32
    )
    query_tiles = query_s.reshape(local_tiles, TILE, local_heads, DH)
    tile_ids = jnp.arange(tile_total, dtype=jnp.int32)

    def attend(state_now, key_piece, value_piece, first_row):
        running_max, totals, weighted = state_now
        piece_len = key_piece.shape[0]
        positions = first_row + jnp.arange(piece_len, dtype=jnp.int32)
        one_hot = (tile_of(positions)[:, None] == tile_ids[None, :]).astype(jnp.float32)
        hits = jnp.einsum("htj,kj->htk", own_masks, one_hot)
        allowed = (hits > 0.5)[:, :, None, :]
        scores = jnp.einsum(
            "tqhd,khd->htqk",
            query_tiles,
            key_piece.reshape(piece_len, local_heads, DH),
            preferred_element_type=jnp.float32,
        ) / math.sqrt(DH)
        block_max = jnp.max(jnp.where(allowed, scores, jnp.float32(-1e30)), axis=-1)
        new_max = jnp.maximum(running_max, block_max)
        weights = jnp.where(allowed, jnp.exp(scores - new_max[..., None]), jnp.float32(0.0))
        factor = jnp.exp(running_max - new_max)
        totals = totals * factor + jnp.sum(weights, axis=-1)
        update = jnp.einsum(
            "htqk,khd->htqd",
            weights.astype(jnp.bfloat16),
            value_piece.reshape(piece_len, local_heads, DH),
            preferred_element_type=jnp.float32,
        )
        weighted = weighted * factor[..., None] + update
        return (new_max, totals, weighted)

    start_state = (
        jnp.full((local_heads, local_tiles, TILE), -1e30, jnp.float32),
        jnp.zeros((local_heads, local_tiles, TILE), jnp.float32),
        jnp.zeros((local_heads, local_tiles, TILE, DH), jnp.float32),
    )
    key_piece = lax.all_gather(key_side, "ctx", axis=0, tiled=True)
    value_piece = lax.all_gather(value_side, "ctx", axis=0, tiled=True)
    piece_len = key_piece.shape[0]
    step_rows = 512
    key_steps = key_piece.reshape(piece_len // step_rows, step_rows, columns)
    value_steps = value_piece.reshape(piece_len // step_rows, step_rows, columns)
    offsets = step_rows * jnp.arange(piece_len // step_rows, dtype=jnp.int32)

    def one_step(inner_state, inputs):
        return (attend(inner_state, inputs[0], inputs[1], inputs[2]), None)

    final_state, unused = lax.scan(one_step, start_state, (key_steps, value_steps, offsets))
    running_max, totals, weighted = final_state
    attn_s = (weighted / totals[..., None]).astype(jnp.bfloat16).reshape(local_heads, row_count, DH)
    attn_s = attn_s.transpose(1, 0, 2).reshape(local_spots, frame_count, columns).transpose(1, 0, 2)
    attn = lax.all_to_all(attn_s, "ctx", split_axis=0, concat_axis=1, tiled=True).reshape(
        row_count, columns
    )
    partial_sum = jnp.dot(attn, out_weight, preferred_element_type=jnp.float32)
    return lax.psum_scatter(
        partial_sum.astype(jnp.bfloat16), "heads", scatter_dimension=1, tiled=True
    )


def solution(mesh):
    placed = (
        P("ctx", "heads"),
        P("ctx", "heads"),
        P("ctx", "heads"),
        P("heads", None),
        P(),
        P("heads"),
    )
    return jax.shard_map(
        body, mesh=mesh, in_specs=placed, out_specs=P("ctx", "heads"), check_vma=False
    )
```

profile of v0, /device:TPU:1, one launch (start us, length us, event | category | flops | bytes accessed | tf_op | source)
XLA Modules:
  0.0 561.8 jit_solution(3239854099723418143)
XLA Ops:
  8.8 3.0 reduce
  11.9 19.6 %all_to_all.45 = bf16[32,2,3072]{2,1,0:T(2,128)(2,1)S(1)} all-to-all(bf16[32,2,3072]{2,1,0:T(2,128)(2,1)S(1)} %reshape.97), channel_id=1, replica_groups=mesh['heads'=4,'ctx'=32] {'ctx'}, dimensions={0} | all-to-all | bytes 786432 | tf_op jit(solution)/shard_map/all_to_all | solution.py:32
  34.4 3.0 reduce.2
  37.6 16.5 %all_to_all.46 = bf16[32,2,3072]{2,1,0:T(2,128)(2,1)S(1)} all-to-all(bf16[32,2,3072]{2,1,0:T(2,128)(2,1)S(1)} %reshape.101), channel_id=1, replica_groups=mesh['heads'=4,'ctx'=32] {'ctx'}, dimensions={0} | all-to-all | bytes 786432 | tf_op jit(solution)/shard_map/all_to_all | solution.py:33
  56.9 3.0 reduce.1
  60.8 5.2 all-to-all-start.1
  67.1 12.1 %all-to-all-done.1 = bf16[32,2,3072]{2,1,0:T(2,128)(2,1)S(1)} async-done(((bf16[32,2,3072]{2,1,0:T(2,128)(2,1)}), bf16[32,2,3072]{2,1,0:T(2,128)(2,1)S(1)}, u32[]{:S(2)}, u32[]{:S(2)}) %all-to-all-start.1) | async-done | bytes 393248 | tf_op jit(solution)/shard_map/all_to_all | solution.py:31
  80.7 20.9 %all-gather.3.cloned.1.call-done = bf16[16384,384]{1,0:T(8,128)(2,1)} async-done(((bf16[512,384]{1,0:T(8,128)(2,1)}), bf16[16384,384]{1,0:T(8,128)(2,1)}) %all-gather.3.cloned.1.call-update) | async-done | bytes 12582928 | tf_op jit(solution)/shard_map/all_gather | solution.py:84
  101.6 64.7 %all-gather.5.cloned.1.call-done = bf16[16384,384]{1,0:T(8,128)(2,1)} async-done(((bf16[512,384]{1,0:T(8,128)(2,1)}), bf16[16384,384]{1,0:T(8,128)(2,1)}) %all-gather.5.cloned.1.call-update) | async-done | bytes 12582928 | tf_op jit(solution)/shard_map/all_gather | solution.py:85
  166.3 332.0 %while.17 = (s32[]{:T(128)}, f32[3,4,128]{2,1,0:T(4,128)S(1)}, f32[3,4,128]{2,1,0:T(4,128)}, f32[3,4,128,128]{3,2,1,0:T(8,128)}, s32[32]{0:T(128)S(1)}, /*index=...) while((s32[]{:T(128)}, f32[3,4,128]{2,1,0:T(4,128)S(1)}, ...), condition=%wide.region_3.4_spmd.clone, body=%wide.region_0.3_spmd.clone.sunk | while | flops 413554176 | bytes 21832052 | solution.py:95
  169.3 2.8 fusion.50
  179.7 2.8 fusion.50
  200.4 2.8 fusion.50
  221.2 2.8 fusion.50
  231.6 2.8 fusion.50
  241.9 2.8 fusion.50
  262.7 2.8 fusion.50
  283.4 2.8 fusion.50
  293.8 2.8 fusion.50
  304.2 2.8 fusion.50
  324.9 2.8 fusion.50
  345.7 2.8 fusion.50
  366.4 2.8 fusion.50
  387.2 2.8 fusion.50
  407.9 2.8 fusion.50
  428.7 2.8 fusion.50
  449.4 2.8 fusion.50
  470.2 2.8 fusion.50
  490.9 2.8 fusion.50
  500.5 15.4 %all_to_all.47 = bf16[32,16,384]{2,1,0:T(8,128)(2,1)S(1)} all-to-all(bf16[32,16,384]{2,1,0:T(8,128)(2,1)S(1)} %copy.61), channel_id=1, replica_groups=mesh['heads'=4,'ctx'=32] {'ctx'}, dimensions={0} | all-to-all | bytes 786432 | tf_op jit(solution)/shard_map/all_to_all | solution.py:99
  516.0 3.5 convolution_convert_fusion
  519.5 35.8 %reduce-scatter.2.cloned.1.call-done = bf16[512,768]{1,0:T(8,128)(2,1)} async-done(((bf16[512,3072]{1,0:T(8,128)(2,1)}), bf16[512,768]{1,0:T(8,128)(2,1)}) %reduce-scatter.2.cloned.1.call-update) | async-done | bytes 786448 | tf_op jit(solution)/shard_map/reduce_scatter | solution.py:103
  (917 shorter events, 287.4 us)
Async XLA Ops:
  6.5 509.4 %copy-start = (bf16[384,3072]{1,0:T(8,128)(2,1)S(1)}, bf16[384,3072]{1,0:T(8,128)(2,1)}, u32[]{:S(2)}) copy-start(bf16[384,3072]{1,0:T(8,128)(2,1)} %param.11) | copy-start | bytes 7077892
  6.5 95.1 %all-gather.3.cloned.1.call-start = ((), (), s32[]{:S(2)}) async-start(), calls=%async_computation.5 | async-start | bytes 12976128 | tf_op jit(solution)/shard_map/all_gather | solution.py:84
  32.8 133.5 %all-gather.5.cloned.1.call-start = ((), (), s32[]{:S(2)}) async-start(), calls=%async_computation.6 | async-start | bytes 12976128 | tf_op jit(solution)/shard_map/all_gather | solution.py:85
  54.4 11.7 %copy-start.7 = (s32[3]{0:T(128)S(1)}, s32[3]{0:T(128)}, u32[]{:S(2)}) copy-start(s32[3]{0:T(128)} %param.13) | copy-start | bytes 40
  60.8 18.4 %all-to-all-start.1 = ((bf16[32,2,3072]{2,1,0:T(2,128)(2,1)}), bf16[32,2,3072]{2,1,0:T(2,128)(2,1)S(1)}, u32[]{:S(2)}, u32[]{:S(2)}) async-start(bf16[32,2,3072]{2,1,0:T(2,128)(2,1)} %reshape.99), calls=%async_computation.1 | async-start | bytes 786432 | tf_op jit(solution)/shard_map/all_to_all | solution.py:31
  66.0 489.2 %reduce-scatter.2.cloned.1.call-start = ((), (), s32[]{:S(2)}) async-start(), calls=%async_computation.7 | async-start | bytes 3932160 | tf_op jit(solution)/shard_map/reduce_scatter | solution.py:103
  169.3 4.1 copy-start.1
  179.7 4.1 copy-start.1
  190.1 4.1 copy-start.1
  200.4 4.1 copy-start.1
  210.8 4.1 copy-start.1
  221.2 4.1 copy-start.1
  231.6 4.1 copy-start.1
  241.9 4.1 copy-start.1
  252.3 4.1 copy-start.1
  262.7 4.1 copy-start.1
  273.1 4.1 copy-start.1
  283.4 4.1 copy-start.1
  293.8 4.1 copy-start.1
  304.2 4.1 copy-start.1
  324.9 4.1 copy-start.1
  345.7 4.1 copy-start.1
  356.1 4.1 copy-start.1
  366.4 4.1 copy-start.1
  387.2 4.1 copy-start.1
  407.9 4.1 copy-start.1
  418.3 4.1 copy-start.1
  428.7 4.1 copy-start.1
  449.4 4.1 copy-start.1
  470.2 4.1 copy-start.1
  480.6 4.1 copy-start.1
  490.9 4.1 copy-start.1
  (230 other events, 639.7 us)
Sparse Core Ops, SparseCore 0:
  32.9 68.6 all-gather.2
  103.9 62.3 all-gather.4
  519.6 35.6 reduce-scatter.1
where the time goes:
time: 564 us; the launch traced here: 562 us
  matrix products  178 us (32%)
  waiting for transfers between devices  134 us (24%)
  local copies, waits for them, and re-layouts  109 us (19%)
  other arithmetic  66.1 us (12%)
  blocking collectives  51.5 us (9%)
  between operations  13.3 us (2%)
    dot_general x32, matrix products, attend(): jnp.einsum('tqhd,khd->htqk', query_tiles, key_piece.reshape(piece_len, lo...  89.6 us
    dot_general x32, matrix products, attend(): jnp.einsum('htqk,khd->htqd', weights.astype(jnp.bfloat16), value_piece.re...  76.5 us
    dynamic_slice x128, local copies, waits for them, and re-layouts, body(): lax.scan(one_step, start_state, (key_steps, value_steps, offsets))  68.4 us
    all_gather x1, waiting for transfers between devices, body(): value_piece = lax.all_gather(value_side, 'ctx', axis=0, tiled=True)  64.7 us
    reduce_sum x32, other arithmetic, attend(): totals = totals * factor + jnp.sum(weights, axis=-1)  37 us
    reduce_scatter x1, waiting for transfers between devices, body(): lax.psum_scatter(partial_sum.astype(jnp.bfloat16), 'heads', scatter_dimen...  35.8 us
    while x544, local copies, waits for them, and re-layouts  28.4 us
    all_gather x1, waiting for transfers between devices, body(): key_piece = lax.all_gather(key_side, 'ctx', axis=0, tiled=True)  20.9 us
  transfers between devices with their start and end apart: 4, of which 4 were waited for; matrix products, arithmetic and copies ran while one was open for 2% of the time, Pallas kernels for 0%

commit v1 on v0

v1 whole, which is shorter than its diff:
```python
import math

import jax
import jax.numpy as jnp
from jax import lax
from jax.experimental import pallas as pl
from jax.experimental.pallas import tpu as pltpu
from jax.sharding import PartitionSpec as P

MESH = pl.DeviceIdType.MESH
DH = 128
TILE = 128
SPOTS = 4
FRAMES = 32
TILES = 128
PLANES = 4
SIDE = 4
HEADS_HERE = 3
WORKERS = 2 * SIDE
SLOTS = TILES // WORKERS
PARTS = 4
PART = 2 * TILES // PARTS
PIECE = TILE // WORKERS
GROUP = 16
STEPS = TILES // GROUP
LOW = -1e30
SCALE2 = math.log2(math.e) / math.sqrt(DH)
BF16 = jnp.bfloat16
F32 = jnp.float32


def where_is(device):
    return lax.div(device, WORKERS), lax.rem(lax.div(device, 2), SIDE), lax.rem(device, 2)


def device_at(row, column, core):
    return (lax.rem(row, SIDE) * SIDE + lax.rem(column, SIDE)) * 2 + core


def spread_kernel(
    q_ref, kv_ref, w_ref, q_all, kv_all, w_all,
    q_send, q_recv, z_send, z_recv, y_send, y_recv, far_send, far_recv,
    core_send, core_recv, w_send, w_recv, w_core_send, w_core_recv, own_sem,
):
    plane = lax.axis_index("heads")
    me = lax.axis_index("ctx")
    row, column, core = where_is(me)
    working = row < HEADS_HERE
    own_row = jnp.minimum(row, HEADS_HERE - 1)
    depth = w_ref.shape[0]
    width = w_all.shape[1]
    sides = (1, SIDE - 1)

    barrier = pltpu.get_barrier_semaphore()

    def greet(step, carry):
        pl.semaphore_signal(
            barrier, inc=1, device_id=(plane, lax.rem(me + step, FRAMES)), device_id_type=MESH
        )
        return carry

    lax.fori_loop(1, FRAMES, greet, 0)
    for hop in range(1, PLANES):
        pl.semaphore_signal(
            barrier, inc=1, device_id=(lax.rem(plane + hop, PLANES), me), device_id_type=MESH
        )
    pl.semaphore_wait(barrier, FRAMES - 1 + PLANES - 1)

    def span(part):
        return pl.ds(part * PART, PART)

    own_copy = pltpu.make_async_copy(
        kv_ref.at[own_row], kv_all.at[column * 2 + core, :, 0], own_sem
    )

    def z_copy(part, hop):
        there = lax.rem(row + hop, SIDE)
        return pltpu.make_async_remote_copy(
            src_ref=kv_ref.at[there, span(part)],
            dst_ref=kv_all.at[column * 2 + core, span(part), hop],
            send_sem=z_send.at[part, hop],
            recv_sem=z_recv.at[part, hop],
            device_id=(plane, device_at(there, column, core)),
            device_id_type=MESH,
        )

    def piece(number, away):
        source = kv_all.at[lax.rem(column + away, SIDE) * 2 + core]
        if number == 0:
            return source.at[:, 0]
        return source.at[span(number - 1), pl.ds(1, SIDE - 1)]

    def y_copy(number, side):
        return pltpu.make_async_remote_copy(
            src_ref=kv_ref.at[own_row] if number == 0 else piece(number, 0),
            dst_ref=piece(number, 0),
            send_sem=y_send.at[number, side],
            recv_sem=y_recv.at[number, side],
            device_id=(plane, device_at(row, column + sides[side], core)),
            device_id_type=MESH,
        )

    def far_copy(number, side):
        source = kv_all.at[lax.rem(column + sides[1 - side], SIDE) * 2 + core]
        if number == 0:
            chunk = source.at[pl.ds(side * TILES, TILES), 0]
        else:
            chunk = source.at[
                pl.ds((number - 1) * PART + side * (PART // 2), PART // 2), pl.ds(1, SIDE - 1)
            ]
        return pltpu.make_async_remote_copy(
            src_ref=chunk,
            dst_ref=chunk,
            send_sem=far_send.at[number, side],
            recv_sem=far_recv.at[number, side],
            device_id=(plane, device_at(row, column + sides[side], core)),
            device_id_type=MESH,
        )

    def core_copy(number, away):
        return pltpu.make_async_remote_copy(
            src_ref=piece(number, away),
            dst_ref=piece(number, away),
            send_sem=core_send.at[number, away],
            recv_sem=core_recv,
            device_id=(plane, device_at(row, column, 1 - core)),
            device_id_type=MESH,
        )

    half = depth // 2

    def w_rows(source, part):
        return w_all.at[pl.ds(pl.multiple_of(source * depth + part * half, 16), half)]

    def w_copy(hop):
        there = lax.rem(plane + hop, PLANES)
        return pltpu.make_async_remote_copy(
            src_ref=w_ref.at[
                pl.ds(pl.multiple_of(core * half, 16), half),
                pl.ds(pl.multiple_of(there * width, 128), width),
            ],
            dst_ref=w_rows(plane, core),
            send_sem=w_send.at[hop],
            recv_sem=w_recv.at[hop],
            device_id=(there, me),
            device_id_type=MESH,
        )

    def w_core_copy(hop):
        rows = w_rows(lax.rem(plane + PLANES - hop, PLANES), core)
        return pltpu.make_async_remote_copy(
            src_ref=rows,
            dst_ref=rows,
            send_sem=w_core_send.at[hop],
            recv_sem=w_core_recv.at[hop],
            device_id=(plane, device_at(row, column, 1 - core)),
            device_id_type=MESH,
        )

    own_w = pltpu.make_async_copy(
        w_ref.at[:, pl.ds(pl.multiple_of(plane * width, 128), width)],
        w_all.at[pl.ds(pl.multiple_of(plane * depth, 128), depth)],
        w_recv.at[0],
    )

    def q_copy(step):
        there = lax.rem(me + step, FRAMES)
        row_there, column_there, core_there = where_is(there)
        return row_there < HEADS_HERE, pltpu.make_async_remote_copy(
            src_ref=q_ref.at[
                jnp.minimum(row_there, HEADS_HERE - 1), :, column_there * 2 + core_there
            ],
            dst_ref=q_all.at[:, me],
            send_sem=q_send.at[step],
            recv_sem=q_recv,
            device_id=(plane, there),
            device_id_type=MESH,
        )

    def to_rows(part, work):
        for hop in range(1, SIDE):

            @pl.when(lax.rem(row + hop, SIDE) < HEADS_HERE)
            def _():
                work(z_copy(part, hop))

    def send_q(step, carry):
        wanted, copy = q_copy(step)

        @pl.when(wanted)
        def _():
            copy.start()

        return carry

    def sent_q(step, carry):
        wanted, copy = q_copy(step)

        @pl.when(wanted)
        def _():
            copy.wait_send()

        return carry

    def send_small():
        for hop in range(1, PLANES):
            w_copy(hop).start()
        own_w.start()
        lax.fori_loop(1, FRAMES, send_q, 0)

    @pl.when(working)
    def _():
        own_copy.start()
        for side in range(2):
            y_copy(0, side).start()

    to_rows(0, lambda copy: copy.start())
    send_small()

    def next_rows(part):
        to_rows(part, lambda copy: copy.wait_send())
        if part + 1 < PARTS:
            to_rows(part + 1, lambda copy: copy.start())

    @pl.when(jnp.logical_not(working))
    def _():
        for part in range(PARTS):
            next_rows(part)

    @pl.when(working)
    def _():
        pltpu.make_async_copy(
            q_ref.at[own_row, :, column * 2 + core], q_all.at[:, me], q_recv
        ).start()
        own_copy.wait()
        core_copy(0, 0).start()

        def pass_on(number):
            for side in range(2):
                y_copy(number, side).wait_recv()
                far_copy(number, side).start()
            for side in range(2):
                core_copy(number, sides[1 - side]).start()

        for part in range(PARTS):
            next_rows(part)
            for hop in range(1, SIDE):
                landed = kv_all.at[column * 2 + core, span(part), hop]
                pltpu.make_async_copy(landed, landed, z_recv.at[part, hop]).wait()
            for side in range(2):
                y_copy(part + 1, side).start()
            core_copy(part + 1, 0).start()
            pass_on(part)
        pass_on(PARTS)
        for number in range(PARTS + 1):
            for side in range(2):
                far_copy(number, side).wait_recv()
            core_copy(number, 2).start()

    for hop in range(1, PLANES):
        w_copy(hop).wait_recv()
        w_core_copy(hop).start()

    @pl.when(working)
    def _():
        pltpu.make_async_copy(q_all, q_all, q_recv).wait()
        other = kv_all.at[pl.ds(0, SIDE)]
        pltpu.make_async_copy(other, other, core_recv).wait()
        for number in range(PARTS + 1):
            for side in range(2):
                y_copy(number, side).wait_send()
                far_copy(number, side).wait_send()
            for away in range(SIDE):
                core_copy(number, away).wait_send()

    own_w.wait()
    lax.fori_loop(1, FRAMES, sent_q, 0)
    for hop in range(1, PLANES):
        w_copy(hop).wait_send()
        w_core_copy(hop).wait()


def spread(q_parts, kv_parts, out_weight):
    depth, columns = out_weight.shape
    return pl.pallas_call(
        spread_kernel,
        out_shape=(
            jax.ShapeDtypeStruct((SLOTS, FRAMES, SPOTS, DH), BF16),
            jax.ShapeDtypeStruct((WORKERS, 2 * TILES, SIDE, SPOTS, DH), BF16),
            jax.ShapeDtypeStruct((depth * PLANES, columns // PLANES), BF16),
        ),
        in_specs=[pl.BlockSpec(memory_space=pl.ANY)] * 3,
        out_specs=(pl.BlockSpec(memory_space=pl.ANY),) * 3,
        scratch_shapes=[
            pltpu.SemaphoreType.DMA((FRAMES,)),
            pltpu.SemaphoreType.DMA,
            pltpu.SemaphoreType.DMA((PARTS, SIDE)),
            pltpu.SemaphoreType.DMA((PARTS, SIDE)),
            pltpu.SemaphoreType.DMA((PARTS + 1, 2)),
            pltpu.SemaphoreType.DMA((PARTS + 1, 2)),
            pltpu.SemaphoreType.DMA((PARTS + 1, 2)),
            pltpu.SemaphoreType.DMA((PARTS + 1, 2)),
            pltpu.SemaphoreType.DMA((PARTS + 1, SIDE)),
            pltpu.SemaphoreType.DMA,
            pltpu.SemaphoreType.DMA((PLANES,)),
            pltpu.SemaphoreType.DMA((PLANES,)),
            pltpu.SemaphoreType.DMA((PLANES,)),
            pltpu.SemaphoreType.DMA((PLANES,)),
            pltpu.SemaphoreType.DMA,
        ],
        compiler_params=pltpu.CompilerParams(
            collective_id=0, has_side_effects=True, vmem_limit_bytes=4 * 1024 * 1024
        ),
    )(q_parts, kv_parts, out_weight)


def attend_kernel(
    list_ref, q_ref, kv_ref, o_ref, even_ref, odd_ref, even_peak, odd_peak,
    base_ref, sum_ref,
):
    kept = ((even_ref, even_peak), (odd_ref, odd_peak))

    def count_of(slot):
        return list_ref[SLOTS, slot]

    def steps_of(slot):
        return lax.div(count_of(slot) + GROUP - 1, GROUP)

    def tile_of(slot, number, first):
        start = pl.multiple_of((first + list_ref[slot, number]) * PIECE, PIECE)
        return jnp.concatenate(
            [kv_ref[worker, pl.ds(start, PIECE), :] for worker in range(WORKERS)], axis=0
        )

    def score(slot, side, step):
        score_ref, peak_ref = kept[side]
        query = q_ref[pl.ds(pl.multiple_of(slot * TILE, TILE), TILE), :]
        keys = [tile_of(slot, step * GROUP + u, 0) for u in range(GROUP)]
        scores = lax.dot_general(
            query,
            jnp.concatenate(keys, axis=0),
            (((1,), (1,)), ((), ())),
            preferred_element_type=F32,
        )
        peak = peak_ref[...]
        for u in range(GROUP):
            part = scores[:, u * TILE : (u + 1) * TILE]
            score_ref[step, :, u * TILE : (u + 1) * TILE] = part
            peak = jnp.maximum(peak, part)
        peak_ref[...] = peak

    def gather(slot, side, step):
        score_ref = kept[side][0]
        base = base_ref[...]
        count = count_of(slot)
        weights, values = [], []
        for u in range(GROUP):
            part = score_ref[step, :, u * TILE : (u + 1) * TILE]
            weights.append(jnp.exp2(part * SCALE2 - base).astype(BF16))
            listed = step * GROUP + u < count
            value = jnp.where(listed, tile_of(slot, step * GROUP + u, TILES), 0).astype(BF16)
            ones = jnp.broadcast_to(jnp.where(listed, 1.0, 0.0).astype(BF16), (TILE, DH))
            values.append(jnp.concatenate([value, ones], axis=1))
        sum_ref[...] += jnp.dot(
            jnp.concatenate(weights, axis=1),
            jnp.concatenate(values, axis=0),
            preferred_element_type=F32,
        )

    def loop(first, last, work):
        def one(step, carry):
            work(step)
            return carry

        lax.fori_loop(first, last, one, 0)

    def one_slot(slot, side, ahead):
        here = steps_of(slot)
        both = jnp.minimum(here, ahead)
        base = jnp.max(kept[side][1][...], axis=1, keepdims=True) * SCALE2
        base_ref[...] = jnp.broadcast_to(base, (TILE, TILE))
        sum_ref[...] = jnp.zeros((TILE, 2 * DH), F32)
        kept[1 - side][1][...] = jnp.full((TILE, TILE), LOW, F32)

        def pair(step):
            gather(slot, side, step)
            score(slot + 1, 1 - side, step)

        loop(0, both, pair)
        loop(both, ahead, lambda step: score(slot + 1, 1 - side, step))
        loop(both, here, lambda step: gather(slot, side, step))
        o_ref[pl.ds(pl.multiple_of(slot * TILE, TILE), TILE), :] = (
            sum_ref[:, :DH] / sum_ref[:, DH:]
        ).astype(BF16)

    even_peak[...] = jnp.full((TILE, TILE), LOW, F32)
    loop(0, steps_of(0), lambda step: score(0, 0, step))

    def two_slots(turn, carry):
        slot = turn * 2
        one_slot(slot, 0, steps_of(slot + 1))
        follows = jnp.minimum(slot + 2, SLOTS - 1)
        one_slot(slot + 1, 1, jnp.where(slot + 2 < SLOTS, steps_of(follows), 0))
        return carry

    lax.fori_loop(0, SLOTS // 2, two_slots, 0)
    if SLOTS % 2:
        one_slot(SLOTS - 1, 0, 0)


def attend(lists, query, kv):
    return pl.pallas_call(
        attend_kernel,
        out_shape=jax.ShapeDtypeStruct(query.shape, BF16),
        in_specs=[
            pl.BlockSpec(memory_space=pltpu.SMEM),
            pl.BlockSpec(memory_space=pltpu.VMEM),
            pl.BlockSpec(memory_space=pltpu.VMEM),
        ],
        out_specs=pl.BlockSpec(memory_space=pltpu.VMEM),
        scratch_shapes=[
            pltpu.VMEM((STEPS, TILE, GROUP * TILE), F32),
            pltpu.VMEM((STEPS, TILE, GROUP * TILE), F32),
            pltpu.VMEM((TILE, TILE), F32),
            pltpu.VMEM((TILE, TILE), F32),
            pltpu.VMEM((TILE, TILE), F32),
            pltpu.VMEM((TILE, 2 * DH), F32),
        ],
        compiler_params=pltpu.CompilerParams(vmem_limit_bytes=40 * 1024 * 1024),
    )(lists, query, kv)


def collect_kernel(o_ref, attn, send, recv, x_send, x_recv):
    plane = lax.axis_index("heads")
    me = lax.axis_index("ctx")
    row, column, core = where_is(me)
    barrier = pltpu.get_barrier_semaphore()

    def greet(step, carry):
        pl.semaphore_signal(
            barrier, inc=1, device_id=(plane, lax.rem(me + step, FRAMES)), device_id_type=MESH
        )
        return carry

    lax.fori_loop(1, FRAMES, greet, 0)
    sides = (lax.rem(plane + 1, PLANES), lax.rem(plane + PLANES - 1, PLANES))
    for there in sides:
        pl.semaphore_signal(barrier, inc=1, device_id=(there, me), device_id_type=MESH)
    pl.semaphore_wait(barrier, FRAMES - 1 + 2)

    mine = jnp.minimum(row, HEADS_HERE - 1)
    goal = attn.at[plane * HEADS_HERE + mine, :, column * 2 + core]

    def back(step):
        there = lax.rem(me + step, FRAMES)
        return pltpu.make_async_remote_copy(
            src_ref=o_ref.at[:, there],
            dst_ref=goal,
            send_sem=send.at[step],
            recv_sem=recv.at[mine],
            device_id=(plane, there),
            device_id_type=MESH,
        )

    def start(step, carry):
        back(step).start()
        return carry

    def end(step, carry):
        back(step).wait_send()
        return carry

    working = row < HEADS_HERE

    @pl.when(working)
    def _():
        lax.fori_loop(1, FRAMES, start, 0)
        pltpu.make_async_copy(o_ref.at[:, me], goal, recv.at[mine]).start()

    cut = SLOTS // 2

    def near(head, side):
        part = attn.at[plane * HEADS_HERE + head]
        return pltpu.make_async_remote_copy(
            src_ref=part,
            dst_ref=part,
            send_sem=x_send.at[head, side],
            recv_sem=x_recv.at[head, side],
            device_id=(sides[side], me),
            device_id_type=MESH,
        )

    def far(head, side):
        part = attn.at[sides[1 - side] * HEADS_HERE + head]
        part = part.at[pl.ds(0, cut)] if side == 0 else part.at[pl.ds(cut, SLOTS - cut)]
        return pltpu.make_async_remote_copy(
            src_ref=part,
            dst_ref=part,
            send_sem=x_send.at[head, 2 + side],
            recv_sem=x_recv.at[head, 2 + side],
            device_id=(sides[side], me),
            device_id_type=MESH,
        )

    for head in range(HEADS_HERE):
        part = attn.at[plane * HEADS_HERE + head]
        pltpu.make_async_copy(part, part, recv.at[head]).wait()
        for side in range(2):
            near(head, side).start()
    for head in range(HEADS_HERE):
        for side in range(2):
            near(head, side).wait_recv()
            far(head, side).start()

    @pl.when(working)
    def _():
        lax.fori_loop(1, FRAMES, end, 0)

    for head in range(HEADS_HERE):
        for side in range(2):
            near(head, side).wait_send()
            far(head, side).wait()


def collect(attended):
    return pl.pallas_call(
        collect_kernel,
        out_shape=jax.ShapeDtypeStruct(
            (PLANES * HEADS_HERE, SLOTS, WORKERS, SPOTS, DH), BF16
        ),
        in_specs=[pl.BlockSpec(memory_space=pl.ANY)],
        out_specs=pl.BlockSpec(memory_space=pl.ANY),
        scratch_shapes=[
            pltpu.SemaphoreType.DMA((FRAMES,)),
            pltpu.SemaphoreType.DMA((HEADS_HERE,)),
            pltpu.SemaphoreType.DMA((HEADS_HERE, 4)),
            pltpu.SemaphoreType.DMA((HEADS_HERE, 4)),
        ],
        compiler_params=pltpu.CompilerParams(
            collective_id=1, has_side_effects=True, vmem_limit_bytes=4 * 1024 * 1024
        ),
    )(attended)


def project_kernel(attn_ref, w_ref, out_ref):
    rows = out_ref.shape[0]
    heads = attn_ref.shape[0]
    wide = jnp.concatenate([attn_ref[h, :rows, :] for h in range(heads)], axis=1)
    out_ref[...] = jnp.dot(wide, w_ref[...], preferred_element_type=F32).astype(BF16)


def project(attn, weight, rows):
    columns = weight.shape[1]
    block = 256
    heads = attn.shape[0]
    return pl.pallas_call(
        project_kernel,
        out_shape=jax.ShapeDtypeStruct((rows, columns), BF16),
        grid=(columns // block,),
        in_specs=[
            pl.BlockSpec((heads, attn.shape[1], DH), lambda i: (0, 0, 0)),
            pl.BlockSpec((weight.shape[0], block), lambda i: (0, i)),
        ],
        out_specs=pl.BlockSpec((rows, block), lambda i: (0, i)),
        compiler_params=pltpu.CompilerParams(vmem_limit_bytes=24 * 1024 * 1024),
    )(attn, weight)


def arrange_kernel(pattern_ref, mask_ref, q_ref, k_ref, v_ref, q_out, kv_out, list_ref):
    me = lax.axis_index("ctx")
    row, column, core = where_is(me)
    rows = q_ref.shape[0]
    for head in range(HEADS_HERE):
        columns = slice(head * DH, (head + 1) * DH)
        q_out[head] = q_ref[:, columns]
        kv_out[head, :rows, :] = k_ref[:, columns]
        kv_out[head, rows:, :] = v_ref[:, columns]

    pattern = pattern_ref[jnp.minimum(row, HEADS_HERE - 1)]
    masks = []
    tiles = [slot * WORKERS + column * 2 + core for slot in range(SLOTS)]
    for tile in tiles:
        masks.append(jnp.where(row < HEADS_HERE, mask_ref[pattern, pl.ds(tile, 1), :], 0))
    seen = jnp.concatenate(masks, axis=0) == 1
    seen = jnp.where(seen, 1.0, 0.0).astype(F32)
    down = lax.broadcasted_iota(jnp.int32, (TILES, TILES), 0)
    along = lax.broadcasted_iota(jnp.int32, (TILES, TILES), 1)
    both = (((1,), (1,)), ((), ()))
    upto = jnp.where(along <= down, 1.0, 0.0).astype(BF16)
    same = jnp.where(along == down, 1.0, 0.0).astype(BF16)
    rank = lax.dot_general(upto, seen.astype(BF16), both, preferred_element_type=F32)
    turned = lax.dot_general(same, seen.astype(BF16), both, preferred_element_type=F32)
    rank = rank.astype(jnp.int32)
    spot = jnp.where(turned > 0.5, rank - 1, -1)
    for slot in range(SLOTS):
        hit = spot[:, slot : slot + 1] == along
        listed = jnp.sum(jnp.where(hit, down, 0), axis=0, keepdims=True)
        spare = along[:1, :] >= rank[TILES - 1 :, slot : slot + 1]
        list_ref[slot : slot + 1, :] = jnp.where(spare, tiles[slot], listed)
    last = jnp.concatenate(
        [rank[TILES - 1 :, :], jnp.zeros((1, TILES - SLOTS), jnp.int32)], axis=1
    )
    list_ref[SLOTS : SLOTS + 1, :] = last


def arrange(head_pattern, tile_masks, queries, key_rows, value_rows):
    rows = queries.shape[0]
    return pl.pallas_call(
        arrange_kernel,
        out_shape=(
            jax.ShapeDtypeStruct((HEADS_HERE, rows, DH), BF16),
            jax.ShapeDtypeStruct((HEADS_HERE, 2 * rows, DH), BF16),
            jax.ShapeDtypeStruct((SLOTS + 1, TILES), jnp.int32),
        ),
        in_specs=[pl.BlockSpec(memory_space=pltpu.SMEM)]
        + [pl.BlockSpec(memory_space=pltpu.VMEM)] * 4,
        out_specs=(pl.BlockSpec(memory_space=pltpu.VMEM),) * 3,
        compiler_params=pltpu.CompilerParams(vmem_limit_bytes=16 * 1024 * 1024),
    )(head_pattern, tile_masks, queries, key_rows, value_rows)


def body(queries, key_rows, value_rows, out_weight, tile_masks, head_pattern):
    rows = queries.shape[0]
    q_parts, kv_parts, lists = arrange(head_pattern, tile_masks, queries, key_rows, value_rows)
    q_all, kv_all, w_all = spread(
        q_parts.reshape(HEADS_HERE, SLOTS, WORKERS, SPOTS, DH),
        kv_parts.reshape(HEADS_HERE, 2 * TILES, SPOTS, DH),
        out_weight,
    )
    attended = attend(
        lists, q_all.reshape(SLOTS * TILE, DH), kv_all.reshape(WORKERS, 2 * TILES * PIECE, DH)
    )
    attn = collect(attended.reshape(SLOTS, FRAMES, SPOTS, DH))
    attn = attn.reshape(PLANES * HEADS_HERE, rows, DH)
    return project(attn, w_all, rows)


def solution(mesh):
    placed = (
        P("ctx", "heads"),
        P("ctx", "heads"),
        P("ctx", "heads"),
        P("heads", None),
        P(),
        P("heads"),
    )
    return jax.shard_map(
        body, mesh=mesh, in_specs=placed, out_specs=P("ctx", "heads"), check_vma=False
    )
```

time: 564 us -> 123 us (0.22)
  matrix products: 178 us -> 0 us
  waiting for transfers between devices: 134 us -> 0 us
  Pallas kernels: 0 us -> 116 us
  local copies, waits for them, and re-layouts: 109 us -> 6.2 us
  other arithmetic: 66.1 us -> 0 us
  blocking collectives: 51.5 us -> 0 us
  between operations: 13.3 us -> 0.04 us
    dot_general x97 -> x0, matrix products: 178 us -> none  [the longest x32 89.6 us: attend(): jnp.einsum('tqhd,khd->htqk', query_tiles, key_piece.reshape(piece_len, lo...]
    pallas_call x0 -> x5, Pallas kernels: none -> 116 us  [the longest x1 52.4 us: spread(): pl.pallas_call(spread_kernel, out_shape=(jax.ShapeDtypeStruct((SLOTS, FRA...]
    all_gather x2 -> x0, waiting for transfers between devices: 85.6 us -> none  [the longest x1 64.7 us: body(): value_piece = lax.all_gather(value_side, 'ctx', axis=0, tiled=True)]
    dynamic_slice x129 -> x0, local copies, waits for them, and re-layouts: 68.4 us -> none  [the longest x128 68.4 us: body(): lax.scan(one_step, start_state, (key_steps, value_steps, offsets))]
    all_to_all x3 -> x0, blocking collectives: 51.5 us -> none  [the longest x1 19.6 us: body(): lax.all_to_all(blocks[1], 'ctx', split_axis=1, concat_axis=0, tiled=True)]
    reduce_sum x32 -> x0, other arithmetic: 37 us -> none  [attend(): totals = totals * factor + jnp.sum(weights, axis=-1)]
    reduce_scatter x1 -> x0, waiting for transfers between devices: 35.8 us -> none  [body(): lax.psum_scatter(partial_sum.astype(jnp.bfloat16), 'heads', scatter_dimen...]
    while x544 -> x0, local copies, waits for them, and re-layouts: 28.4 us -> none
  transfers between devices with their start and end apart: 4 -> 0, of which waited for: 4 -> 0; matrix products, arithmetic and copies ran while one was open for 2% -> 0% of each run, Pallas kernels for 0% -> 0%
where the time goes in v1:
time: 123 us; the launch traced here: 122 us
  Pallas kernels  116 us (94%)
  local copies, waits for them, and re-layouts  6.2 us (5%)
    pallas_call x1, Pallas kernels, spread(): pl.pallas_call(spread_kernel, out_shape=(jax.ShapeDtypeStruct((SLOTS, FRA...  52.4 us
    pallas_call x1, Pallas kernels, collect(): pl.pallas_call(collect_kernel, out_shape=jax.ShapeDtypeStruct((PLANES * H...  31.8 us
    pallas_call x1, Pallas kernels, attend(): pl.pallas_call(attend_kernel, out_shape=jax.ShapeDtypeStruct(query.shape,...  28 us
    unnamed x12, local copies, waits for them, and re-layouts  6.2 us
    pallas_call x1, Pallas kernels, project(): pl.pallas_call(project_kernel, out_shape=jax.ShapeDtypeStruct((rows, colu...  2.69 us

profile of v1, /device:TPU:1, one launch (start us, length us, event | category | flops | bytes accessed | tf_op | source)
XLA Modules:
  0.0 122.4 jit_solution(15386303088100121738)
XLA Ops:
  0.0 0.0 copy-start.1
  0.0 1.0 copy-done.1
  1.0 0.0 copy-start.2
  1.0 1.0 copy-done.2
  2.0 0.0 copy-start.3
  2.0 1.0 copy-done.3
  3.0 0.0 copy-start.4
  3.0 0.9 copy-done.4
  3.9 0.0 copy-start.5
  3.9 0.7 copy-done.5
  4.5 1.3 %shard_map.64 = (bf16[3,512,128]{2,1,0:T(8,128)(2,1)S(1)}, bf16[3,1024,128]{2,1,0:T(8,128)(2,1)S(1)}, s32[17,128]{1,0:T(8,128)S(1)}) custom-call(s32[3]{0:T(128)S(1)} %copy-done.5, s32[2,128,128]{2,1,0:T(8,128)S(1)} %copy-done.4, bf16[512,384]{1,0:T(8,128)(2,1)S(1)} %copy-done.1, bf16[512,384]{1,0:T(8,128)(2,1)S(1)} %copy-done.2, bf16[512,384]{1,0:T(8,128)(2,1)S(1)} %copy-done.3), custom_call_target="tpu_custom_call" | custom-call | tf_op jit(solution)/shard_map/pallas_call | solution.py:608
  5.9 0.0 copy-start
  5.9 1.7 %copy-done = bf16[384,3072]{1,0:T(8,128)(2,1)S(1)} copy-done((bf16[384,3072]{1,0:T(8,128)(2,1)S(1)}, bf16[384,3072]{1,0:T(8,128)(2,1)}, u32[]{:S(2)}) %copy-start) | copy-done | bytes 2359320
  7.5 52.4 %shard_map.65 = (bf16[16,32,4,128]{3,2,1,0:T(4,128)(2,1)S(1)}, bf16[8,256,4,4,128]{4,3,2,1,0:T(4,128)(2,1)S(1)}, bf16[1536,768]{1,0:T(8,128)(2,1)S(1)}) custom-call(bf16[3,16,8,4,128]{4,3,2,1,0:T(4,128)(2,1)S(1)} %bitcast.11, bf16[3,256,4,128]{3,2,1,0:T(4,128)(2,1)S(1)} %bitcast.9, bf16[384,3072]{1,0:T(8,128)(2,1)S(1)} %copy-done), custom_call_target="tpu_custom_call" | custom-call | tf_op jit(solution)/shard_map/pallas_call | solution.py:285
  59.9 28.0 %shard_map.66 = bf16[2048,128]{1,0:T(8,128)(2,1)S(1)} custom-call(s32[17,128]{1,0:T(8,128)S(1)} %get-tuple-element.11.list_ref, bf16[2048,128]{1,0:T(8,128)(2,1)S(1)} %bitcast.10, bf16[8,4096,128]{2,1,0:T(8,128)(2,1)S(1)} %bitcast.6), custom_call_target="tpu_custom_call" | custom-call | tf_op jit(solution)/shard_map/pallas_call | solution.py:412
  87.9 31.8 %shard_map.67 = bf16[12,16,8,4,128]{4,3,2,1,0:T(4,128)(2,1)S(1)} custom-call(bf16[16,32,4,128]{3,2,1,0:T(4,128)(2,1)S(1)} %bitcast.8), custom_call_target="tpu_custom_call" | custom-call | tf_op jit(solution)/shard_map/pallas_call | solution.py:526
  119.7 2.7 %shard_map.68 = bf16[512,768]{1,0:T(8,128)(2,1)} custom-call(bf16[12,512,128]{2,1,0:T(8,128)(2,1)S(1)} %bitcast.7, bf16[1536,768]{1,0:T(8,128)(2,1)S(1)} %get-tuple-element.16.w_ref), custom_call_target="tpu_custom_call" | custom-call | tf_op jit(solution)/shard_map/pallas_call | solution.py:556
Async XLA Ops:
  0.0 1.0 copy-start.1
  1.0 1.0 copy-start.2
  2.0 1.0 copy-start.3
  3.0 0.9 copy-start.4
  3.9 0.7 copy-start.5
  5.9 1.7 %copy-start = (bf16[384,3072]{1,0:T(8,128)(2,1)S(1)}, bf16[384,3072]{1,0:T(8,128)(2,1)}, u32[]{:S(2)}) copy-start(bf16[384,3072]{1,0:T(8,128)(2,1)} %w_ref.1) | copy-start | bytes 7077892

commit v2 on v1

--- a/solution.py
+++ b/solution.py
@@ -315,7 +315,7 @@
 
 
 def attend_kernel(
-    list_ref, q_ref, kv_ref, o_ref, even_ref, odd_ref, even_peak, odd_peak,
+    list_ref, q_ref, kv_ref, o_ref, turned_ref, even_ref, odd_ref, even_peak, odd_peak,
     base_ref, sum_ref,
 ):
     kept = ((even_ref, even_peak), (odd_ref, odd_peak))
@@ -326,8 +326,8 @@
     def steps_of(slot):
         return lax.div(count_of(slot) + GROUP - 1, GROUP)
 
-    def tile_of(slot, number, first):
-        start = pl.multiple_of((first + list_ref[slot, number]) * PIECE, PIECE)
+    def tile_at(tile):
+        start = pl.multiple_of(tile * PIECE, PIECE)
         return jnp.concatenate(
             [kv_ref[worker, pl.ds(start, PIECE), :] for worker in range(WORKERS)], axis=0
         )
@@ -335,13 +335,8 @@
     def score(slot, side, step):
         score_ref, peak_ref = kept[side]
         query = q_ref[pl.ds(pl.multiple_of(slot * TILE, TILE), TILE), :]
-        keys = [tile_of(slot, step * GROUP + u, 0) for u in range(GROUP)]
-        scores = lax.dot_general(
-            query,
-            jnp.concatenate(keys, axis=0),
-            (((1,), (1,)), ((), ())),
-            preferred_element_type=F32,
-        )
+        keys = [turned_ref[list_ref[slot, step * GROUP + u]] for u in range(GROUP)]
+        scores = jnp.dot(query, jnp.concatenate(keys, axis=1), preferred_element_type=F32)
         peak = peak_ref[...]
         for u in range(GROUP):
             part = scores[:, u * TILE : (u + 1) * TILE]
@@ -358,7 +353,7 @@
             part = score_ref[step, :, u * TILE : (u + 1) * TILE]
             weights.append(jnp.exp2(part * SCALE2 - base).astype(BF16))
             listed = step * GROUP + u < count
-            value = jnp.where(listed, tile_of(slot, step * GROUP + u, TILES), 0).astype(BF16)
+            value = jnp.where(listed, tile_at(TILES + list_ref[slot, step * GROUP + u]), 0).astype(BF16)
             ones = jnp.broadcast_to(jnp.where(listed, 1.0, 0.0).astype(BF16), (TILE, DH))
             values.append(jnp.concatenate([value, ones], axis=1))
         sum_ref[...] += jnp.dot(
@@ -393,6 +388,12 @@
             sum_ref[:, :DH] / sum_ref[:, DH:]
         ).astype(BF16)
 
+    def turn(step):
+        for u in range(GROUP):
+            tile = step * GROUP + u
+            turned_ref[tile] = tile_at(tile).T
+
+    loop(0, jnp.where(count_of(0) > 0, STEPS, 0), turn)
     even_peak[...] = jnp.full((TILE, TILE), LOW, F32)
     loop(0, steps_of(0), lambda step: score(0, 0, step))
 
@@ -419,6 +420,7 @@
         ],
         out_specs=pl.BlockSpec(memory_space=pltpu.VMEM),
         scratch_shapes=[
+            pltpu.VMEM((TILES, DH, TILE), BF16),
             pltpu.VMEM((STEPS, TILE, GROUP * TILE), F32),
             pltpu.VMEM((STEPS, TILE, GROUP * TILE), F32),
             pltpu.VMEM((TILE, TILE), F32),

time: 123 us -> 123 us (level)
    pallas_call x1, Pallas kernels: 28 us -> 33.5 us  [attend(): pl.pallas_call(attend_kernel, out_shape=jax.ShapeDtypeStruct(query.shape,...]
    pallas_call x1, Pallas kernels: 31.8 us -> 27.1 us  [collect(): pl.pallas_call(collect_kernel, out_shape=jax.ShapeDtypeStruct((PLANES * H...]
where the time goes in v2:
time: 123 us
  Pallas kernels  117 us (95%)
  local copies, waits for them, and re-layouts  6.2 us (5%)
    pallas_call x1, Pallas kernels, spread(): pl.pallas_call(spread_kernel, out_shape=(jax.ShapeDtypeStruct((SLOTS, FRA...  52.4 us
    pallas_call x1, Pallas kernels, attend(): pl.pallas_call(attend_kernel, out_shape=jax.ShapeDtypeStruct(query.shape,...  33.5 us
    pallas_call x1, Pallas kernels, collect(): pl.pallas_call(collect_kernel, out_shape=jax.ShapeDtypeStruct((PLANES * H...  27.1 us
    unnamed x12, local copies, waits for them, and re-layouts  6.2 us
    pallas_call x1, Pallas kernels, project(): pl.pallas_call(project_kernel, out_shape=jax.ShapeDtypeStruct((rows, colu...  2.69 us

profile of v2, /device:TPU:1, one launch (start us, length us, event | category | flops | bytes accessed | tf_op | source)
XLA Modules:
  0.0 123.2 jit_solution(13315930961407108378)
XLA Ops:
  0.0 0.0 copy-start.1
  0.0 1.0 copy-done.1
  1.0 0.0 copy-start.2
  1.0 1.0 copy-done.2
  2.0 0.0 copy-start.3
  2.0 1.0 copy-done.3
  3.0 0.0 copy-start.4
  3.0 0.9 copy-done.4
  3.9 0.0 copy-start.5
  3.9 0.7 copy-done.5
  4.5 1.3 %shard_map.64 = (bf16[3,512,128]{2,1,0:T(8,128)(2,1)S(1)}, bf16[3,1024,128]{2,1,0:T(8,128)(2,1)S(1)}, s32[17,128]{1,0:T(8,128)S(1)}) custom-call(s32[3]{0:T(128)S(1)} %copy-done.5, s32[2,128,128]{2,1,0:T(8,128)S(1)} %copy-done.4, bf16[512,384]{1,0:T(8,128)(2,1)S(1)} %copy-done.1, bf16[512,384]{1,0:T(8,128)(2,1)S(1)} %copy-done.2, bf16[512,384]{1,0:T(8,128)(2,1)S(1)} %copy-done.3), custom_call_target="tpu_custom_call" | custom-call | tf_op jit(solution)/shard_map/pallas_call | solution.py:610
  5.9 0.0 copy-start
  5.9 1.7 %copy-done = bf16[384,3072]{1,0:T(8,128)(2,1)S(1)} copy-done((bf16[384,3072]{1,0:T(8,128)(2,1)S(1)}, bf16[384,3072]{1,0:T(8,128)(2,1)}, u32[]{:S(2)}) %copy-start) | copy-done | bytes 2359320
  7.5 52.4 %shard_map.65 = (bf16[16,32,4,128]{3,2,1,0:T(4,128)(2,1)S(1)}, bf16[8,256,4,4,128]{4,3,2,1,0:T(4,128)(2,1)S(1)}, bf16[1536,768]{1,0:T(8,128)(2,1)S(1)}) custom-call(bf16[3,16,8,4,128]{4,3,2,1,0:T(4,128)(2,1)S(1)} %bitcast.11, bf16[3,256,4,128]{3,2,1,0:T(4,128)(2,1)S(1)} %bitcast.9, bf16[384,3072]{1,0:T(8,128)(2,1)S(1)} %copy-done), custom_call_target="tpu_custom_call" | custom-call | tf_op jit(solution)/shard_map/pallas_call | solution.py:285
  59.9 33.5 %shard_map.66 = bf16[2048,128]{1,0:T(8,128)(2,1)S(1)} custom-call(s32[17,128]{1,0:T(8,128)S(1)} %get-tuple-element.11.list_ref, bf16[2048,128]{1,0:T(8,128)(2,1)S(1)} %bitcast.10, bf16[8,4096,128]{2,1,0:T(8,128)(2,1)S(1)} %bitcast.6), custom_call_target="tpu_custom_call" | custom-call | tf_op jit(solution)/shard_map/pallas_call | solution.py:413
  93.4 27.1 %shard_map.67 = bf16[12,16,8,4,128]{4,3,2,1,0:T(4,128)(2,1)S(1)} custom-call(bf16[16,32,4,128]{3,2,1,0:T(4,128)(2,1)S(1)} %bitcast.8), custom_call_target="tpu_custom_call" | custom-call | tf_op jit(solution)/shard_map/pallas_call | solution.py:528
  120.5 2.7 %shard_map.68 = bf16[512,768]{1,0:T(8,128)(2,1)} custom-call(bf16[12,512,128]{2,1,0:T(8,128)(2,1)S(1)} %bitcast.7, bf16[1536,768]{1,0:T(8,128)(2,1)S(1)} %get-tuple-element.16.w_ref), custom_call_target="tpu_custom_call" | custom-call | tf_op jit(solution)/shard_map/pallas_call | solution.py:558
Async XLA Ops:
  0.0 1.0 copy-start.1
  1.0 1.0 copy-start.2
  2.0 1.0 copy-start.3
  3.0 0.9 copy-start.4
  3.9 0.7 copy-start.5
  5.9 1.7 %copy-start = (bf16[384,3072]{1,0:T(8,128)(2,1)S(1)}, bf16[384,3072]{1,0:T(8,128)(2,1)}, u32[]{:S(2)}) copy-start(bf16[384,3072]{1,0:T(8,128)(2,1)} %w_ref.1) | copy-start | bytes 7077892

commit v3 on v2

--- a/solution.py
+++ b/solution.py
@@ -21,9 +21,9 @@
 PARTS = 4
 PART = 2 * TILES // PARTS
 PIECE = TILE // WORKERS
-GROUP = 16
-STEPS = TILES // GROUP
-LOW = -1e30
+GROUP = 8
+BESIDE = 4
+FAR = 64.0
 SCALE2 = math.log2(math.e) / math.sqrt(DH)
 BF16 = jnp.bfloat16
 F32 = jnp.float32
@@ -315,16 +315,20 @@
 
 
 def attend_kernel(
-    list_ref, q_ref, kv_ref, o_ref, turned_ref, even_ref, odd_ref, even_peak, odd_peak,
-    base_ref, sum_ref,
+    list_ref, q_ref, kv_ref, o_ref, turned_ref, base_ref, peak_ref, sum_ref,
+    slot_of, first_of, listed_of,
 ):
-    kept = ((even_ref, even_peak), (odd_ref, odd_peak))
-
-    def count_of(slot):
-        return list_ref[SLOTS, slot]
-
-    def steps_of(slot):
-        return lax.div(count_of(slot) + GROUP - 1, GROUP)
+    _, column, core = where_is(lax.axis_index("ctx"))
+
+    def loop(count, work):
+        def one(step, carry):
+            work(step)
+            return carry
+
+        lax.fori_loop(0, count, one, 0)
+
+    def rows_of(slot):
+        return pl.ds(pl.multiple_of(slot * TILE, TILE), TILE)
 
     def tile_at(tile):
         start = pl.multiple_of(tile * PIECE, PIECE)
@@ -332,84 +336,97 @@
             [kv_ref[worker, pl.ds(start, PIECE), :] for worker in range(WORKERS)], axis=0
         )
 
-    def score(slot, side, step):
-        score_ref, peak_ref = kept[side]
-        query = q_ref[pl.ds(pl.multiple_of(slot * TILE, TILE), TILE), :]
-        keys = [turned_ref[list_ref[slot, step * GROUP + u]] for u in range(GROUP)]
-        scores = jnp.dot(query, jnp.concatenate(keys, axis=1), preferred_element_type=F32)
-        peak = peak_ref[...]
-        for u in range(GROUP):
-            part = scores[:, u * TILE : (u + 1) * TILE]
-            score_ref[step, :, u * TILE : (u + 1) * TILE] = part
-            peak = jnp.maximum(peak, part)
-        peak_ref[...] = peak
-
-    def gather(slot, side, step):
-        score_ref = kept[side][0]
-        base = base_ref[...]
-        count = count_of(slot)
-        weights, values = [], []
-        for u in range(GROUP):
-            part = score_ref[step, :, u * TILE : (u + 1) * TILE]
-            weights.append(jnp.exp2(part * SCALE2 - base).astype(BF16))
-            listed = step * GROUP + u < count
-            value = jnp.where(listed, tile_at(TILES + list_ref[slot, step * GROUP + u]), 0).astype(BF16)
-            ones = jnp.broadcast_to(jnp.where(listed, 1.0, 0.0).astype(BF16), (TILE, DH))
-            values.append(jnp.concatenate([value, ones], axis=1))
-        sum_ref[...] += jnp.dot(
-            jnp.concatenate(weights, axis=1),
-            jnp.concatenate(values, axis=0),
-            preferred_element_type=F32,
-        )
-
-    def loop(first, last, work):
+    def enlist(slot, total):
+        count = list_ref[SLOTS, slot]
+        steps = lax.div(count + GROUP - 1, GROUP)
+
         def one(step, carry):
-            work(step)
+            slot_of[total + step] = slot
+            first_of[total + step] = step * GROUP
+            listed_of[total + step] = count - step * GROUP
             return carry
 
-        lax.fori_loop(first, last, one, 0)
-
-    def one_slot(slot, side, ahead):
-        here = steps_of(slot)
-        both = jnp.minimum(here, ahead)
-        base = jnp.max(kept[side][1][...], axis=1, keepdims=True) * SCALE2
-        base_ref[...] = jnp.broadcast_to(base, (TILE, TILE))
-        sum_ref[...] = jnp.zeros((TILE, 2 * DH), F32)
-        kept[1 - side][1][...] = jnp.full((TILE, TILE), LOW, F32)
-
-        def pair(step):
-            gather(slot, side, step)
-            score(slot + 1, 1 - side, step)
-
-        loop(0, both, pair)
-        loop(both, ahead, lambda step: score(slot + 1, 1 - side, step))
-        loop(both, here, lambda step: gather(slot, side, step))
-        o_ref[pl.ds(pl.multiple_of(slot * TILE, TILE), TILE), :] = (
-            sum_ref[:, :DH] / sum_ref[:, DH:]
-        ).astype(BF16)
+        lax.fori_loop(0, steps, one, 0)
+        return total + steps
+
+    total = lax.fori_loop(0, SLOTS, enlist, 0)
+    for spare in range(BESIDE - 1):
+        slot_of[total + spare] = 0
+        first_of[total + spare] = 0
+        listed_of[total + spare] = 0
+    turns = lax.div(total + BESIDE - 1, BESIDE)
+    busy = jnp.where(total > 0, 1, 0)
 
     def turn(step):
         for u in range(GROUP):
             tile = step * GROUP + u
             turned_ref[tile] = tile_at(tile).T
 
-    loop(0, jnp.where(count_of(0) > 0, STEPS, 0), turn)
-    even_peak[...] = jnp.full((TILE, TILE), LOW, F32)
-    loop(0, steps_of(0), lambda step: score(0, 0, step))
-
-    def two_slots(turn, carry):
-        slot = turn * 2
-        one_slot(slot, 0, steps_of(slot + 1))
-        follows = jnp.minimum(slot + 2, SLOTS - 1)
-        one_slot(slot + 1, 1, jnp.where(slot + 2 < SLOTS, steps_of(follows), 0))
-        return carry
-
-    lax.fori_loop(0, SLOTS // 2, two_slots, 0)
-    if SLOTS % 2:
-        one_slot(SLOTS - 1, 0, 0)
+    loop(busy * (TILES // GROUP), turn)
+
+    def own_scores(step):
+        for u in range(BESIDE):
+            slot = step * BESIDE + u
+            own = turned_ref[slot * WORKERS + column * 2 + core]
+            peak_ref[slot] = jnp.dot(q_ref[rows_of(slot), :], own, preferred_element_type=F32)
+
+    loop(busy * (SLOTS // BESIDE), own_scores)
+
+    def start(step):
+        for u in range(BESIDE):
+            slot = step * BESIDE + u
+            base = jnp.max(peak_ref[slot], axis=1, keepdims=True) * SCALE2
+            base_ref[slot] = jnp.broadcast_to(base, (TILE, TILE))
+            sum_ref[slot] = jnp.zeros((TILE, 2 * DH), F32)
+
+    def attend_steps(step):
+        found = []
+        for beside in range(BESIDE):
+            number = step * BESIDE + beside
+            slot, first, listed = slot_of[number], first_of[number], listed_of[number]
+            tiles = [list_ref[slot, first + u] for u in range(GROUP)]
+            keys = jnp.concatenate([turned_ref[tile] for tile in tiles], axis=1)
+            scores = jnp.dot(q_ref[rows_of(slot), :], keys, preferred_element_type=F32)
+            base = base_ref[slot]
+            peak, weights, values = None, [], []
+            for u in range(GROUP):
+                part = scores[:, u * TILE : (u + 1) * TILE]
+                peak = part if peak is None else jnp.maximum(peak, part)
+                weights.append(jnp.exp2(part * SCALE2 - base).astype(BF16))
+                value = jnp.where(u < listed, tile_at(TILES + tiles[u]), 0).astype(BF16)
+                ones = jnp.where(u < listed, 1.0, 0.0).astype(BF16)
+                ones = jnp.broadcast_to(ones, (TILE, DH))
+                values.append(jnp.concatenate([value, ones], axis=1))
+            added = jnp.dot(
+                jnp.concatenate(weights, axis=1),
+                jnp.concatenate(values, axis=0),
+                preferred_element_type=F32,
+            )
+            found.append((slot, peak, added))
+        for slot, peak, added in found:
+            peak_ref[slot] = jnp.maximum(peak_ref[slot], peak)
+            sum_ref[slot] += added
+
+    def attempt(number, needed):
+        loop(needed * (SLOTS // BESIDE), start)
+        loop(needed * turns, attend_steps)
+        above = peak_ref[0] * SCALE2 - base_ref[0]
+        for slot in range(1, SLOTS):
+            above = jnp.maximum(above, peak_ref[slot] * SCALE2 - base_ref[slot])
+        return needed * jnp.where(jnp.max(above) > FAR, 1, 0)
+
+    lax.fori_loop(0, 2, attempt, busy)
+
+    def finish(step):
+        for u in range(BESIDE):
+            slot = step * BESIDE + u
+            o_ref[rows_of(slot), :] = (sum_ref[slot, :, :DH] / sum_ref[slot, :, DH:]).astype(BF16)
+
+    loop(busy * (SLOTS // BESIDE), finish)
 
 
 def attend(lists, query, kv):
+    most = SLOTS * (TILES // GROUP) + BESIDE
     return pl.pallas_call(
         attend_kernel,
         out_shape=jax.ShapeDtypeStruct(query.shape, BF16),
@@ -421,12 +438,12 @@
         out_specs=pl.BlockSpec(memory_space=pltpu.VMEM),
         scratch_shapes=[
             pltpu.VMEM((TILES, DH, TILE), BF16),
-            pltpu.VMEM((STEPS, TILE, GROUP * TILE), F32),
-            pltpu.VMEM((STEPS, TILE, GROUP * TILE), F32),
-            pltpu.VMEM((TILE, TILE), F32),
-            pltpu.VMEM((TILE, TILE), F32),
-            pltpu.VMEM((TILE, TILE), F32),
-            pltpu.VMEM((TILE, 2 * DH), F32),
+            pltpu.VMEM((SLOTS, TILE, TILE), F32),
+            pltpu.VMEM((SLOTS, TILE, TILE), F32),
+            pltpu.VMEM((SLOTS, TILE, 2 * DH), F32),
+            pltpu.SMEM((most,), jnp.int32),
+            pltpu.SMEM((most,), jnp.int32),
+            pltpu.SMEM((most,), jnp.int32),
         ],
         compiler_params=pltpu.CompilerParams(vmem_limit_bytes=40 * 1024 * 1024),
     )(lists, query, kv)

time: 123 us -> 145 us (1.18)
  Pallas kernels: 117 us -> 138 us
    pallas_call x1, Pallas kernels: 27.1 us -> 54.2 us  [collect(): pl.pallas_call(collect_kernel, out_shape=jax.ShapeDtypeStruct((PLANES * H...]
    pallas_call x1, Pallas kernels: 33.5 us -> 27.5 us  [attend(): pl.pallas_call(attend_kernel, out_shape=jax.ShapeDtypeStruct(query.shape,...]
where the time goes in v3:
time: 145 us; the launch traced here: 144 us
  Pallas kernels  138 us (95%)
  local copies, waits for them, and re-layouts  6.2 us (4%)
    pallas_call x1, Pallas kernels, collect(): pl.pallas_call(collect_kernel, out_shape=jax.ShapeDtypeStruct((PLANES * H...  54.2 us
    pallas_call x1, Pallas kernels, spread(): pl.pallas_call(spread_kernel, out_shape=(jax.ShapeDtypeStruct((SLOTS, FRA...  52.4 us
    pallas_call x1, Pallas kernels, attend(): pl.pallas_call(attend_kernel, out_shape=jax.ShapeDtypeStruct(query.shape,...  27.5 us
    unnamed x12, local copies, waits for them, and re-layouts  6.2 us

profile of v3, /device:TPU:1, one launch (start us, length us, event | category | flops | bytes accessed | tf_op | source)
XLA Modules:
  0.0 144.3 jit_solution(288299947882432751)
XLA Ops:
  0.0 0.0 copy-start.1
  0.0 1.0 copy-done.1
  1.0 0.0 copy-start.2
  1.0 1.0 copy-done.2
  2.0 0.0 copy-start.3
  2.0 1.0 copy-done.3
  3.0 0.0 copy-start.4
  3.0 0.9 copy-done.4
  3.9 0.0 copy-start.5
  3.9 0.7 copy-done.5
  4.5 1.3 shard_map.64
  5.9 0.0 copy-start
  5.9 1.7 %copy-done = bf16[384,3072]{1,0:T(8,128)(2,1)S(1)} copy-done((bf16[384,3072]{1,0:T(8,128)(2,1)S(1)}, bf16[384,3072]{1,0:T(8,128)(2,1)}, u32[]{:S(2)}) %copy-start) | copy-done | bytes 2359320
  7.5 52.4 %shard_map.65 = (bf16[16,32,4,128]{3,2,1,0:T(4,128)(2,1)S(1)}, bf16[8,256,4,4,128]{4,3,2,1,0:T(4,128)(2,1)S(1)}, bf16[1536,768]{1,0:T(8,128)(2,1)S(1)}) custom-call(bf16[3,16,8,4,128]{4,3,2,1,0:T(4,128)(2,1)S(1)} %bitcast.11, bf16[3,256,4,128]{3,2,1,0:T(4,128)(2,1)S(1)} %bitcast.9, bf16[384,3072]{1,0:T(8,128)(2,1)S(1)} %copy-done), custom_call_target="tpu_custom_call" | custom-call | tf_op jit(solution)/shard_map/pallas_call | solution.py:285
  59.9 27.5 %shard_map.66 = bf16[2048,128]{1,0:T(8,128)(2,1)S(1)} custom-call(s32[17,128]{1,0:T(8,128)S(1)} %get-tuple-element.11.list_ref, bf16[2048,128]{1,0:T(8,128)(2,1)S(1)} %bitcast.10, bf16[8,4096,128]{2,1,0:T(8,128)(2,1)S(1)} %bitcast.6), custom_call_target="tpu_custom_call" | custom-call | tf_op jit(solution)/shard_map/pallas_call | solution.py:430
  87.4 54.2 %shard_map.67 = bf16[12,16,8,4,128]{4,3,2,1,0:T(4,128)(2,1)S(1)} custom-call(bf16[16,32,4,128]{3,2,1,0:T(4,128)(2,1)S(1)} %bitcast.8), custom_call_target="tpu_custom_call" | custom-call | tf_op jit(solution)/shard_map/pallas_call | solution.py:545
  141.6 2.7 %shard_map.68 = bf16[512,768]{1,0:T(8,128)(2,1)} custom-call(bf16[12,512,128]{2,1,0:T(8,128)(2,1)S(1)} %bitcast.7, bf16[1536,768]{1,0:T(8,128)(2,1)S(1)} %get-tuple-element.16.w_ref), custom_call_target="tpu_custom_call" | custom-call | tf_op jit(solution)/shard_map/pallas_call | solution.py:575
Async XLA Ops:
  0.0 1.0 copy-start.1
  1.0 1.0 copy-start.2
  2.0 1.0 copy-start.3
  3.0 0.9 copy-start.4
  3.9 0.7 copy-start.5
  5.9 1.7 %copy-start = (bf16[384,3072]{1,0:T(8,128)(2,1)S(1)}, bf16[384,3072]{1,0:T(8,128)(2,1)}, u32[]{:S(2)}) copy-start(bf16[384,3072]{1,0:T(8,128)(2,1)} %w_ref.1) | copy-start | bytes 7077892

commit v4 on v3

--- a/solution.py
+++ b/solution.py
@@ -23,7 +23,8 @@
 PIECE = TILE // WORKERS
 GROUP = 8
 BESIDE = 4
-FAR = 64.0
+FAR = 2.0**64
+LOW = -1e30
 SCALE2 = math.log2(math.e) / math.sqrt(DH)
 BF16 = jnp.bfloat16
 F32 = jnp.float32
@@ -315,7 +316,7 @@
 
 
 def attend_kernel(
-    list_ref, q_ref, kv_ref, o_ref, turned_ref, base_ref, peak_ref, sum_ref,
+    list_ref, q_ref, kv_ref, o_ref, keys_ref, values_ref, wide_ref, base_ref, peak_ref, sum_ref,
     slot_of, first_of, listed_of,
 ):
     _, column, core = where_is(lax.axis_index("ctx"))
@@ -357,63 +358,94 @@
     turns = lax.div(total + BESIDE - 1, BESIDE)
     busy = jnp.where(total > 0, 1, 0)
 
-    def turn(step):
+    down = lax.broadcasted_iota(jnp.int32, (DH, TILE), 0)
+    last_row = jnp.where(down == DH - 1, 1.0, 0.0).astype(BF16)
+    other_rows = jnp.where(down == DH - 1, 0.0, 1.0).astype(BF16)
+    ones = jnp.ones((TILE, DH), BF16)
+    values_ref[TILES] = jnp.zeros((TILE, 2 * DH), BF16)
+
+    def unpack(step):
         for u in range(GROUP):
             tile = step * GROUP + u
-            turned_ref[tile] = tile_at(tile).T
-
-    loop(busy * (TILES // GROUP), turn)
-
-    def own_scores(step):
+            keys = tile_at(tile).T
+            keys_ref[tile, :DH, :] = keys
+            keys_ref[tile, DH:, :] = keys * other_rows + last_row
+            values_ref[tile, :, :DH] = tile_at(TILES + tile)
+            values_ref[tile, :, DH:] = ones
+
+    loop(busy * (TILES // GROUP), unpack)
+
+    along = lax.broadcasted_iota(jnp.int32, (TILE, DH), 1)
+
+    def widen(slot, base):
+        query = q_ref[rows_of(slot), :].astype(F32) * SCALE2
+        high = query.astype(BF16)
+        low = query - high.astype(F32)
+        return jnp.concatenate([high, jnp.where(along == DH - 1, -base, low).astype(BF16)], axis=1)
+
+    def set_base(slot, base):
+        base = jnp.broadcast_to(base, (TILE, TILE)).astype(BF16).astype(F32)
+        base_ref[slot] = base
+        wide_ref[rows_of(slot), :] = widen(slot, base)
+
+    def own_base(step):
         for u in range(BESIDE):
             slot = step * BESIDE + u
-            own = turned_ref[slot * WORKERS + column * 2 + core]
-            peak_ref[slot] = jnp.dot(q_ref[rows_of(slot), :], own, preferred_element_type=F32)
-
-    loop(busy * (SLOTS // BESIDE), own_scores)
-
-    def start(step):
-        for u in range(BESIDE):
-            slot = step * BESIDE + u
-            base = jnp.max(peak_ref[slot], axis=1, keepdims=True) * SCALE2
-            base_ref[slot] = jnp.broadcast_to(base, (TILE, TILE))
-            sum_ref[slot] = jnp.zeros((TILE, 2 * DH), F32)
+            own = keys_ref[slot * WORKERS + column * 2 + core]
+            scores = jnp.dot(widen(slot, 0.0), own, preferred_element_type=F32)
+            set_base(slot, jnp.max(scores, axis=1, keepdims=True))
+
+    loop(busy * (SLOTS // BESIDE), own_base)
+
+    def scores_of(number):
+        slot, first = slot_of[number], first_of[number]
+        tiles = [list_ref[slot, first + u] for u in range(GROUP)]
+        keys = jnp.concatenate([keys_ref[tile] for tile in tiles], axis=1)
+        scores = jnp.dot(wide_ref[rows_of(slot), :], keys, preferred_element_type=F32)
+        return slot, tiles, scores
 
     def attend_steps(step):
         found = []
         for beside in range(BESIDE):
             number = step * BESIDE + beside
-            slot, first, listed = slot_of[number], first_of[number], listed_of[number]
-            tiles = [list_ref[slot, first + u] for u in range(GROUP)]
-            keys = jnp.concatenate([turned_ref[tile] for tile in tiles], axis=1)
-            scores = jnp.dot(q_ref[rows_of(slot), :], keys, preferred_element_type=F32)
-            base = base_ref[slot]
-            peak, weights, values = None, [], []
+            slot, tiles, scores = scores_of(number)
+            listed = listed_of[number]
+            values = [values_ref[jnp.where(u < listed, tiles[u], TILES)] for u in range(GROUP)]
+            weights = jnp.exp2(scores).astype(BF16)
+            added = jnp.dot(
+                weights, jnp.concatenate(values, axis=0), preferred_element_type=F32
+            )
+            found.append((slot, added))
+        for slot, added in found:
+            sum_ref[slot] += added
+
+    def peak_steps(step):
+        for beside in range(BESIDE):
+            slot, _, scores = scores_of(step * BESIDE + beside)
+            peak = peak_ref[slot]
             for u in range(GROUP):
-                part = scores[:, u * TILE : (u + 1) * TILE]
-                peak = part if peak is None else jnp.maximum(peak, part)
-                weights.append(jnp.exp2(part * SCALE2 - base).astype(BF16))
-                value = jnp.where(u < listed, tile_at(TILES + tiles[u]), 0).astype(BF16)
-                ones = jnp.where(u < listed, 1.0, 0.0).astype(BF16)
-                ones = jnp.broadcast_to(ones, (TILE, DH))
-                values.append(jnp.concatenate([value, ones], axis=1))
-            added = jnp.dot(
-                jnp.concatenate(weights, axis=1),
-                jnp.concatenate(values, axis=0),
-                preferred_element_type=F32,
-            )
-            found.append((slot, peak, added))
-        for slot, peak, added in found:
-            peak_ref[slot] = jnp.maximum(peak_ref[slot], peak)
-            sum_ref[slot] += added
+                peak = jnp.maximum(peak, scores[:, u * TILE : (u + 1) * TILE])
+            peak_ref[slot] = peak
 
     def attempt(number, needed):
-        loop(needed * (SLOTS // BESIDE), start)
+        def clear(slot):
+            sum_ref[slot] = jnp.zeros((TILE, 2 * DH), F32)
+            peak_ref[slot] = jnp.full((TILE, TILE), LOW, F32)
+
+        loop(needed * SLOTS, clear)
         loop(needed * turns, attend_steps)
-        above = peak_ref[0] * SCALE2 - base_ref[0]
-        for slot in range(1, SLOTS):
-            above = jnp.maximum(above, peak_ref[slot] * SCALE2 - base_ref[slot])
-        return needed * jnp.where(jnp.max(above) > FAR, 1, 0)
+        beyond = jnp.zeros((TILE, DH), F32)
+        for slot in range(SLOTS):
+            beyond = jnp.where(sum_ref[slot, :, DH:] <= FAR, beyond, 1.0)
+        again = needed * jnp.where(jnp.max(beyond) > 0.0, 1, 0)
+        loop(again * turns, peak_steps)
+
+        def rebase(slot):
+            above = jnp.max(peak_ref[slot], axis=1, keepdims=True)
+            set_base(slot, base_ref[slot] + above)
+
+        loop(again * SLOTS, rebase)
+        return again
 
     lax.fori_loop(0, 2, attempt, busy)
 
@@ -437,7 +469,9 @@
         ],
         out_specs=pl.BlockSpec(memory_space=pltpu.VMEM),
         scratch_shapes=[
-            pltpu.VMEM((TILES, DH, TILE), BF16),
+            pltpu.VMEM((TILES, 2 * DH, TILE), BF16),
+            pltpu.VMEM((TILES + 1, TILE, 2 * DH), BF16),
+            pltpu.VMEM((SLOTS * TILE, 2 * DH), BF16),
             pltpu.VMEM((SLOTS, TILE, TILE), F32),
             pltpu.VMEM((SLOTS, TILE, TILE), F32),
             pltpu.VMEM((SLOTS, TILE, 2 * DH), F32),

time: 145 us -> 159 us (1.097)
  Pallas kernels: 138 us -> 153 us
    pallas_call x1, Pallas kernels: 54.2 us -> 67 us  [collect(): pl.pallas_call(collect_kernel, out_shape=jax.ShapeDtypeStruct((PLANES * H...]
    pallas_call x1, Pallas kernels: 27.5 us -> 29.3 us  [attend(): pl.pallas_call(attend_kernel, out_shape=jax.ShapeDtypeStruct(query.shape,...]
where the time goes in v4:
time: 159 us
  Pallas kernels  153 us (96%)
  local copies, waits for them, and re-layouts  6.2 us (4%)
    pallas_call x1, Pallas kernels, collect(): pl.pallas_call(collect_kernel, out_shape=jax.ShapeDtypeStruct((PLANES * H...  67 us
    pallas_call x1, Pallas kernels, spread(): pl.pallas_call(spread_kernel, out_shape=(jax.ShapeDtypeStruct((SLOTS, FRA...  52.4 us
    pallas_call x1, Pallas kernels, attend(): pl.pallas_call(attend_kernel, out_shape=jax.ShapeDtypeStruct(query.shape,...  29.3 us
    unnamed x12, local copies, waits for them, and re-layouts  6.2 us

profile of v4, /device:TPU:1, one launch (start us, length us, event | category | flops | bytes accessed | tf_op | source)
XLA Modules:
  0.0 158.8 jit_solution(7087476661224363682)
XLA Ops:
  0.0 0.0 copy-start.1
  0.0 1.0 copy-done.1
  1.0 0.0 copy-start.2
  1.0 1.0 copy-done.2
  2.0 0.0 copy-start.3
  2.0 1.0 copy-done.3
  3.0 0.0 copy-start.4
  3.0 0.9 copy-done.4
  3.9 0.0 copy-start.5
  3.9 0.7 copy-done.5
  4.5 1.3 shard_map.64
  5.9 0.0 copy-start
  5.9 1.7 %copy-done = bf16[384,3072]{1,0:T(8,128)(2,1)S(1)} copy-done((bf16[384,3072]{1,0:T(8,128)(2,1)S(1)}, bf16[384,3072]{1,0:T(8,128)(2,1)}, u32[]{:S(2)}) %copy-start) | copy-done | bytes 2359320
  7.5 52.4 %shard_map.65 = (bf16[16,32,4,128]{3,2,1,0:T(4,128)(2,1)S(1)}, bf16[8,256,4,4,128]{4,3,2,1,0:T(4,128)(2,1)S(1)}, bf16[1536,768]{1,0:T(8,128)(2,1)S(1)}) custom-call(bf16[3,16,8,4,128]{4,3,2,1,0:T(4,128)(2,1)S(1)} %bitcast.11, bf16[3,256,4,128]{3,2,1,0:T(4,128)(2,1)S(1)} %bitcast.9, bf16[384,3072]{1,0:T(8,128)(2,1)S(1)} %copy-done), custom_call_target="tpu_custom_call" | custom-call | tf_op jit(solution)/shard_map/pallas_call | solution.py:286
  59.9 29.3 %shard_map.66 = bf16[2048,128]{1,0:T(8,128)(2,1)S(1)} custom-call(s32[17,128]{1,0:T(8,128)S(1)} %get-tuple-element.11.list_ref, bf16[2048,128]{1,0:T(8,128)(2,1)S(1)} %bitcast.10, bf16[8,4096,128]{2,1,0:T(8,128)(2,1)S(1)} %bitcast.6), custom_call_target="tpu_custom_call" | custom-call | tf_op jit(solution)/shard_map/pallas_call | solution.py:462
  89.2 67.0 %shard_map.67 = bf16[12,16,8,4,128]{4,3,2,1,0:T(4,128)(2,1)S(1)} custom-call(bf16[16,32,4,128]{3,2,1,0:T(4,128)(2,1)S(1)} %bitcast.8), custom_call_target="tpu_custom_call" | custom-call | tf_op jit(solution)/shard_map/pallas_call | solution.py:579
  156.2 2.7 %shard_map.68 = bf16[512,768]{1,0:T(8,128)(2,1)} custom-call(bf16[12,512,128]{2,1,0:T(8,128)(2,1)S(1)} %bitcast.7, bf16[1536,768]{1,0:T(8,128)(2,1)S(1)} %get-tuple-element.16.w_ref), custom_call_target="tpu_custom_call" | custom-call | tf_op jit(solution)/shard_map/pallas_call | solution.py:609
Async XLA Ops:
  0.0 1.0 copy-start.1
  1.0 1.0 copy-start.2
  2.0 1.0 copy-start.3
  3.0 0.9 copy-start.4
  3.9 0.7 copy-start.5
  5.9 1.7 %copy-start = (bf16[384,3072]{1,0:T(8,128)(2,1)S(1)}, bf16[384,3072]{1,0:T(8,128)(2,1)}, u32[]{:S(2)}) copy-start(bf16[384,3072]{1,0:T(8,128)(2,1)} %w_ref.1) | copy-start | bytes 7077892

commit v5 on v4

--- a/solution.py
+++ b/solution.py
@@ -316,7 +316,7 @@
 
 
 def attend_kernel(
-    list_ref, q_ref, kv_ref, o_ref, keys_ref, values_ref, wide_ref, base_ref, peak_ref, sum_ref,
+    list_ref, q_ref, kv_ref, o_ref, keys_ref, values_ref, base_ref, peak_ref, sum_ref,
     slot_of, first_of, listed_of,
 ):
     _, column, core = where_is(lax.axis_index("ctx"))
@@ -358,62 +358,57 @@
     turns = lax.div(total + BESIDE - 1, BESIDE)
     busy = jnp.where(total > 0, 1, 0)
 
-    down = lax.broadcasted_iota(jnp.int32, (DH, TILE), 0)
-    last_row = jnp.where(down == DH - 1, 1.0, 0.0).astype(BF16)
-    other_rows = jnp.where(down == DH - 1, 0.0, 1.0).astype(BF16)
-    ones = jnp.ones((TILE, DH), BF16)
-    values_ref[TILES] = jnp.zeros((TILE, 2 * DH), BF16)
+    values_ref[TILES] = jnp.zeros((TILE, DH), BF16)
 
     def unpack(step):
         for u in range(GROUP):
             tile = step * GROUP + u
-            keys = tile_at(tile).T
-            keys_ref[tile, :DH, :] = keys
-            keys_ref[tile, DH:, :] = keys * other_rows + last_row
-            values_ref[tile, :, :DH] = tile_at(TILES + tile)
-            values_ref[tile, :, DH:] = ones
+            keys_ref[tile] = tile_at(tile).T
+            values_ref[tile] = tile_at(TILES + tile)
 
     loop(busy * (TILES // GROUP), unpack)
 
-    along = lax.broadcasted_iota(jnp.int32, (TILE, DH), 1)
-
-    def widen(slot, base):
-        query = q_ref[rows_of(slot), :].astype(F32) * SCALE2
-        high = query.astype(BF16)
-        low = query - high.astype(F32)
-        return jnp.concatenate([high, jnp.where(along == DH - 1, -base, low).astype(BF16)], axis=1)
-
     def set_base(slot, base):
-        base = jnp.broadcast_to(base, (TILE, TILE)).astype(BF16).astype(F32)
-        base_ref[slot] = base
-        wide_ref[rows_of(slot), :] = widen(slot, base)
+        base_ref[slot] = jnp.broadcast_to(base * SCALE2, (TILE, TILE))
 
     def own_base(step):
         for u in range(BESIDE):
             slot = step * BESIDE + u
             own = keys_ref[slot * WORKERS + column * 2 + core]
-            scores = jnp.dot(widen(slot, 0.0), own, preferred_element_type=F32)
+            scores = jnp.dot(q_ref[rows_of(slot), :], own, preferred_element_type=F32)
             set_base(slot, jnp.max(scores, axis=1, keepdims=True))
 
     loop(busy * (SLOTS // BESIDE), own_base)
 
-    def scores_of(number):
+    def tiles_of(number):
         slot, first = slot_of[number], first_of[number]
-        tiles = [list_ref[slot, first + u] for u in range(GROUP)]
+        return slot, [list_ref[slot, first + u] for u in range(GROUP)]
+
+    def scores_of(slot, tiles):
         keys = jnp.concatenate([keys_ref[tile] for tile in tiles], axis=1)
-        scores = jnp.dot(wide_ref[rows_of(slot), :], keys, preferred_element_type=F32)
-        return slot, tiles, scores
+        return jnp.dot(q_ref[rows_of(slot), :], keys, preferred_element_type=F32)
 
     def attend_steps(step):
         found = []
         for beside in range(BESIDE):
             number = step * BESIDE + beside
-            slot, tiles, scores = scores_of(number)
+            slot, tiles = tiles_of(number)
             listed = listed_of[number]
-            values = [values_ref[jnp.where(u < listed, tiles[u], TILES)] for u in range(GROUP)]
-            weights = jnp.exp2(scores).astype(BF16)
+            base = base_ref[slot]
+            base = jnp.concatenate([base, base], axis=1)
+            weights, values = [], []
+            for u in range(0, GROUP, 2):
+                scores = scores_of(slot, tiles[u : u + 2])
+                weights.append(jnp.exp2(scores * SCALE2 - base).astype(BF16))
+            for u in range(GROUP):
+                value = values_ref[jnp.where(u < listed, tiles[u], TILES)]
+                ones = jnp.where(u < listed, 1.0, 0.0).astype(BF16)
+                ones = jnp.broadcast_to(ones, (TILE, DH))
+                values.append(jnp.concatenate([value, ones], axis=1))
             added = jnp.dot(
-                weights, jnp.concatenate(values, axis=0), preferred_element_type=F32
+                jnp.concatenate(weights, axis=1),
+                jnp.concatenate(values, axis=0),
+                preferred_element_type=F32,
             )
             found.append((slot, added))
         for slot, added in found:
@@ -421,7 +416,8 @@
 
     def peak_steps(step):
         for beside in range(BESIDE):
-            slot, _, scores = scores_of(step * BESIDE + beside)
+            slot, tiles = tiles_of(step * BESIDE + beside)
+            scores = scores_of(slot, tiles)
             peak = peak_ref[slot]
             for u in range(GROUP):
                 peak = jnp.maximum(peak, scores[:, u * TILE : (u + 1) * TILE])
@@ -441,8 +437,7 @@
         loop(again * turns, peak_steps)
 
         def rebase(slot):
-            above = jnp.max(peak_ref[slot], axis=1, keepdims=True)
-            set_base(slot, base_ref[slot] + above)
+            set_base(slot, jnp.max(peak_ref[slot], axis=1, keepdims=True))
 
         loop(again * SLOTS, rebase)
         return again
@@ -469,9 +464,8 @@
         ],
         out_specs=pl.BlockSpec(memory_space=pltpu.VMEM),
         scratch_shapes=[
-            pltpu.VMEM((TILES, 2 * DH, TILE), BF16),
-            pltpu.VMEM((TILES + 1, TILE, 2 * DH), BF16),
-            pltpu.VMEM((SLOTS * TILE, 2 * DH), BF16),
+            pltpu.VMEM((TILES, DH, TILE), BF16),
+            pltpu.VMEM((TILES + 1, TILE, DH), BF16),
             pltpu.VMEM((SLOTS, TILE, TILE), F32),
             pltpu.VMEM((SLOTS, TILE, TILE), F32),
             pltpu.VMEM((SLOTS, TILE, 2 * DH), F32),

time: 159 us -> 155 us (0.975)
  Pallas kernels: 153 us -> 148 us
    pallas_call x1, Pallas kernels: 67 us -> 64.7 us  [collect(): pl.pallas_call(collect_kernel, out_shape=jax.ShapeDtypeStruct((PLANES * H...]
    pallas_call x1, Pallas kernels: 29.3 us -> 27.2 us  [attend(): pl.pallas_call(attend_kernel, out_shape=jax.ShapeDtypeStruct(query.shape,...]
where the time goes in v5:
time: 155 us
  Pallas kernels  148 us (95%)
  local copies, waits for them, and re-layouts  6.2 us (4%)
    pallas_call x1, Pallas kernels, collect(): pl.pallas_call(collect_kernel, out_shape=jax.ShapeDtypeStruct((PLANES * H...  64.7 us
    pallas_call x1, Pallas kernels, spread(): pl.pallas_call(spread_kernel, out_shape=(jax.ShapeDtypeStruct((SLOTS, FRA...  52.4 us
    pallas_call x1, Pallas kernels, attend(): pl.pallas_call(attend_kernel, out_shape=jax.ShapeDtypeStruct(query.shape,...  27.2 us
    unnamed x12, local copies, waits for them, and re-layouts  6.2 us

profile of v5, /device:TPU:1, one launch (start us, length us, event | category | flops | bytes accessed | tf_op | source)
XLA Modules:
  0.0 154.6 jit_solution(16138591172967726353)
XLA Ops:
  0.0 0.0 copy-start.1
  0.0 1.0 copy-done.1
  1.0 0.0 copy-start.2
  1.0 1.0 copy-done.2
  2.0 0.0 copy-start.3
  2.0 1.0 copy-done.3
  3.0 0.0 copy-start.4
  3.0 0.9 copy-done.4
  3.9 0.0 copy-start.5
  3.9 0.7 copy-done.5
  4.5 1.3 shard_map.64
  5.9 0.0 copy-start
  5.9 1.7 %copy-done = bf16[384,3072]{1,0:T(8,128)(2,1)S(1)} copy-done((bf16[384,3072]{1,0:T(8,128)(2,1)S(1)}, bf16[384,3072]{1,0:T(8,128)(2,1)}, u32[]{:S(2)}) %copy-start) | copy-done | bytes 2359320
  7.5 52.4 %shard_map.65 = (bf16[16,32,4,128]{3,2,1,0:T(4,128)(2,1)S(1)}, bf16[8,256,4,4,128]{4,3,2,1,0:T(4,128)(2,1)S(1)}, bf16[1536,768]{1,0:T(8,128)(2,1)S(1)}) custom-call(bf16[3,16,8,4,128]{4,3,2,1,0:T(4,128)(2,1)S(1)} %bitcast.11, bf16[3,256,4,128]{3,2,1,0:T(4,128)(2,1)S(1)} %bitcast.9, bf16[384,3072]{1,0:T(8,128)(2,1)S(1)} %copy-done), custom_call_target="tpu_custom_call" | custom-call | tf_op jit(solution)/shard_map/pallas_call | solution.py:286
  59.9 27.2 %shard_map.66 = bf16[2048,128]{1,0:T(8,128)(2,1)S(1)} custom-call(s32[17,128]{1,0:T(8,128)S(1)} %get-tuple-element.11.list_ref, bf16[2048,128]{1,0:T(8,128)(2,1)S(1)} %bitcast.10, bf16[8,4096,128]{2,1,0:T(8,128)(2,1)S(1)} %bitcast.6), custom_call_target="tpu_custom_call" | custom-call | tf_op jit(solution)/shard_map/pallas_call | solution.py:457
  87.1 64.7 %shard_map.67 = bf16[12,16,8,4,128]{4,3,2,1,0:T(4,128)(2,1)S(1)} custom-call(bf16[16,32,4,128]{3,2,1,0:T(4,128)(2,1)S(1)} %bitcast.8), custom_call_target="tpu_custom_call" | custom-call | tf_op jit(solution)/shard_map/pallas_call | solution.py:573
  151.9 2.7 %shard_map.68 = bf16[512,768]{1,0:T(8,128)(2,1)} custom-call(bf16[12,512,128]{2,1,0:T(8,128)(2,1)S(1)} %bitcast.7, bf16[1536,768]{1,0:T(8,128)(2,1)S(1)} %get-tuple-element.16.w_ref), custom_call_target="tpu_custom_call" | custom-call | tf_op jit(solution)/shard_map/pallas_call | solution.py:603
Async XLA Ops:
  0.0 1.0 copy-start.1
  1.0 1.0 copy-start.2
  2.0 1.0 copy-start.3
  3.0 0.9 copy-start.4
  3.9 0.7 copy-start.5
  5.9 1.7 %copy-start = (bf16[384,3072]{1,0:T(8,128)(2,1)S(1)}, bf16[384,3072]{1,0:T(8,128)(2,1)}, u32[]{:S(2)}) copy-start(bf16[384,3072]{1,0:T(8,128)(2,1)} %w_ref.1) | copy-start | bytes 7077892

commit v6 on v5

--- a/solution.py
+++ b/solution.py
@@ -20,6 +20,7 @@
 SLOTS = TILES // WORKERS
 PARTS = 4
 PART = 2 * TILES // PARTS
+DETOURS = 2
 PIECE = TILE // WORKERS
 GROUP = 8
 BESIDE = 4
@@ -30,22 +31,27 @@
 F32 = jnp.float32
 
 
-def where_is(device):
-    return lax.div(device, WORKERS), lax.rem(lax.div(device, 2), SIDE), lax.rem(device, 2)
-
-
-def device_at(row, column, core):
-    return (lax.rem(row, SIDE) * SIDE + lax.rem(column, SIDE)) * 2 + core
+def where_is(device, plane):
+    z, y = lax.div(device, 2 * SIDE), lax.rem(lax.div(device, 2), SIDE)
+    odd = lax.rem(plane, 2)
+    return z + odd * (y - z), y + odd * (z - y), lax.rem(device, 2)
+
+
+def device_at(row, column, core, plane):
+    row, column = lax.rem(row, SIDE), lax.rem(column, SIDE)
+    odd = lax.rem(plane, 2)
+    return ((row + odd * (column - row)) * SIDE + column + odd * (row - column)) * 2 + core
 
 
 def spread_kernel(
     q_ref, kv_ref, w_ref, q_all, kv_all, w_all,
     q_send, q_recv, z_send, z_recv, y_send, y_recv, far_send, far_recv,
     core_send, core_recv, w_send, w_recv, w_core_send, w_core_recv, own_sem,
+    held, passed, leg_send, leg_recv,
 ):
     plane = lax.axis_index("heads")
     me = lax.axis_index("ctx")
-    row, column, core = where_is(me)
+    row, column, core = where_is(me, plane)
     working = row < HEADS_HERE
     own_row = jnp.minimum(row, HEADS_HERE - 1)
     depth = w_ref.shape[0]
@@ -81,7 +87,7 @@
             dst_ref=kv_all.at[column * 2 + core, span(part), hop],
             send_sem=z_send.at[part, hop],
             recv_sem=z_recv.at[part, hop],
-            device_id=(plane, device_at(there, column, core)),
+            device_id=(plane, device_at(there, column, core, plane)),
             device_id_type=MESH,
         )
 
@@ -97,7 +103,7 @@
             dst_ref=piece(number, 0),
             send_sem=y_send.at[number, side],
             recv_sem=y_recv.at[number, side],
-            device_id=(plane, device_at(row, column + sides[side], core)),
+            device_id=(plane, device_at(row, column + sides[side], core, plane)),
             device_id_type=MESH,
         )
 
@@ -114,9 +120,58 @@
             dst_ref=chunk,
             send_sem=far_send.at[number, side],
             recv_sem=far_recv.at[number, side],
-            device_id=(plane, device_at(row, column + sides[side], core)),
-            device_id_type=MESH,
-        )
+            device_id=(plane, device_at(row, column + sides[side], core, plane)),
+            device_id_type=MESH,
+        )
+
+    other_row, other_column, _ = where_is(me, plane + 1)
+    relaying = other_row < HEADS_HERE
+
+    def next_plane(side):
+        return lax.rem(plane + sides[side], PLANES)
+
+    def first_leg(number, side):
+        return pltpu.make_async_remote_copy(
+            src_ref=piece(number, 0),
+            dst_ref=held.at[number - 1, side],
+            send_sem=leg_send.at[0, number - 1, side],
+            recv_sem=leg_recv.at[0, number - 1, side],
+            device_id=(next_plane(side), me),
+            device_id_type=MESH,
+        )
+
+    def second_leg(number, side):
+        there = device_at(other_row, other_column + sides[side], core, plane + 1)
+        return pltpu.make_async_remote_copy(
+            src_ref=held.at[number - 1, side],
+            dst_ref=passed.at[number - 1, side],
+            send_sem=leg_send.at[1, number - 1, side],
+            recv_sem=leg_recv.at[1, number - 1, side],
+            device_id=(plane, there),
+            device_id_type=MESH,
+        )
+
+    def third_leg(number, side):
+        source = lax.rem(other_column + sides[1 - side], SIDE) * 2 + core
+        return pltpu.make_async_remote_copy(
+            src_ref=passed.at[number - 1, side],
+            dst_ref=kv_all.at[source, span(number - 1), pl.ds(1, SIDE - 1)],
+            send_sem=leg_send.at[2, number - 1, side],
+            recv_sem=y_recv.at[number, side],
+            device_id=(next_plane(1 - side), me),
+            device_id_type=MESH,
+        )
+
+    def relay(leg, number):
+        @pl.when(relaying)
+        def _():
+            for side in range(2):
+                if leg == 1:
+                    first_leg(number, side).wait_recv()
+                    second_leg(number, side).start()
+                else:
+                    second_leg(number, side).wait_recv()
+                    third_leg(number, side).start()
 
     def core_copy(number, away):
         return pltpu.make_async_remote_copy(
@@ -124,7 +179,7 @@
             dst_ref=piece(number, away),
             send_sem=core_send.at[number, away],
             recv_sem=core_recv,
-            device_id=(plane, device_at(row, column, 1 - core)),
+            device_id=(plane, device_at(row, column, 1 - core, plane)),
             device_id_type=MESH,
         )
 
@@ -154,7 +209,7 @@
             dst_ref=rows,
             send_sem=w_core_send.at[hop],
             recv_sem=w_core_recv.at[hop],
-            device_id=(plane, device_at(row, column, 1 - core)),
+            device_id=(plane, device_at(row, column, 1 - core, plane)),
             device_id_type=MESH,
         )
 
@@ -166,7 +221,7 @@
 
     def q_copy(step):
         there = lax.rem(me + step, FRAMES)
-        row_there, column_there, core_there = where_is(there)
+        row_there, column_there, core_there = where_is(there, plane)
         return row_there < HEADS_HERE, pltpu.make_async_remote_copy(
             src_ref=q_ref.at[
                 jnp.minimum(row_there, HEADS_HERE - 1), :, column_there * 2 + core_there
@@ -223,11 +278,6 @@
         if part + 1 < PARTS:
             to_rows(part + 1, lambda copy: copy.start())
 
-    @pl.when(jnp.logical_not(working))
-    def _():
-        for part in range(PARTS):
-            next_rows(part)
-
     @pl.when(working)
     def _():
         pltpu.make_async_copy(
@@ -236,24 +286,47 @@
         own_copy.wait()
         core_copy(0, 0).start()
 
-        def pass_on(number):
+    def gathered(part):
+        next_rows(part)
+
+        @pl.when(working)
+        def _():
+            for hop in range(1, SIDE):
+                landed = kv_all.at[column * 2 + core, span(part), hop]
+                pltpu.make_async_copy(landed, landed, z_recv.at[part, hop]).wait()
+            for side in range(2):
+                if part < DETOURS:
+                    first_leg(part + 1, side).start()
+                else:
+                    y_copy(part + 1, side).start()
+            core_copy(part + 1, 0).start()
+
+    def pass_on(number):
+        @pl.when(working)
+        def _():
             for side in range(2):
                 y_copy(number, side).wait_recv()
                 far_copy(number, side).start()
             for side in range(2):
                 core_copy(number, sides[1 - side]).start()
 
-        for part in range(PARTS):
-            next_rows(part)
-            for hop in range(1, SIDE):
-                landed = kv_all.at[column * 2 + core, span(part), hop]
-                pltpu.make_async_copy(landed, landed, z_recv.at[part, hop]).wait()
-            for side in range(2):
-                y_copy(part + 1, side).start()
-            core_copy(part + 1, 0).start()
-            pass_on(part)
-        pass_on(PARTS)
-        for number in range(PARTS + 1):
+    gathered(0)
+    gathered(1)
+    pass_on(0)
+    relay(1, 1)
+    gathered(2)
+    relay(1, 2)
+    gathered(3)
+    relay(2, 1)
+    pass_on(3)
+    relay(2, 2)
+    pass_on(1)
+    pass_on(4)
+    pass_on(2)
+
+    @pl.when(working)
+    def _():
+        for number in (0, 3, 1, 4, 2):
             for side in range(2):
                 far_copy(number, side).wait_recv()
             core_copy(number, 2).start()
@@ -269,10 +342,20 @@
         pltpu.make_async_copy(other, other, core_recv).wait()
         for number in range(PARTS + 1):
             for side in range(2):
-                y_copy(number, side).wait_send()
+                if 0 < number <= DETOURS:
+                    first_leg(number, side).wait_send()
+                else:
+                    y_copy(number, side).wait_send()
                 far_copy(number, side).wait_send()
             for away in range(SIDE):
                 core_copy(number, away).wait_send()
+
+    @pl.when(relaying)
+    def _():
+        for number in range(1, DETOURS + 1):
+            for side in range(2):
+                second_leg(number, side).wait_send()
+                third_leg(number, side).wait_send()
 
     own_w.wait()
     lax.fori_loop(1, FRAMES, sent_q, 0)
@@ -308,9 +391,13 @@
             pltpu.SemaphoreType.DMA((PLANES,)),
             pltpu.SemaphoreType.DMA((PLANES,)),
             pltpu.SemaphoreType.DMA,
+            pltpu.VMEM((DETOURS, 2, PART, SIDE - 1, SPOTS, DH), BF16),
+            pltpu.VMEM((DETOURS, 2, PART, SIDE - 1, SPOTS, DH), BF16),
+            pltpu.SemaphoreType.DMA((3, DETOURS, 2)),
+            pltpu.SemaphoreType.DMA((2, DETOURS, 2)),
         ],
         compiler_params=pltpu.CompilerParams(
-            collective_id=0, has_side_effects=True, vmem_limit_bytes=4 * 1024 * 1024
+            collective_id=0, has_side_effects=True, vmem_limit_bytes=12 * 1024 * 1024
         ),
     )(q_parts, kv_parts, out_weight)
 
@@ -319,7 +406,7 @@
     list_ref, q_ref, kv_ref, o_ref, keys_ref, values_ref, base_ref, peak_ref, sum_ref,
     slot_of, first_of, listed_of,
 ):
-    _, column, core = where_is(lax.axis_index("ctx"))
+    _, column, core = where_is(lax.axis_index("ctx"), lax.axis_index("heads"))
 
     def loop(count, work):
         def one(step, carry):
@@ -480,7 +567,7 @@
 def collect_kernel(o_ref, attn, send, recv, x_send, x_recv):
     plane = lax.axis_index("heads")
     me = lax.axis_index("ctx")
-    row, column, core = where_is(me)
+    row, column, core = where_is(me, plane)
     barrier = pltpu.get_barrier_semaphore()
 
     def greet(step, carry):
@@ -615,7 +702,7 @@
 
 def arrange_kernel(pattern_ref, mask_ref, q_ref, k_ref, v_ref, q_out, kv_out, list_ref):
     me = lax.axis_index("ctx")
-    row, column, core = where_is(me)
+    row, column, core = where_is(me, lax.axis_index("heads"))
     rows = q_ref.shape[0]
     for head in range(HEADS_HERE):
         columns = slice(head * DH, (head + 1) * DH)

time: 155 us -> 164 us (1.058)
  Pallas kernels: 148 us -> 157 us
    pallas_call x1, Pallas kernels: 27.2 us -> 30.8 us  [attend(): pl.pallas_call(attend_kernel, out_shape=jax.ShapeDtypeStruct(query.shape,...]
    pallas_call x1, Pallas kernels: 64.7 us -> 67.4 us  [collect(): pl.pallas_call(collect_kernel, out_shape=jax.ShapeDtypeStruct((PLANES * H...]
    pallas_call x1, Pallas kernels: 52.4 us -> 54.4 us  [spread(): pl.pallas_call(spread_kernel, out_shape=(jax.ShapeDtypeStruct((SLOTS, FRA...]
where the time goes in v6:
time: 164 us; the launch traced here: 163 us
  Pallas kernels  157 us (96%)
  local copies, waits for them, and re-layouts  6.2 us (4%)
    pallas_call x1, Pallas kernels, collect(): pl.pallas_call(collect_kernel, out_shape=jax.ShapeDtypeStruct((PLANES * H...  67.4 us
    pallas_call x1, Pallas kernels, spread(): pl.pallas_call(spread_kernel, out_shape=(jax.ShapeDtypeStruct((SLOTS, FRA...  54.4 us
    pallas_call x1, Pallas kernels, attend(): pl.pallas_call(attend_kernel, out_shape=jax.ShapeDtypeStruct(query.shape,...  30.8 us
    unnamed x12, local copies, waits for them, and re-layouts  6.2 us

profile of v6, /device:TPU:1, one launch (start us, length us, event | category | flops | bytes accessed | tf_op | source)
XLA Modules:
  0.0 162.9 jit_solution(2522579028948095520)
XLA Ops:
  0.0 0.0 copy-start.1
  0.0 1.0 copy-done.1
  1.0 0.0 copy-start.2
  1.0 1.0 copy-done.2
  2.0 0.0 copy-start.3
  2.0 1.0 copy-done.3
  3.0 0.0 copy-start.4
  3.0 0.9 copy-done.4
  3.9 0.0 copy-start.5
  3.9 0.7 copy-done.5
  4.5 1.3 shard_map.64
  5.9 0.0 copy-start
  5.9 1.7 %copy-done = bf16[384,3072]{1,0:T(8,128)(2,1)S(1)} copy-done((bf16[384,3072]{1,0:T(8,128)(2,1)S(1)}, bf16[384,3072]{1,0:T(8,128)(2,1)}, u32[]{:S(2)}) %copy-start) | copy-done | bytes 2359320
  7.5 54.4 %shard_map.65 = (bf16[16,32,4,128]{3,2,1,0:T(4,128)(2,1)S(1)}, bf16[8,256,4,4,128]{4,3,2,1,0:T(4,128)(2,1)S(1)}, bf16[1536,768]{1,0:T(8,128)(2,1)S(1)}) custom-call(bf16[3,16,8,4,128]{4,3,2,1,0:T(4,128)(2,1)S(1)} %bitcast.11, bf16[3,256,4,128]{3,2,1,0:T(4,128)(2,1)S(1)} %bitcast.9, bf16[384,3072]{1,0:T(8,128)(2,1)S(1)} %copy-done), custom_call_target="tpu_custom_call" | custom-call | tf_op jit(solution)/shard_map/pallas_call | solution.py:369
  61.9 30.8 %shard_map.66 = bf16[2048,128]{1,0:T(8,128)(2,1)S(1)} custom-call(s32[17,128]{1,0:T(8,128)S(1)} %get-tuple-element.11.list_ref, bf16[2048,128]{1,0:T(8,128)(2,1)S(1)} %bitcast.10, bf16[8,4096,128]{2,1,0:T(8,128)(2,1)S(1)} %bitcast.6), custom_call_target="tpu_custom_call" | custom-call | tf_op jit(solution)/shard_map/pallas_call | solution.py:544
  92.7 67.4 %shard_map.67 = bf16[12,16,8,4,128]{4,3,2,1,0:T(4,128)(2,1)S(1)} custom-call(bf16[16,32,4,128]{3,2,1,0:T(4,128)(2,1)S(1)} %bitcast.8), custom_call_target="tpu_custom_call" | custom-call | tf_op jit(solution)/shard_map/pallas_call | solution.py:660
  160.2 2.7 %shard_map.68 = bf16[512,768]{1,0:T(8,128)(2,1)} custom-call(bf16[12,512,128]{2,1,0:T(8,128)(2,1)S(1)} %bitcast.7, bf16[1536,768]{1,0:T(8,128)(2,1)S(1)} %get-tuple-element.16.w_ref), custom_call_target="tpu_custom_call" | custom-call | tf_op jit(solution)/shard_map/pallas_call | solution.py:690
Async XLA Ops:
  0.0 1.0 copy-start.1
  1.0 1.0 copy-start.2
  2.0 1.0 copy-start.3
  3.0 0.9 copy-start.4
  3.9 0.7 copy-start.5
  5.9 1.7 %copy-start = (bf16[384,3072]{1,0:T(8,128)(2,1)S(1)}, bf16[384,3072]{1,0:T(8,128)(2,1)}, u32[]{:S(2)}) copy-start(bf16[384,3072]{1,0:T(8,128)(2,1)} %w_ref.1) | copy-start | bytes 7077892

commit v7 on v5

--- a/solution.py
+++ b/solution.py
@@ -39,17 +39,15 @@
 
 
 def spread_kernel(
-    q_ref, kv_ref, w_ref, q_all, kv_all, w_all,
+    q_ref, kv_ref, q_all, kv_all,
     q_send, q_recv, z_send, z_recv, y_send, y_recv, far_send, far_recv,
-    core_send, core_recv, w_send, w_recv, w_core_send, w_core_recv, own_sem,
+    core_send, core_recv, own_sem,
 ):
     plane = lax.axis_index("heads")
     me = lax.axis_index("ctx")
     row, column, core = where_is(me)
     working = row < HEADS_HERE
     own_row = jnp.minimum(row, HEADS_HERE - 1)
-    depth = w_ref.shape[0]
-    width = w_all.shape[1]
     sides = (1, SIDE - 1)
 
     barrier = pltpu.get_barrier_semaphore()
@@ -61,11 +59,7 @@
         return carry
 
     lax.fori_loop(1, FRAMES, greet, 0)
-    for hop in range(1, PLANES):
-        pl.semaphore_signal(
-            barrier, inc=1, device_id=(lax.rem(plane + hop, PLANES), me), device_id_type=MESH
-        )
-    pl.semaphore_wait(barrier, FRAMES - 1 + PLANES - 1)
+    pl.semaphore_wait(barrier, FRAMES - 1)
 
     def span(part):
         return pl.ds(part * PART, PART)
@@ -128,42 +122,6 @@
             device_id_type=MESH,
         )
 
-    half = depth // 2
-
-    def w_rows(source, part):
-        return w_all.at[pl.ds(pl.multiple_of(source * depth + part * half, 16), half)]
-
-    def w_copy(hop):
-        there = lax.rem(plane + hop, PLANES)
-        return pltpu.make_async_remote_copy(
-            src_ref=w_ref.at[
-                pl.ds(pl.multiple_of(core * half, 16), half),
-                pl.ds(pl.multiple_of(there * width, 128), width),
-            ],
-            dst_ref=w_rows(plane, core),
-            send_sem=w_send.at[hop],
-            recv_sem=w_recv.at[hop],
-            device_id=(there, me),
-            device_id_type=MESH,
-        )
-
-    def w_core_copy(hop):
-        rows = w_rows(lax.rem(plane + PLANES - hop, PLANES), core)
-        return pltpu.make_async_remote_copy(
-            src_ref=rows,
-            dst_ref=rows,
-            send_sem=w_core_send.at[hop],
-            recv_sem=w_core_recv.at[hop],
-            device_id=(plane, device_at(row, column, 1 - core)),
-            device_id_type=MESH,
-        )
-
-    own_w = pltpu.make_async_copy(
-        w_ref.at[:, pl.ds(pl.multiple_of(plane * width, 128), width)],
-        w_all.at[pl.ds(pl.multiple_of(plane * depth, 128), depth)],
-        w_recv.at[0],
-    )
-
     def q_copy(step):
         there = lax.rem(me + step, FRAMES)
         row_there, column_there, core_there = where_is(there)
@@ -203,12 +161,6 @@
 
         return carry
 
-    def send_small():
-        for hop in range(1, PLANES):
-            w_copy(hop).start()
-        own_w.start()
-        lax.fori_loop(1, FRAMES, send_q, 0)
-
     @pl.when(working)
     def _():
         own_copy.start()
@@ -216,7 +168,7 @@
             y_copy(0, side).start()
 
     to_rows(0, lambda copy: copy.start())
-    send_small()
+    lax.fori_loop(1, FRAMES, send_q, 0)
 
     def next_rows(part):
         to_rows(part, lambda copy: copy.wait_send())
@@ -258,10 +210,6 @@
                 far_copy(number, side).wait_recv()
             core_copy(number, 2).start()
 
-    for hop in range(1, PLANES):
-        w_copy(hop).wait_recv()
-        w_core_copy(hop).start()
-
     @pl.when(working)
     def _():
         pltpu.make_async_copy(q_all, q_all, q_recv).wait()
@@ -274,24 +222,18 @@
             for away in range(SIDE):
                 core_copy(number, away).wait_send()
 
-    own_w.wait()
     lax.fori_loop(1, FRAMES, sent_q, 0)
-    for hop in range(1, PLANES):
-        w_copy(hop).wait_send()
-        w_core_copy(hop).wait()
-
-
-def spread(q_parts, kv_parts, out_weight):
-    depth, columns = out_weight.shape
+
+
+def spread(q_parts, kv_parts):
     return pl.pallas_call(
         spread_kernel,
         out_shape=(
             jax.ShapeDtypeStruct((SLOTS, FRAMES, SPOTS, DH), BF16),
             jax.ShapeDtypeStruct((WORKERS, 2 * TILES, SIDE, SPOTS, DH), BF16),
-            jax.ShapeDtypeStruct((depth * PLANES, columns // PLANES), BF16),
         ),
-        in_specs=[pl.BlockSpec(memory_space=pl.ANY)] * 3,
-        out_specs=(pl.BlockSpec(memory_space=pl.ANY),) * 3,
+        in_specs=[pl.BlockSpec(memory_space=pl.ANY)] * 2,
+        out_specs=(pl.BlockSpec(memory_space=pl.ANY),) * 2,
         scratch_shapes=[
             pltpu.SemaphoreType.DMA((FRAMES,)),
             pltpu.SemaphoreType.DMA,
@@ -303,16 +245,12 @@
             pltpu.SemaphoreType.DMA((PARTS + 1, 2)),
             pltpu.SemaphoreType.DMA((PARTS + 1, SIDE)),
             pltpu.SemaphoreType.DMA,
-            pltpu.SemaphoreType.DMA((PLANES,)),
-            pltpu.SemaphoreType.DMA((PLANES,)),
-            pltpu.SemaphoreType.DMA((PLANES,)),
-            pltpu.SemaphoreType.DMA((PLANES,)),
             pltpu.SemaphoreType.DMA,
         ],
         compiler_params=pltpu.CompilerParams(
             collective_id=0, has_side_effects=True, vmem_limit_bytes=4 * 1024 * 1024
         ),
-    )(q_parts, kv_parts, out_weight)
+    )(q_parts, kv_parts)
 
 
 def attend_kernel(
@@ -474,6 +412,11 @@
             pltpu.SMEM((most,), jnp.int32),
         ],
         compiler_params=pltpu.CompilerParams(vmem_limit_bytes=40 * 1024 * 1024),
+        cost_estimate=pl.CostEstimate(
+            flops=2 * 2 * SLOTS * TILE * TILES * TILE * DH,
+            bytes_accessed=2 * TILES * TILE * DH * 2,
+            transcendentals=SLOTS * TILE * TILES * TILE,
+        ),
     )(lists, query, kv)
 
 
@@ -589,31 +532,46 @@
     )(attended)
 
 
-def project_kernel(attn_ref, w_ref, out_ref):
-    rows = out_ref.shape[0]
-    heads = attn_ref.shape[0]
-    wide = jnp.concatenate([attn_ref[h, :rows, :] for h in range(heads)], axis=1)
-    out_ref[...] = jnp.dot(wide, w_ref[...], preferred_element_type=F32).astype(BF16)
-
-
-def project(attn, weight, rows):
-    columns = weight.shape[1]
+def project_kernel(attn_ref, *refs):
+    weights, out_ref = refs[:-1], refs[-1]
+    plane = lax.axis_index("heads")
+    wide, tall = [], []
+    for hop, weight in enumerate(weights):
+        source = lax.rem(plane + PLANES - hop, PLANES)
+        wide += [attn_ref[source * HEADS_HERE + h] for h in range(HEADS_HERE)]
+        tall.append(weight[...])
+    out_ref[...] = jnp.dot(
+        jnp.concatenate(wide, axis=1),
+        jnp.concatenate(tall, axis=0),
+        preferred_element_type=F32,
+    ).astype(BF16)
+
+
+def project(attn, weights, rows):
+    depth, columns = weights[0].shape
     block = 256
-    heads = attn.shape[0]
     return pl.pallas_call(
         project_kernel,
         out_shape=jax.ShapeDtypeStruct((rows, columns), BF16),
         grid=(columns // block,),
-        in_specs=[
-            pl.BlockSpec((heads, attn.shape[1], DH), lambda i: (0, 0, 0)),
-            pl.BlockSpec((weight.shape[0], block), lambda i: (0, i)),
-        ],
+        in_specs=[pl.BlockSpec(attn.shape, lambda i: (0, 0, 0))]
+        + [pl.BlockSpec((depth, block), lambda i: (0, i))] * len(weights),
         out_specs=pl.BlockSpec((rows, block), lambda i: (0, i)),
         compiler_params=pltpu.CompilerParams(vmem_limit_bytes=24 * 1024 * 1024),
-    )(attn, weight)
-
-
-def arrange_kernel(pattern_ref, mask_ref, q_ref, k_ref, v_ref, q_out, kv_out, list_ref):
+    )(attn, *weights)
+
+
+def arrange_kernel(pattern_ref, mask_ref, q_ref, k_ref, v_ref, w_ref, *refs):
+    w_out, (q_out, kv_out, list_ref, sems) = refs[:PLANES], refs[PLANES:]
+    plane = lax.axis_index("heads")
+    width = w_out[0].shape[1]
+    cuts = []
+    for hop in range(PLANES):
+        first = pl.multiple_of(lax.rem(plane + hop, PLANES) * width, 128)
+        cuts.append(
+            pltpu.make_async_copy(w_ref.at[:, pl.ds(first, width)], w_out[hop], sems.at[hop])
+        )
+        cuts[-1].start()
     me = lax.axis_index("ctx")
     row, column, core = where_is(me)
     rows = q_ref.shape[0]
@@ -648,38 +606,54 @@
         [rank[TILES - 1 :, :], jnp.zeros((1, TILES - SLOTS), jnp.int32)], axis=1
     )
     list_ref[SLOTS : SLOTS + 1, :] = last
-
-
-def arrange(head_pattern, tile_masks, queries, key_rows, value_rows):
+    for cut in cuts:
+        cut.wait()
+
+
+def arrange(head_pattern, tile_masks, queries, key_rows, value_rows, out_weight):
     rows = queries.shape[0]
+    depth, columns = out_weight.shape
     return pl.pallas_call(
         arrange_kernel,
         out_shape=(
+            *[jax.ShapeDtypeStruct((depth, columns // PLANES), BF16)] * PLANES,
             jax.ShapeDtypeStruct((HEADS_HERE, rows, DH), BF16),
             jax.ShapeDtypeStruct((HEADS_HERE, 2 * rows, DH), BF16),
             jax.ShapeDtypeStruct((SLOTS + 1, TILES), jnp.int32),
         ),
         in_specs=[pl.BlockSpec(memory_space=pltpu.SMEM)]
-        + [pl.BlockSpec(memory_space=pltpu.VMEM)] * 4,
-        out_specs=(pl.BlockSpec(memory_space=pltpu.VMEM),) * 3,
+        + [pl.BlockSpec(memory_space=pltpu.VMEM)] * 4
+        + [pl.BlockSpec(memory_space=pl.ANY)],
+        out_specs=(
+            *[pl.BlockSpec(memory_space=pl.ANY)] * PLANES,
+            *[pl.BlockSpec(memory_space=pltpu.VMEM)] * 3,
+        ),
+        scratch_shapes=[pltpu.SemaphoreType.DMA((PLANES,))],
         compiler_params=pltpu.CompilerParams(vmem_limit_bytes=16 * 1024 * 1024),
-    )(head_pattern, tile_masks, queries, key_rows, value_rows)
+    )(head_pattern, tile_masks, queries, key_rows, value_rows, out_weight)
 
 
 def body(queries, key_rows, value_rows, out_weight, tile_masks, head_pattern):
     rows = queries.shape[0]
-    q_parts, kv_parts, lists = arrange(head_pattern, tile_masks, queries, key_rows, value_rows)
-    q_all, kv_all, w_all = spread(
+    *weights, q_parts, kv_parts, lists = arrange(
+        head_pattern, tile_masks, queries, key_rows, value_rows, out_weight
+    )
+    q_all, kv_all = spread(
         q_parts.reshape(HEADS_HERE, SLOTS, WORKERS, SPOTS, DH),
         kv_parts.reshape(HEADS_HERE, 2 * TILES, SPOTS, DH),
-        out_weight,
     )
+    q_all, *weights = lax.optimization_barrier((q_all, *weights))
+    for hop in range(1, PLANES):
+        ring = [(plane, (plane + hop) % PLANES) for plane in range(PLANES)]
+        weights[hop] = lax.ppermute(weights[hop], "heads", ring)
     attended = attend(
-        lists, q_all.reshape(SLOTS * TILE, DH), kv_all.reshape(WORKERS, 2 * TILES * PIECE, DH)
+        lists,
+        q_all.reshape(SLOTS * TILE, DH),
+        kv_all.reshape(WORKERS, 2 * TILES * PIECE, DH),
     )
     attn = collect(attended.reshape(SLOTS, FRAMES, SPOTS, DH))
     attn = attn.reshape(PLANES * HEADS_HERE, rows, DH)
-    return project(attn, w_all, rows)
+    return project(attn, weights, rows)
 
 
 def solution(mesh):

time: 155 us -> 164 us (1.058)
  Pallas kernels: 148 us -> 153 us
  starting transfers between devices: 0 us -> 4.88 us
    ppermute x0 -> x3, starting transfers between devices: none -> 4.88 us  [body(): weights[hop] = lax.ppermute(weights[hop], 'heads', ring)]
    pallas_call x1, Pallas kernels: 27.2 us -> 30 us  [attend(): pl.pallas_call(attend_kernel, out_shape=jax.ShapeDtypeStruct(query.shape,...]
    pallas_call x1, Pallas kernels: 64.7 us -> 67.2 us  [collect(): pl.pallas_call(collect_kernel, out_shape=jax.ShapeDtypeStruct((PLANES * H...]
  transfers between devices with their start and end apart: 0 -> 3, of which waited for: 0 -> 0; matrix products, arithmetic and copies ran while one was open for 0% -> 0% of each run, Pallas kernels for 0% -> 59%
where the time goes in v7:
time: 164 us
  Pallas kernels  153 us (93%)
  local copies, waits for them, and re-layouts  6.21 us (4%)
  starting transfers between devices  4.88 us (3%)
    pallas_call x1, Pallas kernels, collect(): pl.pallas_call(collect_kernel, out_shape=jax.ShapeDtypeStruct((PLANES * H...  67.2 us
    pallas_call x1, Pallas kernels, spread(): pl.pallas_call(spread_kernel, out_shape=(jax.ShapeDtypeStruct((SLOTS, FRA...  51.1 us
    pallas_call x1, Pallas kernels, attend(): pl.pallas_call(attend_kernel, out_shape=jax.ShapeDtypeStruct(query.shape,...  30 us
    unnamed x12, local copies, waits for them, and re-layouts  6.21 us
    ppermute x3, starting transfers between devices, body(): weights[hop] = lax.ppermute(weights[hop], 'heads', ring)  4.88 us
  transfers between devices with their start and end apart: 3, of which 0 were waited for; matrix products, arithmetic and copies ran while one was open for 0% of the time, Pallas kernels for 59%

profile of v7, /device:TPU:1, one launch (start us, length us, event | category | flops | bytes accessed | tf_op | source)
XLA Modules:
  0.0 163.8 jit_solution(11168647626927360111)
XLA Ops:
  0.0 0.0 copy-start
  0.0 1.7 %copy-done = bf16[384,3072]{1,0:T(8,128)(2,1)S(1)} copy-done((bf16[384,3072]{1,0:T(8,128)(2,1)S(1)}, bf16[384,3072]{1,0:T(8,128)(2,1)}, u32[]{:S(2)}) %copy-start) | copy-done | bytes 2359320
  1.7 0.0 copy-start.1
  1.7 1.0 copy-done.1
  2.7 0.0 copy-start.2
  2.7 1.0 copy-done.2
  3.7 0.0 copy-start.3
  3.7 1.0 copy-done.3
  4.7 0.0 copy-start.4
  4.7 0.9 copy-done.4
  5.6 0.0 copy-start.5
  5.6 0.7 copy-done.5
  6.2 1.6 shard_map.64
  7.8 51.1 %shard_map.65 = (bf16[16,32,4,128]{3,2,1,0:T(4,128)(2,1)S(1)}, bf16[8,256,4,4,128]{4,3,2,1,0:T(4,128)(2,1)S(1)}) custom-call(bf16[3,16,8,4,128]{4,3,2,1,0:T(4,128)(2,1)S(1)} %bitcast.9, bf16[3,256,4,128]{3,2,1,0:T(4,128)(2,1)S(1)} %bitcast.7), custom_call_target="tpu_custom_call" | custom-call | tf_op jit(solution)/shard_map/pallas_call | solution.py:229
  58.9 1.3 collective-permute-start
  60.2 2.5 %collective-permute-start.1 = (bf16[384,768]{1,0:T(8,128)(2,1)S(1)}, bf16[384,768]{1,0:T(8,128)(2,1)S(1)}, u32[]{:S(2)}, u32[]{:S(2)}) collective-permute-start(bf16[384,768]{1,0:T(8,128)(2,1)S(1)} %get-tuple-element.31), channel_id=1, source_target_pairs={{0,64},{32,96},{64,0},{96,32},{1,65},{33,97},{65,1},{97,33},{2,66}... | collective-permute-start | bytes 1769480 | tf_op jit(solution)/shard_map/ppermute | solution.py:648
  62.7 1.1 collective-permute-start.2
  63.8 30.0 %shard_map.66 = bf16[2048,128]{1,0:T(8,128)(2,1)S(1)} custom-call(s32[17,128]{1,0:T(8,128)S(1)} %get-tuple-element.19.list_ref, bf16[2048,128]{1,0:T(8,128)(2,1)S(1)} %bitcast.11, bf16[8,4096,128]{2,1,0:T(8,128)(2,1)S(1)} %bitcast.10), custom_call_target="tpu_custom_call" | custom-call | flops 17179869184 | bytes 8388608 | tf_op jit(solution)/shard_map/pallas_call | solution.py:395
  93.8 67.2 %shard_map.67 = bf16[12,16,8,4,128]{4,3,2,1,0:T(4,128)(2,1)S(1)} custom-call(bf16[16,32,4,128]{3,2,1,0:T(4,128)(2,1)S(1)} %bitcast.8), custom_call_target="tpu_custom_call" | custom-call | tf_op jit(solution)/shard_map/pallas_call | solution.py:516
  161.0 0.0 collective-permute-done.refs_1_
  161.1 0.0 collective-permute-done.1.refs_2_
  161.1 0.0 collective-permute-done.2.refs_3_
  161.1 2.7 %shard_map.68 = bf16[512,768]{1,0:T(8,128)(2,1)} custom-call(bf16[12,512,128]{2,1,0:T(8,128)(2,1)S(1)} %bitcast.6, bf16[384,768]{1,0:T(8,128)(2,1)S(1)} %get-tuple-element.29.refs_0_, bf16[384,768]{1,0:T(8,128)(2,1)S(1)} %collective-permute-done.refs_1_, bf16[384,768]{1,0:T(8,128)(2,1)S(1)} %collective-permute-done.1.refs_2_, ...), custom_call_target="tpu_custom_call" | custom-call | tf_op jit(solution)/shard_map/pallas_call | solution.py:553
Async XLA Ops:
  0.0 1.7 %copy-start = (bf16[384,3072]{1,0:T(8,128)(2,1)S(1)}, bf16[384,3072]{1,0:T(8,128)(2,1)}, u32[]{:S(2)}) copy-start(bf16[384,3072]{1,0:T(8,128)(2,1)} %w_ref.1) | copy-start | bytes 7077892
  1.7 1.0 copy-start.1
  2.7 1.0 copy-start.2
  3.7 1.0 copy-start.3
  4.7 0.9 copy-start.4
  5.6 0.7 copy-start.5
  58.9 102.1 %collective-permute-start = (bf16[384,768]{1,0:T(8,128)(2,1)S(1)}, bf16[384,768]{1,0:T(8,128)(2,1)S(1)}, u32[]{:S(2)}, u32[]{:S(2)}) collective-permute-start(bf16[384,768]{1,0:T(8,128)(2,1)S(1)} %get-tuple-element.30), channel_id=1, source_target_pairs={{0,32},{32,64},{64,96},{96,0},{1,33},{33,65},{65,97},{97,1},{2,34}... | collective-permute-start | bytes 1769480 | tf_op jit(solution)/shard_map/ppermute | solution.py:648
  60.2 100.8 %collective-permute-start.1 = (bf16[384,768]{1,0:T(8,128)(2,1)S(1)}, bf16[384,768]{1,0:T(8,128)(2,1)S(1)}, u32[]{:S(2)}, u32[]{:S(2)}) collective-permute-start(bf16[384,768]{1,0:T(8,128)(2,1)S(1)} %get-tuple-element.31), channel_id=1, source_target_pairs={{0,64},{32,96},{64,0},{96,32},{1,65},{33,97},{65,1},{97,33},{2,66}... | collective-permute-start | bytes 1769480 | tf_op jit(solution)/shard_map/ppermute | solution.py:648
  62.7 98.4 %collective-permute-start.2 = (bf16[384,768]{1,0:T(8,128)(2,1)S(1)}, bf16[384,768]{1,0:T(8,128)(2,1)S(1)}, u32[]{:S(2)}, u32[]{:S(2)}) collective-permute-start(bf16[384,768]{1,0:T(8,128)(2,1)S(1)} %get-tuple-element.32), channel_id=1, source_target_pairs={{0,96},{32,0},{64,32},{96,64},{1,97},{33,1},{65,33},{97,65},{2,98}... | collective-permute-start | bytes 1769480 | tf_op jit(solution)/shard_map/ppermute | solution.py:648

commit v8 on v6

--- a/solution.py
+++ b/solution.py
@@ -20,7 +20,10 @@
 SLOTS = TILES // WORKERS
 PARTS = 4
 PART = 2 * TILES // PARTS
-DETOURS = 2
+PIECES = ((0, TILES, 0, 1), (TILES, TILES, 0, 1)) + tuple(
+    (part * PART, PART, 1, SIDE - 1) for part in range(PARTS)
+)
+ROUND = (1, 2)
 PIECE = TILE // WORKERS
 GROUP = 8
 BESIDE = 4
@@ -47,7 +50,7 @@
     q_ref, kv_ref, w_ref, q_all, kv_all, w_all,
     q_send, q_recv, z_send, z_recv, y_send, y_recv, far_send, far_recv,
     core_send, core_recv, w_send, w_recv, w_core_send, w_core_recv, own_sem,
-    held, passed, leg_send, leg_recv,
+    held_own, held_part, passed_own, passed_part, leg_send, leg_recv,
 ):
     plane = lax.axis_index("heads")
     me = lax.axis_index("ctx")
@@ -91,15 +94,18 @@
             device_id_type=MESH,
         )
 
+    def cut(source, number, share=None):
+        first, count, row_first, row_count = PIECES[number]
+        if share is not None:
+            first, count = first + share * (count // 2), count // 2
+        return source.at[pl.ds(first, count), pl.ds(row_first, row_count)]
+
     def piece(number, away):
-        source = kv_all.at[lax.rem(column + away, SIDE) * 2 + core]
-        if number == 0:
-            return source.at[:, 0]
-        return source.at[span(number - 1), pl.ds(1, SIDE - 1)]
+        return cut(kv_all.at[lax.rem(column + away, SIDE) * 2 + core], number)
 
     def y_copy(number, side):
         return pltpu.make_async_remote_copy(
-            src_ref=kv_ref.at[own_row] if number == 0 else piece(number, 0),
+            src_ref=piece(number, 0),
             dst_ref=piece(number, 0),
             send_sem=y_send.at[number, side],
             recv_sem=y_recv.at[number, side],
@@ -108,13 +114,7 @@
         )
 
     def far_copy(number, side):
-        source = kv_all.at[lax.rem(column + sides[1 - side], SIDE) * 2 + core]
-        if number == 0:
-            chunk = source.at[pl.ds(side * TILES, TILES), 0]
-        else:
-            chunk = source.at[
-                pl.ds((number - 1) * PART + side * (PART // 2), PART // 2), pl.ds(1, SIDE - 1)
-            ]
+        chunk = cut(kv_all.at[lax.rem(column + sides[1 - side], SIDE) * 2 + core], number, side)
         return pltpu.make_async_remote_copy(
             src_ref=chunk,
             dst_ref=chunk,
@@ -124,6 +124,8 @@
             device_id_type=MESH,
         )
 
+    held, passed = (held_own, held_part), (passed_own, passed_part)
+
     other_row, other_column, _ = where_is(me, plane + 1)
     relaying = other_row < HEADS_HERE
 
@@ -133,9 +135,9 @@
     def first_leg(number, side):
         return pltpu.make_async_remote_copy(
             src_ref=piece(number, 0),
-            dst_ref=held.at[number - 1, side],
-            send_sem=leg_send.at[0, number - 1, side],
-            recv_sem=leg_recv.at[0, number - 1, side],
+            dst_ref=held[ROUND.index(number)].at[side],
+            send_sem=leg_send.at[0, number, side],
+            recv_sem=leg_recv.at[0, number, side],
             device_id=(next_plane(side), me),
             device_id_type=MESH,
         )
@@ -143,20 +145,20 @@
     def second_leg(number, side):
         there = device_at(other_row, other_column + sides[side], core, plane + 1)
         return pltpu.make_async_remote_copy(
-            src_ref=held.at[number - 1, side],
-            dst_ref=passed.at[number - 1, side],
-            send_sem=leg_send.at[1, number - 1, side],
-            recv_sem=leg_recv.at[1, number - 1, side],
+            src_ref=held[ROUND.index(number)].at[side],
+            dst_ref=passed[ROUND.index(number)].at[side],
+            send_sem=leg_send.at[1, number, side],
+            recv_sem=leg_recv.at[1, number, side],
             device_id=(plane, there),
             device_id_type=MESH,
         )
 
     def third_leg(number, side):
-        source = lax.rem(other_column + sides[1 - side], SIDE) * 2 + core
-        return pltpu.make_async_remote_copy(
-            src_ref=passed.at[number - 1, side],
-            dst_ref=kv_all.at[source, span(number - 1), pl.ds(1, SIDE - 1)],
-            send_sem=leg_send.at[2, number - 1, side],
+        source = kv_all.at[lax.rem(other_column + sides[1 - side], SIDE) * 2 + core]
+        return pltpu.make_async_remote_copy(
+            src_ref=passed[ROUND.index(number)].at[side],
+            dst_ref=cut(source, number),
+            send_sem=leg_send.at[2, number, side],
             recv_sem=y_recv.at[number, side],
             device_id=(next_plane(1 - side), me),
             device_id_type=MESH,
@@ -258,33 +260,37 @@
 
         return carry
 
-    def send_small():
+    def send_weights():
         for hop in range(1, PLANES):
             w_copy(hop).start()
         own_w.start()
-        lax.fori_loop(1, FRAMES, send_q, 0)
+
+    def send_on(number):
+        for side in range(2):
+            if number in ROUND:
+                first_leg(number, side).start()
+            else:
+                y_copy(number, side).start()
+        core_copy(number, 0).start()
+
+    to_rows(0, lambda copy: copy.start())
 
     @pl.when(working)
     def _():
         own_copy.start()
-        for side in range(2):
-            y_copy(0, side).start()
-
-    to_rows(0, lambda copy: copy.start())
-    send_small()
+        own_copy.wait()
+        send_on(0)
+        send_on(1)
+        pltpu.make_async_copy(
+            q_ref.at[own_row, :, column * 2 + core], q_all.at[:, me], q_recv
+        ).start()
+
+    lax.fori_loop(1, FRAMES, send_q, 0)
 
     def next_rows(part):
         to_rows(part, lambda copy: copy.wait_send())
         if part + 1 < PARTS:
             to_rows(part + 1, lambda copy: copy.start())
-
-    @pl.when(working)
-    def _():
-        pltpu.make_async_copy(
-            q_ref.at[own_row, :, column * 2 + core], q_all.at[:, me], q_recv
-        ).start()
-        own_copy.wait()
-        core_copy(0, 0).start()
 
     def gathered(part):
         next_rows(part)
@@ -294,12 +300,7 @@
             for hop in range(1, SIDE):
                 landed = kv_all.at[column * 2 + core, span(part), hop]
                 pltpu.make_async_copy(landed, landed, z_recv.at[part, hop]).wait()
-            for side in range(2):
-                if part < DETOURS:
-                    first_leg(part + 1, side).start()
-                else:
-                    y_copy(part + 1, side).start()
-            core_copy(part + 1, 0).start()
+            send_on(part + 2)
 
     def pass_on(number):
         @pl.when(working)
@@ -311,22 +312,24 @@
                 core_copy(number, sides[1 - side]).start()
 
     gathered(0)
-    gathered(1)
     pass_on(0)
     relay(1, 1)
+    gathered(1)
+    relay(1, 2)
+    send_weights()
     gathered(2)
-    relay(1, 2)
-    gathered(3)
     relay(2, 1)
     pass_on(3)
+    gathered(3)
     relay(2, 2)
     pass_on(1)
     pass_on(4)
     pass_on(2)
+    pass_on(5)
 
     @pl.when(working)
     def _():
-        for number in (0, 3, 1, 4, 2):
+        for number in (0, 3, 1, 4, 2, 5):
             for side in range(2):
                 far_copy(number, side).wait_recv()
             core_copy(number, 2).start()
@@ -340,9 +343,9 @@
         pltpu.make_async_copy(q_all, q_all, q_recv).wait()
         other = kv_all.at[pl.ds(0, SIDE)]
         pltpu.make_async_copy(other, other, core_recv).wait()
-        for number in range(PARTS + 1):
+        for number in range(len(PIECES)):
             for side in range(2):
-                if 0 < number <= DETOURS:
+                if number in ROUND:
                     first_leg(number, side).wait_send()
                 else:
                     y_copy(number, side).wait_send()
@@ -352,7 +355,7 @@
 
     @pl.when(relaying)
     def _():
-        for number in range(1, DETOURS + 1):
+        for number in ROUND:
             for side in range(2):
                 second_leg(number, side).wait_send()
                 third_leg(number, side).wait_send()
@@ -380,21 +383,23 @@
             pltpu.SemaphoreType.DMA,
             pltpu.SemaphoreType.DMA((PARTS, SIDE)),
             pltpu.SemaphoreType.DMA((PARTS, SIDE)),
-            pltpu.SemaphoreType.DMA((PARTS + 1, 2)),
-            pltpu.SemaphoreType.DMA((PARTS + 1, 2)),
-            pltpu.SemaphoreType.DMA((PARTS + 1, 2)),
-            pltpu.SemaphoreType.DMA((PARTS + 1, 2)),
-            pltpu.SemaphoreType.DMA((PARTS + 1, SIDE)),
+            pltpu.SemaphoreType.DMA((len(PIECES), 2)),
+            pltpu.SemaphoreType.DMA((len(PIECES), 2)),
+            pltpu.SemaphoreType.DMA((len(PIECES), 2)),
+            pltpu.SemaphoreType.DMA((len(PIECES), 2)),
+            pltpu.SemaphoreType.DMA((len(PIECES), SIDE)),
             pltpu.SemaphoreType.DMA,
             pltpu.SemaphoreType.DMA((PLANES,)),
             pltpu.SemaphoreType.DMA((PLANES,)),
             pltpu.SemaphoreType.DMA((PLANES,)),
             pltpu.SemaphoreType.DMA((PLANES,)),
             pltpu.SemaphoreType.DMA,
-            pltpu.VMEM((DETOURS, 2, PART, SIDE - 1, SPOTS, DH), BF16),
-            pltpu.VMEM((DETOURS, 2, PART, SIDE - 1, SPOTS, DH), BF16),
-            pltpu.SemaphoreType.DMA((3, DETOURS, 2)),
-            pltpu.SemaphoreType.DMA((2, DETOURS, 2)),
+            *[
+                pltpu.VMEM((2, PIECES[number][1], PIECES[number][3], SPOTS, DH), BF16)
+                for number in ROUND + ROUND
+            ],
+            pltpu.SemaphoreType.DMA((3, len(PIECES), 2)),
+            pltpu.SemaphoreType.DMA((2, len(PIECES), 2)),
         ],
         compiler_params=pltpu.CompilerParams(
             collective_id=0, has_side_effects=True, vmem_limit_bytes=12 * 1024 * 1024

time: 164 us -> 162 us (0.988)
  Pallas kernels: 157 us -> 155 us
    pallas_call x1, Pallas kernels: 67.4 us -> 63.5 us  [collect(): pl.pallas_call(collect_kernel, out_shape=jax.ShapeDtypeStruct((PLANES * H...]
    pallas_call x1, Pallas kernels: 54.4 us -> 58 us  [spread(): pl.pallas_call(spread_kernel, out_shape=(jax.ShapeDtypeStruct((SLOTS, FRA...]
where the time goes in v8:
time: 162 us
  Pallas kernels  155 us (96%)
  local copies, waits for them, and re-layouts  6.2 us (4%)
    pallas_call x1, Pallas kernels, collect(): pl.pallas_call(collect_kernel, out_shape=jax.ShapeDtypeStruct((PLANES * H...  63.5 us
    pallas_call x1, Pallas kernels, spread(): pl.pallas_call(spread_kernel, out_shape=(jax.ShapeDtypeStruct((SLOTS, FRA...  58 us
    pallas_call x1, Pallas kernels, attend(): pl.pallas_call(attend_kernel, out_shape=jax.ShapeDtypeStruct(query.shape,...  29.9 us
    unnamed x12, local copies, waits for them, and re-layouts  6.2 us

profile of v8, /device:TPU:1, one launch (start us, length us, event | category | flops | bytes accessed | tf_op | source)
XLA Modules:
  0.0 161.7 jit_solution(2802748966939114312)
XLA Ops:
  0.0 0.0 copy-start.1
  0.0 1.0 copy-done.1
  1.0 0.0 copy-start.2
  1.0 1.0 copy-done.2
  2.0 0.0 copy-start.3
  2.0 1.0 copy-done.3
  3.0 0.0 copy-start.4
  3.0 0.9 copy-done.4
  3.9 0.0 copy-start.5
  3.9 0.7 copy-done.5
  4.5 1.3 shard_map.64
  5.9 0.0 copy-start
  5.9 1.7 %copy-done = bf16[384,3072]{1,0:T(8,128)(2,1)S(1)} copy-done((bf16[384,3072]{1,0:T(8,128)(2,1)S(1)}, bf16[384,3072]{1,0:T(8,128)(2,1)}, u32[]{:S(2)}) %copy-start) | copy-done | bytes 2359320
  7.5 58.0 %shard_map.65 = (bf16[16,32,4,128]{3,2,1,0:T(4,128)(2,1)S(1)}, bf16[8,256,4,4,128]{4,3,2,1,0:T(4,128)(2,1)S(1)}, bf16[1536,768]{1,0:T(8,128)(2,1)S(1)}) custom-call(bf16[3,16,8,4,128]{4,3,2,1,0:T(4,128)(2,1)S(1)} %bitcast.11, bf16[3,256,4,128]{3,2,1,0:T(4,128)(2,1)S(1)} %bitcast.9, bf16[384,3072]{1,0:T(8,128)(2,1)S(1)} %copy-done), custom_call_target="tpu_custom_call" | custom-call | tf_op jit(solution)/shard_map/pallas_call | solution.py:372
  65.5 29.9 %shard_map.66 = bf16[2048,128]{1,0:T(8,128)(2,1)S(1)} custom-call(s32[17,128]{1,0:T(8,128)S(1)} %get-tuple-element.11.list_ref, bf16[2048,128]{1,0:T(8,128)(2,1)S(1)} %bitcast.10, bf16[8,4096,128]{2,1,0:T(8,128)(2,1)S(1)} %bitcast.6), custom_call_target="tpu_custom_call" | custom-call | tf_op jit(solution)/shard_map/pallas_call | solution.py:549
  95.4 63.5 %shard_map.67 = bf16[12,16,8,4,128]{4,3,2,1,0:T(4,128)(2,1)S(1)} custom-call(bf16[16,32,4,128]{3,2,1,0:T(4,128)(2,1)S(1)} %bitcast.8), custom_call_target="tpu_custom_call" | custom-call | tf_op jit(solution)/shard_map/pallas_call | solution.py:665
  159.0 2.7 %shard_map.68 = bf16[512,768]{1,0:T(8,128)(2,1)} custom-call(bf16[12,512,128]{2,1,0:T(8,128)(2,1)S(1)} %bitcast.7, bf16[1536,768]{1,0:T(8,128)(2,1)S(1)} %get-tuple-element.16.w_ref), custom_call_target="tpu_custom_call" | custom-call | tf_op jit(solution)/shard_map/pallas_call | solution.py:695
Async XLA Ops:
  0.0 1.0 copy-start.1
  1.0 1.0 copy-start.2
  2.0 1.0 copy-start.3
  3.0 0.9 copy-start.4
  3.9 0.7 copy-start.5
  5.9 1.7 %copy-start = (bf16[384,3072]{1,0:T(8,128)(2,1)S(1)}, bf16[384,3072]{1,0:T(8,128)(2,1)}, u32[]{:S(2)}) copy-start(bf16[384,3072]{1,0:T(8,128)(2,1)} %w_ref.1) | copy-start | bytes 7077892

commit v9 on v5

--- a/solution.py
+++ b/solution.py
@@ -22,6 +22,7 @@
 PART = 2 * TILES // PARTS
 PIECE = TILE // WORKERS
 GROUP = 8
+CHUNK = 32
 BESIDE = 4
 FAR = 2.0**64
 LOW = -1e30
@@ -310,15 +311,25 @@
             pltpu.SemaphoreType.DMA,
         ],
         compiler_params=pltpu.CompilerParams(
-            collective_id=0, has_side_effects=True, vmem_limit_bytes=4 * 1024 * 1024
+            collective_id=0, has_side_effects=True, vmem_limit_bytes=57 * 1024 * 1024
         ),
     )(q_parts, kv_parts, out_weight)
 
 
 def attend_kernel(
-    list_ref, q_ref, kv_ref, o_ref, keys_ref, values_ref, base_ref, peak_ref, sum_ref,
-    slot_of, first_of, listed_of,
+    list_ref, q_ref, kv_hbm, o_ref, kv_ref, keys_ref, values_ref, base_ref, peak_ref, sum_ref,
+    slot_of, first_of, listed_of, kv_sem,
 ):
+    def chunk(number, first):
+        rows = pl.ds((first + number * CHUNK) * PIECE, CHUNK * PIECE)
+        return pltpu.make_async_copy(
+            kv_hbm.at[:, rows], kv_ref.at[:, rows], kv_sem.at[number, min(first, 1)]
+        )
+
+    for number in range(TILES // CHUNK):
+        chunk(number, 0).start()
+        chunk(number, TILES).start()
+
     _, column, core = where_is(lax.axis_index("ctx"))
 
     def loop(count, work):
@@ -366,7 +377,11 @@
             keys_ref[tile] = tile_at(tile).T
             values_ref[tile] = tile_at(TILES + tile)
 
-    loop(busy * (TILES // GROUP), unpack)
+    for number in range(TILES // CHUNK):
+        chunk(number, 0).wait()
+        chunk(number, TILES).wait()
+        steps = CHUNK // GROUP
+        loop(busy * steps, lambda step: unpack(step + number * steps))
 
     def set_base(slot, base):
         base_ref[slot] = jnp.broadcast_to(base * SCALE2, (TILE, TILE))
@@ -460,10 +475,11 @@
         in_specs=[
             pl.BlockSpec(memory_space=pltpu.SMEM),
             pl.BlockSpec(memory_space=pltpu.VMEM),
-            pl.BlockSpec(memory_space=pltpu.VMEM),
+            pl.BlockSpec(memory_space=pl.ANY),
         ],
         out_specs=pl.BlockSpec(memory_space=pltpu.VMEM),
         scratch_shapes=[
+            pltpu.VMEM(kv.shape, BF16),
             pltpu.VMEM((TILES, DH, TILE), BF16),
             pltpu.VMEM((TILES + 1, TILE, DH), BF16),
             pltpu.VMEM((SLOTS, TILE, TILE), F32),
@@ -472,8 +488,9 @@
             pltpu.SMEM((most,), jnp.int32),
             pltpu.SMEM((most,), jnp.int32),
             pltpu.SMEM((most,), jnp.int32),
+            pltpu.SemaphoreType.DMA((TILES // CHUNK, 2)),
         ],
-        compiler_params=pltpu.CompilerParams(vmem_limit_bytes=40 * 1024 * 1024),
+        compiler_params=pltpu.CompilerParams(vmem_limit_bytes=57 * 1024 * 1024),
     )(lists, query, kv)
 
 
@@ -590,39 +607,41 @@
 
 
 def project_kernel(attn_ref, w_ref, out_ref):
-    rows = out_ref.shape[0]
     heads = attn_ref.shape[0]
-    wide = jnp.concatenate([attn_ref[h, :rows, :] for h in range(heads)], axis=1)
-    out_ref[...] = jnp.dot(wide, w_ref[...], preferred_element_type=F32).astype(BF16)
+    wide = jnp.concatenate([attn_ref[h] for h in range(heads)], axis=1)
+    block = 256
+    for first in range(0, out_ref.shape[1], block):
+        columns = slice(first, first + block)
+        out_ref[:, columns] = jnp.dot(
+            wide, w_ref[:, columns], preferred_element_type=F32
+        ).astype(BF16)
 
 
 def project(attn, weight, rows):
-    columns = weight.shape[1]
-    block = 256
-    heads = attn.shape[0]
     return pl.pallas_call(
         project_kernel,
-        out_shape=jax.ShapeDtypeStruct((rows, columns), BF16),
-        grid=(columns // block,),
-        in_specs=[
-            pl.BlockSpec((heads, attn.shape[1], DH), lambda i: (0, 0, 0)),
-            pl.BlockSpec((weight.shape[0], block), lambda i: (0, i)),
-        ],
-        out_specs=pl.BlockSpec((rows, block), lambda i: (0, i)),
+        out_shape=jax.ShapeDtypeStruct((rows, weight.shape[1]), BF16),
+        in_specs=[pl.BlockSpec(memory_space=pltpu.VMEM)] * 2,
+        out_specs=pl.BlockSpec(memory_space=pltpu.VMEM),
         compiler_params=pltpu.CompilerParams(vmem_limit_bytes=24 * 1024 * 1024),
     )(attn, weight)
 
 
-def arrange_kernel(pattern_ref, mask_ref, q_ref, k_ref, v_ref, q_out, kv_out, list_ref):
+def arrange_kernel(
+    pattern_ref, mask_hbm, q_hbm, k_hbm, v_hbm, q_out, kv_out, list_ref,
+    mask_ref, q_ref, k_ref, v_ref, sems,
+):
+    sources = (mask_hbm, q_hbm, k_hbm, v_hbm)
+    targets = (mask_ref, q_ref, k_ref, v_ref)
+    moves = [
+        pltpu.make_async_copy(source, target, sems.at[i])
+        for i, (source, target) in enumerate(zip(sources, targets))
+    ]
+    for move in moves:
+        move.start()
     me = lax.axis_index("ctx")
     row, column, core = where_is(me)
-    rows = q_ref.shape[0]
-    for head in range(HEADS_HERE):
-        columns = slice(head * DH, (head + 1) * DH)
-        q_out[head] = q_ref[:, columns]
-        kv_out[head, :rows, :] = k_ref[:, columns]
-        kv_out[head, rows:, :] = v_ref[:, columns]
-
+    moves[0].wait()
     pattern = pattern_ref[jnp.minimum(row, HEADS_HERE - 1)]
     masks = []
     tiles = [slot * WORKERS + column * 2 + core for slot in range(SLOTS)]
@@ -650,6 +669,17 @@
     list_ref[SLOTS : SLOTS + 1, :] = last
 
 
+    rows = q_ref.shape[0]
+    for move, source, target, first in (
+        (moves[1], q_ref, q_out, 0),
+        (moves[2], k_ref, kv_out, 0),
+        (moves[3], v_ref, kv_out, rows),
+    ):
+        move.wait()
+        for head in range(HEADS_HERE):
+            target[head, first : first + rows, :] = source[:, head * DH : (head + 1) * DH]
+
+
 def arrange(head_pattern, tile_masks, queries, key_rows, value_rows):
     rows = queries.shape[0]
     return pl.pallas_call(
@@ -660,9 +690,16 @@
             jax.ShapeDtypeStruct((SLOTS + 1, TILES), jnp.int32),
         ),
         in_specs=[pl.BlockSpec(memory_space=pltpu.SMEM)]
-        + [pl.BlockSpec(memory_space=pltpu.VMEM)] * 4,
+        + [pl.BlockSpec(memory_space=pl.ANY)] * 4,
         out_specs=(pl.BlockSpec(memory_space=pltpu.VMEM),) * 3,
-        compiler_params=pltpu.CompilerParams(vmem_limit_bytes=16 * 1024 * 1024),
+        scratch_shapes=[
+            pltpu.VMEM(tile_masks.shape, jnp.int32),
+            pltpu.VMEM(queries.shape, BF16),
+            pltpu.VMEM(queries.shape, BF16),
+            pltpu.VMEM(queries.shape, BF16),
+            pltpu.SemaphoreType.DMA((4,)),
+        ],
+        compiler_params=pltpu.CompilerParams(vmem_limit_bytes=57 * 1024 * 1024),
     )(head_pattern, tile_masks, queries, key_rows, value_rows)
 
 

time: 155 us -> 157 us (1.013)
  Pallas kernels: 148 us -> 156 us
  local copies, waits for them, and re-layouts: 6.2 us -> 1.04 us
    pallas_call x1, Pallas kernels: 27.2 us -> 32.6 us  [attend(): pl.pallas_call(attend_kernel, out_shape=jax.ShapeDtypeStruct(query.shape,...]
    unnamed x12 -> x4, local copies, waits for them, and re-layouts: 6.2 us -> 1.04 us
    pallas_call x1, Pallas kernels: 1.3 us -> 3.32 us  [arrange(): pl.pallas_call(arrange_kernel, out_shape=(jax.ShapeDtypeStruct((HEADS_HER...]
where the time goes in v9:
time: 157 us
  Pallas kernels  156 us (99%)
    pallas_call x1, Pallas kernels, collect(): pl.pallas_call(collect_kernel, out_shape=jax.ShapeDtypeStruct((PLANES * H...  64.9 us
    pallas_call x1, Pallas kernels, spread(): pl.pallas_call(spread_kernel, out_shape=(jax.ShapeDtypeStruct((SLOTS, FRA...  52.6 us
    pallas_call x1, Pallas kernels, attend(): pl.pallas_call(attend_kernel, out_shape=jax.ShapeDtypeStruct(query.shape,...  32.6 us
    pallas_call x1, Pallas kernels, arrange(): pl.pallas_call(arrange_kernel, out_shape=(jax.ShapeDtypeStruct((HEADS_HER...  3.32 us

profile of v9, /device:TPU:1, one launch (start us, length us, event | category | flops | bytes accessed | tf_op | source)
XLA Modules:
  0.0 156.8 jit_solution(10904945690006467119)
XLA Ops:
  0.0 3.3 %shard_map.64 = (bf16[3,512,128]{2,1,0:T(8,128)(2,1)}, bf16[3,1024,128]{2,1,0:T(8,128)(2,1)}, s32[17,128]{1,0:T(8,128)}) custom-call(s32[3]{0:T(128)} %pattern_ref.1, s32[2,128,128]{2,1,0:T(8,128)} %mask_hbm.1, bf16[512,384]{1,0:T(8,128)(2,1)} %q_hbm.1, bf16[512,384]{1,0:T(8,128)(2,1)} %k_hbm.1, bf16[512,384]{1,0:T(8,128)(2,1)} %v_hbm.1), custom_call_target="tpu_custom_call" | custom-call | tf_op jit(solution)/shard_map/pallas_call | solution.py:685
  3.3 52.6 %shard_map.65 = (bf16[16,32,4,128]{3,2,1,0:T(4,128)(2,1)}, bf16[8,256,4,4,128]{4,3,2,1,0:T(4,128)(2,1)}, bf16[1536,768]{1,0:T(8,128)(2,1)}) custom-call(bf16[3,16,8,4,128]{4,3,2,1,0:T(4,128)(2,1)} %bitcast.11, bf16[3,256,4,128]{3,2,1,0:T(4,128)(2,1)} %bitcast.9, bf16[384,3072]{1,0:T(8,128)(2,1)} %w_ref.1), custom_call_target="tpu_custom_call" | custom-call | tf_op jit(solution)/shard_map/pallas_call | solution.py:287
  55.9 0.0 copy-start
  55.9 32.6 %shard_map.66 = bf16[2048,128]{1,0:T(8,128)(2,1)} custom-call(s32[17,128]{1,0:T(8,128)} %get-tuple-element.11.list_ref, bf16[2048,128]{1,0:T(8,128)(2,1)} %bitcast.10, bf16[8,4096,128]{2,1,0:T(8,128)(2,1)} %bitcast.8), custom_call_target="tpu_custom_call" | custom-call | tf_op jit(solution)/shard_map/pallas_call | solution.py:472
  88.5 0.0 copy-start.1
  88.5 1.0 copy-done.1
  89.6 64.9 %shard_map.67 = bf16[12,16,8,4,128]{4,3,2,1,0:T(4,128)(2,1)S(1)} custom-call(bf16[16,32,4,128]{3,2,1,0:T(4,128)(2,1)S(1)} %bitcast.7), custom_call_target="tpu_custom_call" | custom-call | tf_op jit(solution)/shard_map/pallas_call | solution.py:590
  154.5 0.0 copy-done
  154.5 2.3 %shard_map.68 = bf16[512,768]{1,0:T(8,128)(2,1)} custom-call(bf16[12,512,128]{2,1,0:T(8,128)(2,1)S(1)} %bitcast.6, bf16[1536,768]{1,0:T(8,128)(2,1)S(1)} %copy-done), custom_call_target="tpu_custom_call" | custom-call | tf_op jit(solution)/shard_map/pallas_call | solution.py:621
Async XLA Ops:
  55.9 98.6 %copy-start = (bf16[1536,768]{1,0:T(8,128)(2,1)S(1)}, bf16[1536,768]{1,0:T(8,128)(2,1)}, u32[]{:S(2)}) copy-start(bf16[1536,768]{1,0:T(8,128)(2,1)} %get-tuple-element.16.w_ref) | copy-start | bytes 7077892
  88.5 1.0 copy-start.1

commit v10 on v9

--- a/solution.py
+++ b/solution.py
@@ -21,9 +21,10 @@
 PARTS = 4
 PART = 2 * TILES // PARTS
 PIECE = TILE // WORKERS
-GROUP = 8
-CHUNK = 32
-BESIDE = 4
+GROUP = 4
+CHUNK = 16
+UNPACK = 8
+BESIDE = 8
 FAR = 2.0**64
 LOW = -1e30
 SCALE2 = math.log2(math.e) / math.sqrt(DH)
@@ -326,9 +327,13 @@
             kv_hbm.at[:, rows], kv_ref.at[:, rows], kv_sem.at[number, min(first, 1)]
         )
 
-    for number in range(TILES // CHUNK):
-        chunk(number, 0).start()
-        chunk(number, TILES).start()
+    def bring(number):
+        if number < TILES // CHUNK:
+            chunk(number, 0).start()
+            chunk(number, TILES).start()
+
+    bring(0)
+    bring(1)
 
     _, column, core = where_is(lax.axis_index("ctx"))
 
@@ -372,15 +377,16 @@
     values_ref[TILES] = jnp.zeros((TILE, DH), BF16)
 
     def unpack(step):
-        for u in range(GROUP):
-            tile = step * GROUP + u
+        for u in range(UNPACK):
+            tile = step * UNPACK + u
             keys_ref[tile] = tile_at(tile).T
             values_ref[tile] = tile_at(TILES + tile)
 
     for number in range(TILES // CHUNK):
         chunk(number, 0).wait()
         chunk(number, TILES).wait()
-        steps = CHUNK // GROUP
+        bring(number + 2)
+        steps = CHUNK // UNPACK
         loop(busy * steps, lambda step: unpack(step + number * steps))
 
     def set_base(slot, base):

time: 157 us -> 161 us (1.025)
  Pallas kernels: 156 us -> 159 us
    pallas_call x1, Pallas kernels: 64.9 us -> 67.3 us  [collect(): pl.pallas_call(collect_kernel, out_shape=jax.ShapeDtypeStruct((PLANES * H...]
where the time goes in v10:
time: 161 us
  Pallas kernels  159 us (99%)
    pallas_call x1, Pallas kernels, collect(): pl.pallas_call(collect_kernel, out_shape=jax.ShapeDtypeStruct((PLANES * H...  67.3 us
    pallas_call x1, Pallas kernels, spread(): pl.pallas_call(spread_kernel, out_shape=(jax.ShapeDtypeStruct((SLOTS, FRA...  52.6 us
    pallas_call x1, Pallas kernels, attend(): pl.pallas_call(attend_kernel, out_shape=jax.ShapeDtypeStruct(query.shape,...  34 us
    pallas_call x1, Pallas kernels, arrange(): pl.pallas_call(arrange_kernel, out_shape=(jax.ShapeDtypeStruct((HEADS_HER...  3.32 us

profile of v10, /device:TPU:1, one launch (start us, length us, event | category | flops | bytes accessed | tf_op | source)
XLA Modules:
  0.0 160.6 jit_solution(17549327799125430637)
XLA Ops:
  0.0 3.3 %shard_map.64 = (bf16[3,512,128]{2,1,0:T(8,128)(2,1)}, bf16[3,1024,128]{2,1,0:T(8,128)(2,1)}, s32[17,128]{1,0:T(8,128)}) custom-call(s32[3]{0:T(128)} %pattern_ref.1, s32[2,128,128]{2,1,0:T(8,128)} %mask_hbm.1, bf16[512,384]{1,0:T(8,128)(2,1)} %q_hbm.1, bf16[512,384]{1,0:T(8,128)(2,1)} %k_hbm.1, bf16[512,384]{1,0:T(8,128)(2,1)} %v_hbm.1), custom_call_target="tpu_custom_call" | custom-call | tf_op jit(solution)/shard_map/pallas_call | solution.py:691
  3.3 52.6 %shard_map.65 = (bf16[16,32,4,128]{3,2,1,0:T(4,128)(2,1)}, bf16[8,256,4,4,128]{4,3,2,1,0:T(4,128)(2,1)}, bf16[1536,768]{1,0:T(8,128)(2,1)}) custom-call(bf16[3,16,8,4,128]{4,3,2,1,0:T(4,128)(2,1)} %bitcast.11, bf16[3,256,4,128]{3,2,1,0:T(4,128)(2,1)} %bitcast.9, bf16[384,3072]{1,0:T(8,128)(2,1)} %w_ref.1), custom_call_target="tpu_custom_call" | custom-call | tf_op jit(solution)/shard_map/pallas_call | solution.py:288
  55.9 0.0 copy-start
  55.9 34.0 %shard_map.66 = bf16[2048,128]{1,0:T(8,128)(2,1)} custom-call(s32[17,128]{1,0:T(8,128)} %get-tuple-element.11.list_ref, bf16[2048,128]{1,0:T(8,128)(2,1)} %bitcast.10, bf16[8,4096,128]{2,1,0:T(8,128)(2,1)} %bitcast.8), custom_call_target="tpu_custom_call" | custom-call | tf_op jit(solution)/shard_map/pallas_call | solution.py:478
  89.9 0.0 copy-start.1
  90.0 1.0 copy-done.1
  91.0 67.3 %shard_map.67 = bf16[12,16,8,4,128]{4,3,2,1,0:T(4,128)(2,1)S(1)} custom-call(bf16[16,32,4,128]{3,2,1,0:T(4,128)(2,1)S(1)} %bitcast.7), custom_call_target="tpu_custom_call" | custom-call | tf_op jit(solution)/shard_map/pallas_call | solution.py:596
  158.3 0.0 copy-done
  158.3 2.3 %shard_map.68 = bf16[512,768]{1,0:T(8,128)(2,1)} custom-call(bf16[12,512,128]{2,1,0:T(8,128)(2,1)S(1)} %bitcast.6, bf16[1536,768]{1,0:T(8,128)(2,1)S(1)} %copy-done), custom_call_target="tpu_custom_call" | custom-call | tf_op jit(solution)/shard_map/pallas_call | solution.py:627
Async XLA Ops:
  55.9 102.4 %copy-start = (bf16[1536,768]{1,0:T(8,128)(2,1)S(1)}, bf16[1536,768]{1,0:T(8,128)(2,1)}, u32[]{:S(2)}) copy-start(bf16[1536,768]{1,0:T(8,128)(2,1)} %get-tuple-element.16.w_ref) | copy-start | bytes 7077892
  89.9 1.0 copy-start.1

commit v11 on v9

--- a/solution.py
+++ b/solution.py
@@ -40,7 +40,7 @@
 
 
 def spread_kernel(
-    q_ref, kv_ref, w_ref, q_all, kv_all, w_all,
+    q_ref, kv_ref, w_ref, kv_all, w_all,
     q_send, q_recv, z_send, z_recv, y_send, y_recv, far_send, far_recv,
     core_send, core_recv, w_send, w_recv, w_core_send, w_core_recv, own_sem,
 ):
@@ -72,7 +72,7 @@
         return pl.ds(part * PART, PART)
 
     own_copy = pltpu.make_async_copy(
-        kv_ref.at[own_row], kv_all.at[column * 2 + core, :, 0], own_sem
+        kv_ref.at[own_row], kv_all.at[column * 2 + core, pl.ds(0, 2 * TILES), 0], own_sem
     )
 
     def z_copy(part, hop):
@@ -89,7 +89,7 @@
     def piece(number, away):
         source = kv_all.at[lax.rem(column + away, SIDE) * 2 + core]
         if number == 0:
-            return source.at[:, 0]
+            return source.at[pl.ds(0, 2 * TILES), 0]
         return source.at[span(number - 1), pl.ds(1, SIDE - 1)]
 
     def y_copy(number, side):
@@ -165,6 +165,8 @@
         w_recv.at[0],
     )
 
+    queries = kv_all.at[:, pl.ds(2 * TILES, SLOTS)]
+
     def q_copy(step):
         there = lax.rem(me + step, FRAMES)
         row_there, column_there, core_there = where_is(there)
@@ -172,7 +174,7 @@
             src_ref=q_ref.at[
                 jnp.minimum(row_there, HEADS_HERE - 1), :, column_there * 2 + core_there
             ],
-            dst_ref=q_all.at[:, me],
+            dst_ref=queries.at[column * 2 + core, :, lax.rem(row_there - row + SIDE, SIDE)],
             send_sem=q_send.at[step],
             recv_sem=q_recv,
             device_id=(plane, there),
@@ -232,7 +234,7 @@
     @pl.when(working)
     def _():
         pltpu.make_async_copy(
-            q_ref.at[own_row, :, column * 2 + core], q_all.at[:, me], q_recv
+            q_ref.at[own_row, :, column * 2 + core], queries.at[column * 2 + core, :, 0], q_recv
         ).start()
         own_copy.wait()
         core_copy(0, 0).start()
@@ -265,8 +267,8 @@
 
     @pl.when(working)
     def _():
-        pltpu.make_async_copy(q_all, q_all, q_recv).wait()
-        other = kv_all.at[pl.ds(0, SIDE)]
+        pltpu.make_async_copy(queries, queries, q_recv).wait()
+        other = kv_all.at[pl.ds(0, SIDE), pl.ds(0, 2 * TILES)]
         pltpu.make_async_copy(other, other, core_recv).wait()
         for number in range(PARTS + 1):
             for side in range(2):
@@ -287,12 +289,11 @@
     return pl.pallas_call(
         spread_kernel,
         out_shape=(
-            jax.ShapeDtypeStruct((SLOTS, FRAMES, SPOTS, DH), BF16),
-            jax.ShapeDtypeStruct((WORKERS, 2 * TILES, SIDE, SPOTS, DH), BF16),
+            jax.ShapeDtypeStruct((WORKERS, 2 * TILES + SLOTS, SIDE, SPOTS, DH), BF16),
             jax.ShapeDtypeStruct((depth * PLANES, columns // PLANES), BF16),
         ),
         in_specs=[pl.BlockSpec(memory_space=pl.ANY)] * 3,
-        out_specs=(pl.BlockSpec(memory_space=pl.ANY),) * 3,
+        out_specs=(pl.BlockSpec(memory_space=pl.ANY),) * 2,
         scratch_shapes=[
             pltpu.SemaphoreType.DMA((FRAMES,)),
             pltpu.SemaphoreType.DMA,
@@ -317,18 +318,19 @@
 
 
 def attend_kernel(
-    list_ref, q_ref, kv_hbm, o_ref, kv_ref, keys_ref, values_ref, base_ref, peak_ref, sum_ref,
+    list_ref, kv_hbm, o_ref, kv_ref, q_ref, keys_ref, base_ref, peak_ref, sum_ref,
     slot_of, first_of, listed_of, kv_sem,
 ):
-    def chunk(number, first):
-        rows = pl.ds((first + number * CHUNK) * PIECE, CHUNK * PIECE)
-        return pltpu.make_async_copy(
-            kv_hbm.at[:, rows], kv_ref.at[:, rows], kv_sem.at[number, min(first, 1)]
-        )
-
-    for number in range(TILES // CHUNK):
-        chunk(number, 0).start()
-        chunk(number, TILES).start()
+    def bring(number, first, tiles):
+        rows = pl.ds(first * PIECE, tiles * PIECE)
+        return pltpu.make_async_copy(kv_hbm.at[:, rows], kv_ref.at[:, rows], kv_sem.at[number])
+
+    chunks = TILES // CHUNK
+    moves = [bring(number, number * CHUNK, CHUNK) for number in range(chunks)]
+    moves.append(bring(chunks, 2 * TILES, SLOTS))
+    moves.append(bring(chunks + 1, TILES, TILES))
+    for move in moves:
+        move.start()
 
     _, column, core = where_is(lax.axis_index("ctx"))
 
@@ -369,19 +371,16 @@
     turns = lax.div(total + BESIDE - 1, BESIDE)
     busy = jnp.where(total > 0, 1, 0)
 
-    values_ref[TILES] = jnp.zeros((TILE, DH), BF16)
-
     def unpack(step):
         for u in range(GROUP):
             tile = step * GROUP + u
             keys_ref[tile] = tile_at(tile).T
-            values_ref[tile] = tile_at(TILES + tile)
-
-    for number in range(TILES // CHUNK):
-        chunk(number, 0).wait()
-        chunk(number, TILES).wait()
+
+    for number in range(chunks):
+        moves[number].wait()
         steps = CHUNK // GROUP
         loop(busy * steps, lambda step: unpack(step + number * steps))
+    moves[chunks].wait()
 
     def set_base(slot, base):
         base_ref[slot] = jnp.broadcast_to(base * SCALE2, (TILE, TILE))
@@ -390,10 +389,13 @@
         for u in range(BESIDE):
             slot = step * BESIDE + u
             own = keys_ref[slot * WORKERS + column * 2 + core]
-            scores = jnp.dot(q_ref[rows_of(slot), :], own, preferred_element_type=F32)
+            query = tile_at(2 * TILES + slot)
+            q_ref[rows_of(slot), :] = query
+            scores = jnp.dot(query, own, preferred_element_type=F32)
             set_base(slot, jnp.max(scores, axis=1, keepdims=True))
 
     loop(busy * (SLOTS // BESIDE), own_base)
+    moves[chunks + 1].wait()
 
     def tiles_of(number):
         slot, first = slot_of[number], first_of[number]
@@ -410,13 +412,12 @@
             slot, tiles = tiles_of(number)
             listed = listed_of[number]
             base = base_ref[slot]
-            base = jnp.concatenate([base, base], axis=1)
+            scores = scores_of(slot, tiles)
             weights, values = [], []
-            for u in range(0, GROUP, 2):
-                scores = scores_of(slot, tiles[u : u + 2])
-                weights.append(jnp.exp2(scores * SCALE2 - base).astype(BF16))
             for u in range(GROUP):
-                value = values_ref[jnp.where(u < listed, tiles[u], TILES)]
+                part = scores[:, u * TILE : (u + 1) * TILE]
+                weights.append(jnp.exp2(part * SCALE2 - base).astype(BF16))
+                value = jnp.where(u < listed, tile_at(TILES + tiles[u]), 0).astype(BF16)
                 ones = jnp.where(u < listed, 1.0, 0.0).astype(BF16)
                 ones = jnp.broadcast_to(ones, (TILE, DH))
                 values.append(jnp.concatenate([value, ones], axis=1))
@@ -467,31 +468,27 @@
     loop(busy * (SLOTS // BESIDE), finish)
 
 
-def attend(lists, query, kv):
+def attend(lists, kv):
     most = SLOTS * (TILES // GROUP) + BESIDE
     return pl.pallas_call(
         attend_kernel,
-        out_shape=jax.ShapeDtypeStruct(query.shape, BF16),
-        in_specs=[
-            pl.BlockSpec(memory_space=pltpu.SMEM),
-            pl.BlockSpec(memory_space=pltpu.VMEM),
-            pl.BlockSpec(memory_space=pl.ANY),
-        ],
+        out_shape=jax.ShapeDtypeStruct((SLOTS * TILE, DH), BF16),
+        in_specs=[pl.BlockSpec(memory_space=pltpu.SMEM), pl.BlockSpec(memory_space=pl.ANY)],
         out_specs=pl.BlockSpec(memory_space=pltpu.VMEM),
         scratch_shapes=[
             pltpu.VMEM(kv.shape, BF16),
+            pltpu.VMEM((SLOTS * TILE, DH), BF16),
             pltpu.VMEM((TILES, DH, TILE), BF16),
-            pltpu.VMEM((TILES + 1, TILE, DH), BF16),
             pltpu.VMEM((SLOTS, TILE, TILE), F32),
             pltpu.VMEM((SLOTS, TILE, TILE), F32),
             pltpu.VMEM((SLOTS, TILE, 2 * DH), F32),
             pltpu.SMEM((most,), jnp.int32),
             pltpu.SMEM((most,), jnp.int32),
             pltpu.SMEM((most,), jnp.int32),
-            pltpu.SemaphoreType.DMA((TILES // CHUNK, 2)),
+            pltpu.SemaphoreType.DMA((TILES // CHUNK + 2,)),
         ],
-        compiler_params=pltpu.CompilerParams(vmem_limit_bytes=57 * 1024 * 1024),
-    )(lists, query, kv)
+        compiler_params=pltpu.CompilerParams(vmem_limit_bytes=50 * 1024 * 1024),
+    )(lists, kv)
 
 
 def collect_kernel(o_ref, attn, send, recv, x_send, x_recv):
@@ -515,10 +512,15 @@
     mine = jnp.minimum(row, HEADS_HERE - 1)
     goal = attn.at[plane * HEADS_HERE + mine, :, column * 2 + core]
 
+    def rows_for(there):
+        row_there, column_there, core_there = where_is(there)
+        above = lax.rem(row - row_there + SIDE, SIDE)
+        return o_ref.at[:, column_there * 2 + core_there, above]
+
     def back(step):
         there = lax.rem(me + step, FRAMES)
         return pltpu.make_async_remote_copy(
-            src_ref=o_ref.at[:, there],
+            src_ref=rows_for(there),
             dst_ref=goal,
             send_sem=send.at[step],
             recv_sem=recv.at[mine],
@@ -539,7 +541,7 @@
     @pl.when(working)
     def _():
         lax.fori_loop(1, FRAMES, start, 0)
-        pltpu.make_async_copy(o_ref.at[:, me], goal, recv.at[mine]).start()
+        pltpu.make_async_copy(rows_for(me), goal, recv.at[mine]).start()
 
     cut = SLOTS // 2
 
@@ -706,15 +708,13 @@
 def body(queries, key_rows, value_rows, out_weight, tile_masks, head_pattern):
     rows = queries.shape[0]
     q_parts, kv_parts, lists = arrange(head_pattern, tile_masks, queries, key_rows, value_rows)
-    q_all, kv_all, w_all = spread(
+    kv_all, w_all = spread(
         q_parts.reshape(HEADS_HERE, SLOTS, WORKERS, SPOTS, DH),
         kv_parts.reshape(HEADS_HERE, 2 * TILES, SPOTS, DH),
         out_weight,
     )
-    attended = attend(
-        lists, q_all.reshape(SLOTS * TILE, DH), kv_all.reshape(WORKERS, 2 * TILES * PIECE, DH)
-    )
-    attn = collect(attended.reshape(SLOTS, FRAMES, SPOTS, DH))
+    attended = attend(lists, kv_all.reshape(WORKERS, (2 * TILES + SLOTS) * PIECE, DH))
+    attn = collect(attended.reshape(SLOTS, WORKERS, SIDE, SPOTS, DH))
     attn = attn.reshape(PLANES * HEADS_HERE, rows, DH)
     return project(attn, w_all, rows)
 

time: 157 us -> 157 us (level)
    pallas_call x1, Pallas kernels: 64.9 us -> 72.4 us  [collect(): pl.pallas_call(collect_kernel, out_shape=jax.ShapeDtypeStruct((PLANES * H...]
    pallas_call x2, Pallas kernels: 85.2 us -> 79 us  [the longest x1 52.6 us: spread(): pl.pallas_call(spread_kernel, out_shape=(jax.ShapeDtypeStruct((WORKERS, 2...]
where the time goes in v11:
time: 157 us
  Pallas kernels  157 us (100%)
    pallas_call x1, Pallas kernels, collect(): pl.pallas_call(collect_kernel, out_shape=jax.ShapeDtypeStruct((PLANES * H...  72.4 us
    pallas_call x1, Pallas kernels, spread(): pl.pallas_call(spread_kernel, out_shape=(jax.ShapeDtypeStruct((WORKERS, 2...  52.6 us
    pallas_call x1, Pallas kernels, attend(): pl.pallas_call(attend_kernel, out_shape=jax.ShapeDtypeStruct((SLOTS * TIL...  26.4 us
    pallas_call x1, Pallas kernels, arrange(): pl.pallas_call(arrange_kernel, out_shape=(jax.ShapeDtypeStruct((HEADS_HER...  3.32 us

profile of v11, /device:TPU:1, one launch (start us, length us, event | category | flops | bytes accessed | tf_op | source)
XLA Modules:
  0.0 157.1 jit_solution(12732107485385942986)
XLA Ops:
  0.0 3.3 %shard_map.64 = (bf16[3,512,128]{2,1,0:T(8,128)(2,1)}, bf16[3,1024,128]{2,1,0:T(8,128)(2,1)}, s32[17,128]{1,0:T(8,128)}) custom-call(s32[3]{0:T(128)} %pattern_ref.1, s32[2,128,128]{2,1,0:T(8,128)} %mask_hbm.1, bf16[512,384]{1,0:T(8,128)(2,1)} %q_hbm.1, bf16[512,384]{1,0:T(8,128)(2,1)} %k_hbm.1, bf16[512,384]{1,0:T(8,128)(2,1)} %v_hbm.1), custom_call_target="tpu_custom_call" | custom-call | tf_op jit(solution)/shard_map/pallas_call | solution.py:687
  3.3 0.0 copy-start.1
  3.3 52.6 %shard_map.65 = (bf16[8,272,4,4,128]{4,3,2,1,0:T(4,128)(2,1)}, bf16[1536,768]{1,0:T(8,128)(2,1)}) custom-call(bf16[3,16,8,4,128]{4,3,2,1,0:T(4,128)(2,1)} %bitcast.9, bf16[3,256,4,128]{3,2,1,0:T(4,128)(2,1)} %bitcast.8, bf16[384,3072]{1,0:T(8,128)(2,1)} %w_ref.1), custom_call_target="tpu_custom_call" | custom-call | tf_op jit(solution)/shard_map/pallas_call | solution.py:289
  55.9 0.0 copy-done.1
  55.9 0.0 copy-start
  55.9 26.4 %shard_map.66 = bf16[2048,128]{1,0:T(8,128)(2,1)S(1)} custom-call(s32[17,128]{1,0:T(8,128)S(1)} %copy-done.1, bf16[8,4352,128]{2,1,0:T(8,128)(2,1)} %bitcast.7), custom_call_target="tpu_custom_call" | custom-call | tf_op jit(solution)/shard_map/pallas_call | solution.py:473
  82.4 72.4 %shard_map.67 = bf16[12,16,8,4,128]{4,3,2,1,0:T(4,128)(2,1)S(1)} custom-call(bf16[16,8,4,4,128]{4,3,2,1,0:T(4,128)(2,1)S(1)} %bitcast.6), custom_call_target="tpu_custom_call" | custom-call | tf_op jit(solution)/shard_map/pallas_call | solution.py:592
  154.8 0.0 copy-done
  154.8 2.3 %shard_map.68 = bf16[512,768]{1,0:T(8,128)(2,1)} custom-call(bf16[12,512,128]{2,1,0:T(8,128)(2,1)S(1)} %bitcast.5, bf16[1536,768]{1,0:T(8,128)(2,1)S(1)} %copy-done), custom_call_target="tpu_custom_call" | custom-call | tf_op jit(solution)/shard_map/pallas_call | solution.py:623
Async XLA Ops:
  3.3 52.6 %copy-start.1 = (s32[17,128]{1,0:T(8,128)S(1)}, s32[17,128]{1,0:T(8,128)}, u32[]{:S(2)}) copy-start(s32[17,128]{1,0:T(8,128)} %get-tuple-element.10.list_ref) | copy-start | bytes 26116
  55.9 98.9 %copy-start = (bf16[1536,768]{1,0:T(8,128)(2,1)S(1)}, bf16[1536,768]{1,0:T(8,128)(2,1)}, u32[]{:S(2)}) copy-start(bf16[1536,768]{1,0:T(8,128)(2,1)} %get-tuple-element.14.w_ref) | copy-start | bytes 7077892

commit v12 on v11

--- a/solution.py
+++ b/solution.py
@@ -219,12 +219,13 @@
             y_copy(0, side).start()
 
     to_rows(0, lambda copy: copy.start())
+    to_rows(1, lambda copy: copy.start())
     send_small()
 
     def next_rows(part):
         to_rows(part, lambda copy: copy.wait_send())
-        if part + 1 < PARTS:
-            to_rows(part + 1, lambda copy: copy.start())
+        if part + 2 < PARTS:
+            to_rows(part + 2, lambda copy: copy.start())
 
     @pl.when(jnp.logical_not(working))
     def _():
@@ -317,6 +318,15 @@
     )(q_parts, kv_parts, out_weight)
 
 
+def turned_rows(rows):
+    to = lax.broadcasted_iota(jnp.int32, (rows, rows), 0)
+    source = lax.broadcasted_iota(jnp.int32, (rows, rows), 1)
+    group = WORKERS * SPOTS
+    place = lax.div(lax.rem(to, group), SPOTS)
+    wanted = to + (WORKERS - 1 - 2 * place) * SPOTS
+    return jnp.where(source == wanted, 1.0, 0.0).astype(BF16)
+
+
 def attend_kernel(
     list_ref, kv_hbm, o_ref, kv_ref, q_ref, keys_ref, base_ref, peak_ref, sum_ref,
     slot_of, first_of, listed_of, kv_sem,
@@ -388,7 +398,9 @@
     def own_base(step):
         for u in range(BESIDE):
             slot = step * BESIDE + u
-            own = keys_ref[slot * WORKERS + column * 2 + core]
+            place = column * 2 + core
+            late = jnp.where(slot < SLOTS // 2, 0, WORKERS - 1 - 2 * place)
+            own = keys_ref[slot * WORKERS + place + late]
             query = tile_at(2 * TILES + slot)
             q_ref[rows_of(slot), :] = query
             scores = jnp.dot(query, own, preferred_element_type=F32)
@@ -610,12 +622,15 @@
 
 def project_kernel(attn_ref, w_ref, out_ref):
     heads = attn_ref.shape[0]
+    half = out_ref.shape[0] // 2
     wide = jnp.concatenate([attn_ref[h] for h in range(heads)], axis=1)
     block = 256
     for first in range(0, out_ref.shape[1], block):
         columns = slice(first, first + block)
-        out_ref[:, columns] = jnp.dot(
-            wide, w_ref[:, columns], preferred_element_type=F32
+        mixed = jnp.dot(wide, w_ref[:, columns], preferred_element_type=F32).astype(BF16)
+        out_ref[:half, columns] = mixed[:half]
+        out_ref[half:, columns] = jnp.dot(
+            turned_rows(half), mixed[half:], preferred_element_type=F32
         ).astype(BF16)
 
 
@@ -646,7 +661,11 @@
     moves[0].wait()
     pattern = pattern_ref[jnp.minimum(row, HEADS_HERE - 1)]
     masks = []
-    tiles = [slot * WORKERS + column * 2 + core for slot in range(SLOTS)]
+    place = column * 2 + core
+    tiles = [
+        slot * WORKERS + (place if slot < SLOTS // 2 else WORKERS - 1 - place)
+        for slot in range(SLOTS)
+    ]
     for tile in tiles:
         masks.append(jnp.where(row < HEADS_HERE, mask_ref[pattern, pl.ds(tile, 1), :], 0))
     seen = jnp.concatenate(masks, axis=0) == 1
@@ -680,6 +699,10 @@
         move.wait()
         for head in range(HEADS_HERE):
             target[head, first : first + rows, :] = source[:, head * DH : (head + 1) * DH]
+    half = rows // 2
+    later = jnp.dot(turned_rows(half), q_ref[half:, :], preferred_element_type=F32).astype(BF16)
+    for head in range(HEADS_HERE):
+        q_out[head, half:, :] = later[:, head * DH : (head + 1) * DH]
 
 
 def arrange(head_pattern, tile_masks, queries, key_rows, value_rows):

time: 157 us -> 155 us (0.987)
  Pallas kernels: 157 us -> 155 us
    pallas_call x1, Pallas kernels: 72.4 us -> 67.1 us  [collect(): pl.pallas_call(collect_kernel, out_shape=jax.ShapeDtypeStruct((PLANES * H...]
    pallas_call x1, Pallas kernels: 52.6 us -> 54.7 us  [spread(): pl.pallas_call(spread_kernel, out_shape=(jax.ShapeDtypeStruct((WORKERS, 2...]
where the time goes in v12:
time: 155 us
  Pallas kernels  155 us (100%)
    pallas_call x1, Pallas kernels, collect(): pl.pallas_call(collect_kernel, out_shape=jax.ShapeDtypeStruct((PLANES * H...  67.1 us
    pallas_call x1, Pallas kernels, spread(): pl.pallas_call(spread_kernel, out_shape=(jax.ShapeDtypeStruct((WORKERS, 2...  54.7 us
    pallas_call x1, Pallas kernels, attend(): pl.pallas_call(attend_kernel, out_shape=jax.ShapeDtypeStruct((SLOTS * TIL...  25.6 us
    pallas_call x1, Pallas kernels, project(): pl.pallas_call(project_kernel, out_shape=jax.ShapeDtypeStruct((rows, weig...  3.68 us
    pallas_call x1, Pallas kernels, arrange(): pl.pallas_call(arrange_kernel, out_shape=(jax.ShapeDtypeStruct((HEADS_HER...  3.51 us

profile of v12, /device:TPU:1, one launch (start us, length us, event | category | flops | bytes accessed | tf_op | source)
XLA Modules:
  0.0 154.6 jit_solution(13283759513456275660)
XLA Ops:
  0.0 3.5 %shard_map.64 = (bf16[3,512,128]{2,1,0:T(8,128)(2,1)}, bf16[3,1024,128]{2,1,0:T(8,128)(2,1)}, s32[17,128]{1,0:T(8,128)}) custom-call(s32[3]{0:T(128)} %pattern_ref.1, s32[2,128,128]{2,1,0:T(8,128)} %mask_hbm.1, bf16[512,384]{1,0:T(8,128)(2,1)} %q_hbm.1, bf16[512,384]{1,0:T(8,128)(2,1)} %k_hbm.1, bf16[512,384]{1,0:T(8,128)(2,1)} %v_hbm.1), custom_call_target="tpu_custom_call" | custom-call | tf_op jit(solution)/shard_map/pallas_call | solution.py:710
  3.5 0.0 copy-start.1
  3.5 54.7 %shard_map.65 = (bf16[8,272,4,4,128]{4,3,2,1,0:T(4,128)(2,1)}, bf16[1536,768]{1,0:T(8,128)(2,1)}) custom-call(bf16[3,16,8,4,128]{4,3,2,1,0:T(4,128)(2,1)} %bitcast.9, bf16[3,256,4,128]{3,2,1,0:T(4,128)(2,1)} %bitcast.8, bf16[384,3072]{1,0:T(8,128)(2,1)} %w_ref.1), custom_call_target="tpu_custom_call" | custom-call | tf_op jit(solution)/shard_map/pallas_call | solution.py:290
  58.2 0.0 copy-done.1
  58.2 0.0 copy-start
  58.3 25.6 %shard_map.66 = bf16[2048,128]{1,0:T(8,128)(2,1)S(1)} custom-call(s32[17,128]{1,0:T(8,128)S(1)} %copy-done.1, bf16[8,4352,128]{2,1,0:T(8,128)(2,1)} %bitcast.7), custom_call_target="tpu_custom_call" | custom-call | tf_op jit(solution)/shard_map/pallas_call | solution.py:485
  83.8 67.1 %shard_map.67 = bf16[12,16,8,4,128]{4,3,2,1,0:T(4,128)(2,1)S(1)} custom-call(bf16[16,8,4,4,128]{4,3,2,1,0:T(4,128)(2,1)S(1)} %bitcast.6), custom_call_target="tpu_custom_call" | custom-call | tf_op jit(solution)/shard_map/pallas_call | solution.py:604
  151.0 0.0 copy-done
  151.0 3.7 %shard_map.68 = bf16[512,768]{1,0:T(8,128)(2,1)} custom-call(bf16[12,512,128]{2,1,0:T(8,128)(2,1)S(1)} %bitcast.5, bf16[1536,768]{1,0:T(8,128)(2,1)S(1)} %copy-done), custom_call_target="tpu_custom_call" | custom-call | tf_op jit(solution)/shard_map/pallas_call | solution.py:638
Async XLA Ops:
  3.5 54.7 %copy-start.1 = (s32[17,128]{1,0:T(8,128)S(1)}, s32[17,128]{1,0:T(8,128)}, u32[]{:S(2)}) copy-start(s32[17,128]{1,0:T(8,128)} %get-tuple-element.10.list_ref) | copy-start | bytes 26116
  58.2 92.7 %copy-start = (bf16[1536,768]{1,0:T(8,128)(2,1)S(1)}, bf16[1536,768]{1,0:T(8,128)(2,1)}, u32[]{:S(2)}) copy-start(bf16[1536,768]{1,0:T(8,128)(2,1)} %get-tuple-element.14.w_ref) | copy-start | bytes 7077892

commit v13 on v12

--- a/solution.py
+++ b/solution.py
@@ -18,8 +18,8 @@
 HEADS_HERE = 3
 WORKERS = 2 * SIDE
 SLOTS = TILES // WORKERS
-PARTS = 4
-PART = 2 * TILES // PARTS
+SIZES = (80, 80, 64, 32)
+PARTS = len(SIZES)
 PIECE = TILE // WORKERS
 GROUP = 8
 CHUNK = 32
@@ -69,7 +69,7 @@
     pl.semaphore_wait(barrier, FRAMES - 1 + PLANES - 1)
 
     def span(part):
-        return pl.ds(part * PART, PART)
+        return pl.ds(sum(SIZES[:part]), SIZES[part])
 
     own_copy = pltpu.make_async_copy(
         kv_ref.at[own_row], kv_all.at[column * 2 + core, pl.ds(0, 2 * TILES), 0], own_sem
@@ -104,12 +104,10 @@
 
     def far_copy(number, side):
         source = kv_all.at[lax.rem(column + sides[1 - side], SIDE) * 2 + core]
-        if number == 0:
-            chunk = source.at[pl.ds(side * TILES, TILES), 0]
-        else:
-            chunk = source.at[
-                pl.ds((number - 1) * PART + side * (PART // 2), PART // 2), pl.ds(1, SIDE - 1)
-            ]
+        first, count = (0, 2 * TILES) if number == 0 else (sum(SIZES[: number - 1]), SIZES[number - 1])
+        share = count * 3 // 8
+        tiles = pl.ds(first + share, count - share) if side else pl.ds(first, share)
+        chunk = source.at[tiles, 0] if number == 0 else source.at[tiles, pl.ds(1, SIDE - 1)]
         return pltpu.make_async_remote_copy(
             src_ref=chunk,
             dst_ref=chunk,
@@ -219,13 +217,12 @@
             y_copy(0, side).start()
 
     to_rows(0, lambda copy: copy.start())
-    to_rows(1, lambda copy: copy.start())
     send_small()
 
     def next_rows(part):
         to_rows(part, lambda copy: copy.wait_send())
-        if part + 2 < PARTS:
-            to_rows(part + 2, lambda copy: copy.start())
+        if part + 1 < PARTS:
+            to_rows(part + 1, lambda copy: copy.start())
 
     @pl.when(jnp.logical_not(working))
     def _():
@@ -627,11 +624,14 @@
     block = 256
     for first in range(0, out_ref.shape[1], block):
         columns = slice(first, first + block)
-        mixed = jnp.dot(wide, w_ref[:, columns], preferred_element_type=F32).astype(BF16)
-        out_ref[:half, columns] = mixed[:half]
-        out_ref[half:, columns] = jnp.dot(
-            turned_rows(half), mixed[half:], preferred_element_type=F32
-        ).astype(BF16)
+        mixed = jnp.dot(wide, w_ref[:, columns], preferred_element_type=F32)
+        out_ref[:half, columns] = mixed[:half].astype(BF16)
+        group, pair = WORKERS * SPOTS, 2 * SPOTS
+        blocks = []
+        for start in range(half, 2 * half, group):
+            for last in range(start + group, start, -pair):
+                blocks.append(pltpu.roll(mixed[last - pair : last], SPOTS, 0))
+        out_ref[half:, columns] = jnp.concatenate(blocks, axis=0).astype(BF16)
 
 
 def project(attn, weight, rows):

time: 155 us -> 160 us (1.032)
  Pallas kernels: 155 us -> 160 us
    pallas_call x1, Pallas kernels: 67.1 us -> 71 us  [collect(): pl.pallas_call(collect_kernel, out_shape=jax.ShapeDtypeStruct((PLANES * H...]
    pallas_call x1, Pallas kernels: 25.6 us -> 28.1 us  [attend(): pl.pallas_call(attend_kernel, out_shape=jax.ShapeDtypeStruct((SLOTS * TIL...]
where the time goes in v13:
time: 160 us
  Pallas kernels  160 us (100%)
    pallas_call x1, Pallas kernels, collect(): pl.pallas_call(collect_kernel, out_shape=jax.ShapeDtypeStruct((PLANES * H...  71 us
    pallas_call x1, Pallas kernels, spread(): pl.pallas_call(spread_kernel, out_shape=(jax.ShapeDtypeStruct((WORKERS, 2...  55 us
    pallas_call x1, Pallas kernels, attend(): pl.pallas_call(attend_kernel, out_shape=jax.ShapeDtypeStruct((SLOTS * TIL...  28.1 us
    pallas_call x1, Pallas kernels, arrange(): pl.pallas_call(arrange_kernel, out_shape=(jax.ShapeDtypeStruct((HEADS_HER...  3.51 us

profile of v13, /device:TPU:1, one launch (start us, length us, event | category | flops | bytes accessed | tf_op | source)
XLA Modules:
  0.0 160.0 jit_solution(4252991554709255640)
XLA Ops:
  0.0 3.5 %shard_map.64 = (bf16[3,512,128]{2,1,0:T(8,128)(2,1)}, bf16[3,1024,128]{2,1,0:T(8,128)(2,1)}, s32[17,128]{1,0:T(8,128)}) custom-call(s32[3]{0:T(128)} %pattern_ref.1, s32[2,128,128]{2,1,0:T(8,128)} %mask_hbm.1, bf16[512,384]{1,0:T(8,128)(2,1)} %q_hbm.1, bf16[512,384]{1,0:T(8,128)(2,1)} %k_hbm.1, bf16[512,384]{1,0:T(8,128)(2,1)} %v_hbm.1), custom_call_target="tpu_custom_call" | custom-call | tf_op jit(solution)/shard_map/pallas_call | solution.py:710
  3.5 0.0 copy-start.1
  3.5 55.0 %shard_map.65 = (bf16[8,272,4,4,128]{4,3,2,1,0:T(4,128)(2,1)}, bf16[1536,768]{1,0:T(8,128)(2,1)}) custom-call(bf16[3,16,8,4,128]{4,3,2,1,0:T(4,128)(2,1)} %bitcast.9, bf16[3,256,4,128]{3,2,1,0:T(4,128)(2,1)} %bitcast.8, bf16[384,3072]{1,0:T(8,128)(2,1)} %w_ref.1), custom_call_target="tpu_custom_call" | custom-call | tf_op jit(solution)/shard_map/pallas_call | solution.py:287
  58.5 0.0 copy-done.1
  58.5 0.0 copy-start
  58.5 28.1 %shard_map.66 = bf16[2048,128]{1,0:T(8,128)(2,1)S(1)} custom-call(s32[17,128]{1,0:T(8,128)S(1)} %copy-done.1, bf16[8,4352,128]{2,1,0:T(8,128)(2,1)} %bitcast.7), custom_call_target="tpu_custom_call" | custom-call | tf_op jit(solution)/shard_map/pallas_call | solution.py:482
  86.7 71.0 %shard_map.67 = bf16[12,16,8,4,128]{4,3,2,1,0:T(4,128)(2,1)S(1)} custom-call(bf16[16,8,4,4,128]{4,3,2,1,0:T(4,128)(2,1)S(1)} %bitcast.6), custom_call_target="tpu_custom_call" | custom-call | tf_op jit(solution)/shard_map/pallas_call | solution.py:601
  157.7 0.0 copy-done
  157.7 2.3 %shard_map.68 = bf16[512,768]{1,0:T(8,128)(2,1)} custom-call(bf16[12,512,128]{2,1,0:T(8,128)(2,1)S(1)} %bitcast.5, bf16[1536,768]{1,0:T(8,128)(2,1)S(1)} %copy-done), custom_call_target="tpu_custom_call" | custom-call | tf_op jit(solution)/shard_map/pallas_call | solution.py:638
Async XLA Ops:
  3.5 55.0 %copy-start.1 = (s32[17,128]{1,0:T(8,128)S(1)}, s32[17,128]{1,0:T(8,128)}, u32[]{:S(2)}) copy-start(s32[17,128]{1,0:T(8,128)} %get-tuple-element.10.list_ref) | copy-start | bytes 26116
  58.5 99.2 %copy-start = (bf16[1536,768]{1,0:T(8,128)(2,1)S(1)}, bf16[1536,768]{1,0:T(8,128)(2,1)}, u32[]{:S(2)}) copy-start(bf16[1536,768]{1,0:T(8,128)(2,1)} %get-tuple-element.14.w_ref) | copy-start | bytes 7077892

commit v14 on v13

--- a/solution.py
+++ b/solution.py
@@ -18,7 +18,7 @@
 HEADS_HERE = 3
 WORKERS = 2 * SIDE
 SLOTS = TILES // WORKERS
-SIZES = (80, 80, 64, 32)
+SIZES = (64, 64, 64, 64)
 PARTS = len(SIZES)
 PIECE = TILE // WORKERS
 GROUP = 8
@@ -105,7 +105,7 @@
     def far_copy(number, side):
         source = kv_all.at[lax.rem(column + sides[1 - side], SIDE) * 2 + core]
         first, count = (0, 2 * TILES) if number == 0 else (sum(SIZES[: number - 1]), SIZES[number - 1])
-        share = count * 3 // 8
+        share = count * 5 // 8
         tiles = pl.ds(first + share, count - share) if side else pl.ds(first, share)
         chunk = source.at[tiles, 0] if number == 0 else source.at[tiles, pl.ds(1, SIDE - 1)]
         return pltpu.make_async_remote_copy(

time: 160 us -> 155 us (0.969)
  Pallas kernels: 160 us -> 154 us
    pallas_call x1, Pallas kernels: 71 us -> 63.9 us  [collect(): pl.pallas_call(collect_kernel, out_shape=jax.ShapeDtypeStruct((PLANES * H...]
where the time goes in v14:
time: 155 us; the launch traced here: 154 us
  Pallas kernels  154 us (99%)
    pallas_call x1, Pallas kernels, collect(): pl.pallas_call(collect_kernel, out_shape=jax.ShapeDtypeStruct((PLANES * H...  63.9 us
    pallas_call x1, Pallas kernels, spread(): pl.pallas_call(spread_kernel, out_shape=(jax.ShapeDtypeStruct((WORKERS, 2...  55.4 us
    pallas_call x1, Pallas kernels, attend(): pl.pallas_call(attend_kernel, out_shape=jax.ShapeDtypeStruct((SLOTS * TIL...  29.1 us
    pallas_call x1, Pallas kernels, arrange(): pl.pallas_call(arrange_kernel, out_shape=(jax.ShapeDtypeStruct((HEADS_HER...  3.51 us

profile of v14, /device:TPU:1, one launch (start us, length us, event | category | flops | bytes accessed | tf_op | source)
XLA Modules:
  0.0 154.2 jit_solution(6249709553685741849)
XLA Ops:
  0.0 3.5 %shard_map.64 = (bf16[3,512,128]{2,1,0:T(8,128)(2,1)}, bf16[3,1024,128]{2,1,0:T(8,128)(2,1)}, s32[17,128]{1,0:T(8,128)}) custom-call(s32[3]{0:T(128)} %pattern_ref.1, s32[2,128,128]{2,1,0:T(8,128)} %mask_hbm.1, bf16[512,384]{1,0:T(8,128)(2,1)} %q_hbm.1, bf16[512,384]{1,0:T(8,128)(2,1)} %k_hbm.1, bf16[512,384]{1,0:T(8,128)(2,1)} %v_hbm.1), custom_call_target="tpu_custom_call" | custom-call | tf_op jit(solution)/shard_map/pallas_call | solution.py:710
  3.5 0.0 copy-start.1
  3.5 55.4 %shard_map.65 = (bf16[8,272,4,4,128]{4,3,2,1,0:T(4,128)(2,1)}, bf16[1536,768]{1,0:T(8,128)(2,1)}) custom-call(bf16[3,16,8,4,128]{4,3,2,1,0:T(4,128)(2,1)} %bitcast.9, bf16[3,256,4,128]{3,2,1,0:T(4,128)(2,1)} %bitcast.8, bf16[384,3072]{1,0:T(8,128)(2,1)} %w_ref.1), custom_call_target="tpu_custom_call" | custom-call | tf_op jit(solution)/shard_map/pallas_call | solution.py:287
  58.9 0.0 copy-done.1
  58.9 0.0 copy-start
  58.9 29.1 %shard_map.66 = bf16[2048,128]{1,0:T(8,128)(2,1)S(1)} custom-call(s32[17,128]{1,0:T(8,128)S(1)} %copy-done.1, bf16[8,4352,128]{2,1,0:T(8,128)(2,1)} %bitcast.7), custom_call_target="tpu_custom_call" | custom-call | tf_op jit(solution)/shard_map/pallas_call | solution.py:482
  88.0 63.9 %shard_map.67 = bf16[12,16,8,4,128]{4,3,2,1,0:T(4,128)(2,1)S(1)} custom-call(bf16[16,8,4,4,128]{4,3,2,1,0:T(4,128)(2,1)S(1)} %bitcast.6), custom_call_target="tpu_custom_call" | custom-call | tf_op jit(solution)/shard_map/pallas_call | solution.py:601
  151.9 0.0 copy-done
  151.9 2.3 %shard_map.68 = bf16[512,768]{1,0:T(8,128)(2,1)} custom-call(bf16[12,512,128]{2,1,0:T(8,128)(2,1)S(1)} %bitcast.5, bf16[1536,768]{1,0:T(8,128)(2,1)S(1)} %copy-done), custom_call_target="tpu_custom_call" | custom-call | tf_op jit(solution)/shard_map/pallas_call | solution.py:638
Async XLA Ops:
  3.5 55.4 %copy-start.1 = (s32[17,128]{1,0:T(8,128)S(1)}, s32[17,128]{1,0:T(8,128)}, u32[]{:S(2)}) copy-start(s32[17,128]{1,0:T(8,128)} %get-tuple-element.10.list_ref) | copy-start | bytes 26116
  58.9 93.0 %copy-start = (bf16[1536,768]{1,0:T(8,128)(2,1)S(1)}, bf16[1536,768]{1,0:T(8,128)(2,1)}, u32[]{:S(2)}) copy-start(bf16[1536,768]{1,0:T(8,128)(2,1)} %get-tuple-element.14.w_ref) | copy-start | bytes 7077892

commit v15 on v14

--- a/solution.py
+++ b/solution.py
@@ -42,7 +42,7 @@
 def spread_kernel(
     q_ref, kv_ref, w_ref, kv_all, w_all,
     q_send, q_recv, z_send, z_recv, y_send, y_recv, far_send, far_recv,
-    core_send, core_recv, w_send, w_recv, w_core_send, w_core_recv, own_sem,
+    core_send, core_recv, last_recv, w_send, w_recv, w_core_send, w_core_recv, own_sem,
 ):
     plane = lax.axis_index("heads")
     me = lax.axis_index("ctx")
@@ -102,18 +102,21 @@
             device_id_type=MESH,
         )
 
-    def far_copy(number, side):
+    def far_copy(number, side, over=0):
         source = kv_all.at[lax.rem(column + sides[1 - side], SIDE) * 2 + core]
         first, count = (0, 2 * TILES) if number == 0 else (sum(SIZES[: number - 1]), SIZES[number - 1])
-        share = count * 5 // 8
+        share = count // 2
         tiles = pl.ds(first + share, count - share) if side else pl.ds(first, share)
         chunk = source.at[tiles, 0] if number == 0 else source.at[tiles, pl.ds(1, SIDE - 1)]
         return pltpu.make_async_remote_copy(
             src_ref=chunk,
             dst_ref=chunk,
-            send_sem=far_send.at[number, side],
-            recv_sem=far_recv.at[number, side],
-            device_id=(plane, device_at(row, column + sides[side], core)),
+            send_sem=far_send.at[number, side, over],
+            recv_sem=far_recv.at[number, side, over],
+            device_id=(
+                plane,
+                device_at(row, column + sides[side], core + over - 2 * core * over),
+            ),
             device_id_type=MESH,
         )
 
@@ -122,7 +125,7 @@
             src_ref=piece(number, away),
             dst_ref=piece(number, away),
             send_sem=core_send.at[number, away],
-            recv_sem=core_recv,
+            recv_sem=last_recv if number == PARTS else core_recv,
             device_id=(plane, device_at(row, column, 1 - core)),
             device_id_type=MESH,
         )
@@ -241,6 +244,8 @@
             for side in range(2):
                 y_copy(number, side).wait_recv()
                 far_copy(number, side).start()
+                if number == PARTS:
+                    far_copy(number, side, 1).start()
             for side in range(2):
                 core_copy(number, sides[1 - side]).start()
 
@@ -257,7 +262,10 @@
         for number in range(PARTS + 1):
             for side in range(2):
                 far_copy(number, side).wait_recv()
-            core_copy(number, 2).start()
+                if number == PARTS:
+                    far_copy(number, side, 1).wait_recv()
+            if number < PARTS:
+                core_copy(number, 2).start()
 
     for hop in range(1, PLANES):
         w_copy(hop).wait_recv()
@@ -266,14 +274,21 @@
     @pl.when(working)
     def _():
         pltpu.make_async_copy(queries, queries, q_recv).wait()
-        other = kv_all.at[pl.ds(0, SIDE), pl.ds(0, 2 * TILES)]
+        last = SIZES[-1]
+        early = (2 * TILES + (2 * TILES - last) * (SIDE - 1)) // SIDE
+        other = kv_all.at[pl.ds(0, SIDE), pl.ds(0, early)]
         pltpu.make_async_copy(other, other, core_recv).wait()
+        other = kv_all.at[pl.ds(0, SIDE - 1), pl.ds(0, last), pl.ds(0, SIDE - 1)]
+        pltpu.make_async_copy(other, other, last_recv).wait()
         for number in range(PARTS + 1):
             for side in range(2):
                 y_copy(number, side).wait_send()
                 far_copy(number, side).wait_send()
+                if number == PARTS:
+                    far_copy(number, side, 1).wait_send()
             for away in range(SIDE):
-                core_copy(number, away).wait_send()
+                if number < PARTS or away != 2:
+                    core_copy(number, away).wait_send()
 
     own_w.wait()
     lax.fori_loop(1, FRAMES, sent_q, 0)
@@ -299,9 +314,10 @@
             pltpu.SemaphoreType.DMA((PARTS, SIDE)),
             pltpu.SemaphoreType.DMA((PARTS + 1, 2)),
             pltpu.SemaphoreType.DMA((PARTS + 1, 2)),
-            pltpu.SemaphoreType.DMA((PARTS + 1, 2)),
-            pltpu.SemaphoreType.DMA((PARTS + 1, 2)),
+            pltpu.SemaphoreType.DMA((PARTS + 1, 2, 2)),
+            pltpu.SemaphoreType.DMA((PARTS + 1, 2, 2)),
             pltpu.SemaphoreType.DMA((PARTS + 1, SIDE)),
+            pltpu.SemaphoreType.DMA,
             pltpu.SemaphoreType.DMA,
             pltpu.SemaphoreType.DMA((PLANES,)),
             pltpu.SemaphoreType.DMA((PLANES,)),

time: 155 us -> 155 us (level)
    pallas_call x1, Pallas kernels: 63.9 us -> 67 us  [collect(): pl.pallas_call(collect_kernel, out_shape=jax.ShapeDtypeStruct((PLANES * H...]
    pallas_call x1, Pallas kernels: 29.1 us -> 27.3 us  [attend(): pl.pallas_call(attend_kernel, out_shape=jax.ShapeDtypeStruct((SLOTS * TIL...]
where the time goes in v15:
time: 155 us; the launch traced here: 154 us
  Pallas kernels  154 us (99%)
    pallas_call x1, Pallas kernels, collect(): pl.pallas_call(collect_kernel, out_shape=jax.ShapeDtypeStruct((PLANES * H...  67 us
    pallas_call x1, Pallas kernels, spread(): pl.pallas_call(spread_kernel, out_shape=(jax.ShapeDtypeStruct((WORKERS, 2...  54 us
    pallas_call x1, Pallas kernels, attend(): pl.pallas_call(attend_kernel, out_shape=jax.ShapeDtypeStruct((SLOTS * TIL...  27.3 us
    pallas_call x1, Pallas kernels, arrange(): pl.pallas_call(arrange_kernel, out_shape=(jax.ShapeDtypeStruct((HEADS_HER...  3.51 us

profile of v15, /device:TPU:1, one launch (start us, length us, event | category | flops | bytes accessed | tf_op | source)
XLA Modules:
  0.0 154.1 jit_solution(17110737823253922784)
XLA Ops:
  0.0 3.5 %shard_map.64 = (bf16[3,512,128]{2,1,0:T(8,128)(2,1)}, bf16[3,1024,128]{2,1,0:T(8,128)(2,1)}, s32[17,128]{1,0:T(8,128)}) custom-call(s32[3]{0:T(128)} %pattern_ref.1, s32[2,128,128]{2,1,0:T(8,128)} %mask_hbm.1, bf16[512,384]{1,0:T(8,128)(2,1)} %q_hbm.1, bf16[512,384]{1,0:T(8,128)(2,1)} %k_hbm.1, bf16[512,384]{1,0:T(8,128)(2,1)} %v_hbm.1), custom_call_target="tpu_custom_call" | custom-call | tf_op jit(solution)/shard_map/pallas_call | solution.py:726
  3.5 0.0 copy-start.1
  3.5 54.0 %shard_map.65 = (bf16[8,272,4,4,128]{4,3,2,1,0:T(4,128)(2,1)}, bf16[1536,768]{1,0:T(8,128)(2,1)}) custom-call(bf16[3,16,8,4,128]{4,3,2,1,0:T(4,128)(2,1)} %bitcast.9, bf16[3,256,4,128]{3,2,1,0:T(4,128)(2,1)} %bitcast.8, bf16[384,3072]{1,0:T(8,128)(2,1)} %w_ref.1), custom_call_target="tpu_custom_call" | custom-call | tf_op jit(solution)/shard_map/pallas_call | solution.py:302
  57.6 0.0 copy-done.1
  57.6 0.0 copy-start
  57.6 27.3 %shard_map.66 = bf16[2048,128]{1,0:T(8,128)(2,1)S(1)} custom-call(s32[17,128]{1,0:T(8,128)S(1)} %copy-done.1, bf16[8,4352,128]{2,1,0:T(8,128)(2,1)} %bitcast.7), custom_call_target="tpu_custom_call" | custom-call | tf_op jit(solution)/shard_map/pallas_call | solution.py:498
  84.8 67.0 %shard_map.67 = bf16[12,16,8,4,128]{4,3,2,1,0:T(4,128)(2,1)S(1)} custom-call(bf16[16,8,4,4,128]{4,3,2,1,0:T(4,128)(2,1)S(1)} %bitcast.6), custom_call_target="tpu_custom_call" | custom-call | tf_op jit(solution)/shard_map/pallas_call | solution.py:617
  151.8 0.0 copy-done
  151.8 2.3 %shard_map.68 = bf16[512,768]{1,0:T(8,128)(2,1)} custom-call(bf16[12,512,128]{2,1,0:T(8,128)(2,1)S(1)} %bitcast.5, bf16[1536,768]{1,0:T(8,128)(2,1)S(1)} %copy-done), custom_call_target="tpu_custom_call" | custom-call | tf_op jit(solution)/shard_map/pallas_call | solution.py:654
Async XLA Ops:
  3.5 54.0 %copy-start.1 = (s32[17,128]{1,0:T(8,128)S(1)}, s32[17,128]{1,0:T(8,128)}, u32[]{:S(2)}) copy-start(s32[17,128]{1,0:T(8,128)} %get-tuple-element.10.list_ref) | copy-start | bytes 26116
  57.6 94.3 %copy-start = (bf16[1536,768]{1,0:T(8,128)(2,1)S(1)}, bf16[1536,768]{1,0:T(8,128)(2,1)}, u32[]{:S(2)}) copy-start(bf16[1536,768]{1,0:T(8,128)(2,1)} %get-tuple-element.14.w_ref) | copy-start | bytes 7077892

commit v16 on v14

--- a/solution.py
+++ b/solution.py
@@ -105,7 +105,7 @@
     def far_copy(number, side):
         source = kv_all.at[lax.rem(column + sides[1 - side], SIDE) * 2 + core]
         first, count = (0, 2 * TILES) if number == 0 else (sum(SIZES[: number - 1]), SIZES[number - 1])
-        share = count * 5 // 8
+        share = count // 2
         tiles = pl.ds(first + share, count - share) if side else pl.ds(first, share)
         chunk = source.at[tiles, 0] if number == 0 else source.at[tiles, pl.ds(1, SIDE - 1)]
         return pltpu.make_async_remote_copy(

time: 155 us -> 153 us (0.987)
    pallas_call x1, Pallas kernels: 55.4 us -> 52.6 us  [spread(): pl.pallas_call(spread_kernel, out_shape=(jax.ShapeDtypeStruct((WORKERS, 2...]
where the time goes in v16:
time: 153 us
  Pallas kernels  153 us (100%)
    pallas_call x1, Pallas kernels, collect(): pl.pallas_call(collect_kernel, out_shape=jax.ShapeDtypeStruct((PLANES * H...  64.3 us
    pallas_call x1, Pallas kernels, spread(): pl.pallas_call(spread_kernel, out_shape=(jax.ShapeDtypeStruct((WORKERS, 2...  52.6 us
    pallas_call x1, Pallas kernels, attend(): pl.pallas_call(attend_kernel, out_shape=jax.ShapeDtypeStruct((SLOTS * TIL...  29.9 us
    pallas_call x1, Pallas kernels, arrange(): pl.pallas_call(arrange_kernel, out_shape=(jax.ShapeDtypeStruct((HEADS_HER...  3.51 us

profile of v16, /device:TPU:1, one launch (start us, length us, event | category | flops | bytes accessed | tf_op | source)
XLA Modules:
  0.0 152.6 jit_solution(5350797133259033483)
XLA Ops:
  0.0 3.5 %shard_map.64 = (bf16[3,512,128]{2,1,0:T(8,128)(2,1)}, bf16[3,1024,128]{2,1,0:T(8,128)(2,1)}, s32[17,128]{1,0:T(8,128)}) custom-call(s32[3]{0:T(128)} %pattern_ref.1, s32[2,128,128]{2,1,0:T(8,128)} %mask_hbm.1, bf16[512,384]{1,0:T(8,128)(2,1)} %q_hbm.1, bf16[512,384]{1,0:T(8,128)(2,1)} %k_hbm.1, bf16[512,384]{1,0:T(8,128)(2,1)} %v_hbm.1), custom_call_target="tpu_custom_call" | custom-call | tf_op jit(solution)/shard_map/pallas_call | solution.py:710
  3.5 0.0 copy-start.1
  3.5 52.6 %shard_map.65 = (bf16[8,272,4,4,128]{4,3,2,1,0:T(4,128)(2,1)}, bf16[1536,768]{1,0:T(8,128)(2,1)}) custom-call(bf16[3,16,8,4,128]{4,3,2,1,0:T(4,128)(2,1)} %bitcast.9, bf16[3,256,4,128]{3,2,1,0:T(4,128)(2,1)} %bitcast.8, bf16[384,3072]{1,0:T(8,128)(2,1)} %w_ref.1), custom_call_target="tpu_custom_call" | custom-call | tf_op jit(solution)/shard_map/pallas_call | solution.py:287
  56.1 0.0 copy-done.1
  56.1 0.0 copy-start
  56.1 29.9 %shard_map.66 = bf16[2048,128]{1,0:T(8,128)(2,1)S(1)} custom-call(s32[17,128]{1,0:T(8,128)S(1)} %copy-done.1, bf16[8,4352,128]{2,1,0:T(8,128)(2,1)} %bitcast.7), custom_call_target="tpu_custom_call" | custom-call | tf_op jit(solution)/shard_map/pallas_call | solution.py:482
  86.0 64.3 %shard_map.67 = bf16[12,16,8,4,128]{4,3,2,1,0:T(4,128)(2,1)S(1)} custom-call(bf16[16,8,4,4,128]{4,3,2,1,0:T(4,128)(2,1)S(1)} %bitcast.6), custom_call_target="tpu_custom_call" | custom-call | tf_op jit(solution)/shard_map/pallas_call | solution.py:601
  150.3 0.0 copy-done
  150.3 2.3 %shard_map.68 = bf16[512,768]{1,0:T(8,128)(2,1)} custom-call(bf16[12,512,128]{2,1,0:T(8,128)(2,1)S(1)} %bitcast.5, bf16[1536,768]{1,0:T(8,128)(2,1)S(1)} %copy-done), custom_call_target="tpu_custom_call" | custom-call | tf_op jit(solution)/shard_map/pallas_call | solution.py:638
Async XLA Ops:
  3.5 52.6 %copy-start.1 = (s32[17,128]{1,0:T(8,128)S(1)}, s32[17,128]{1,0:T(8,128)}, u32[]{:S(2)}) copy-start(s32[17,128]{1,0:T(8,128)} %get-tuple-element.10.list_ref) | copy-start | bytes 26116
  56.1 94.2 %copy-start = (bf16[1536,768]{1,0:T(8,128)(2,1)S(1)}, bf16[1536,768]{1,0:T(8,128)(2,1)}, u32[]{:S(2)}) copy-start(bf16[1536,768]{1,0:T(8,128)(2,1)} %get-tuple-element.14.w_ref) | copy-start | bytes 7077892

commit v17 on v16

--- a/solution.py
+++ b/solution.py
@@ -23,7 +23,7 @@
 PIECE = TILE // WORKERS
 GROUP = 8
 CHUNK = 32
-BESIDE = 4
+BESIDE = 8
 FAR = 2.0**64
 LOW = -1e30
 SCALE2 = math.log2(math.e) / math.sqrt(DH)

time: 153 us -> 147 us (0.961)
  Pallas kernels: 153 us -> 146 us
    pallas_call x1, Pallas kernels: 29.9 us -> 22.4 us  [attend(): pl.pallas_call(attend_kernel, out_shape=jax.ShapeDtypeStruct((SLOTS * TIL...]
where the time goes in v17:
time: 147 us; the launch traced here: 146 us
  Pallas kernels  146 us (99%)
    pallas_call x1, Pallas kernels, collect(): pl.pallas_call(collect_kernel, out_shape=jax.ShapeDtypeStruct((PLANES * H...  65.2 us
    pallas_call x1, Pallas kernels, spread(): pl.pallas_call(spread_kernel, out_shape=(jax.ShapeDtypeStruct((WORKERS, 2...  52.6 us
    pallas_call x1, Pallas kernels, attend(): pl.pallas_call(attend_kernel, out_shape=jax.ShapeDtypeStruct((SLOTS * TIL...  22.4 us
    pallas_call x1, Pallas kernels, arrange(): pl.pallas_call(arrange_kernel, out_shape=(jax.ShapeDtypeStruct((HEADS_HER...  3.51 us

profile of v17, /device:TPU:1, one launch (start us, length us, event | category | flops | bytes accessed | tf_op | source)
XLA Modules:
  0.0 146.1 jit_solution(9491991783304576259)
XLA Ops:
  0.0 3.5 %shard_map.64 = (bf16[3,512,128]{2,1,0:T(8,128)(2,1)}, bf16[3,1024,128]{2,1,0:T(8,128)(2,1)}, s32[17,128]{1,0:T(8,128)}) custom-call(s32[3]{0:T(128)} %pattern_ref.1, s32[2,128,128]{2,1,0:T(8,128)} %mask_hbm.1, bf16[512,384]{1,0:T(8,128)(2,1)} %q_hbm.1, bf16[512,384]{1,0:T(8,128)(2,1)} %k_hbm.1, bf16[512,384]{1,0:T(8,128)(2,1)} %v_hbm.1), custom_call_target="tpu_custom_call" | custom-call | tf_op jit(solution)/shard_map/pallas_call | solution.py:710
  3.5 0.0 copy-start.1
  3.5 52.6 %shard_map.65 = (bf16[8,272,4,4,128]{4,3,2,1,0:T(4,128)(2,1)}, bf16[1536,768]{1,0:T(8,128)(2,1)}) custom-call(bf16[3,16,8,4,128]{4,3,2,1,0:T(4,128)(2,1)} %bitcast.9, bf16[3,256,4,128]{3,2,1,0:T(4,128)(2,1)} %bitcast.8, bf16[384,3072]{1,0:T(8,128)(2,1)} %w_ref.1), custom_call_target="tpu_custom_call" | custom-call | tf_op jit(solution)/shard_map/pallas_call | solution.py:287
  56.1 0.0 copy-done.1
  56.1 0.0 copy-start
  56.1 22.4 %shard_map.66 = bf16[2048,128]{1,0:T(8,128)(2,1)S(1)} custom-call(s32[17,128]{1,0:T(8,128)S(1)} %copy-done.1, bf16[8,4352,128]{2,1,0:T(8,128)(2,1)} %bitcast.7), custom_call_target="tpu_custom_call" | custom-call | tf_op jit(solution)/shard_map/pallas_call | solution.py:482
  78.5 65.2 %shard_map.67 = bf16[12,16,8,4,128]{4,3,2,1,0:T(4,128)(2,1)S(1)} custom-call(bf16[16,8,4,4,128]{4,3,2,1,0:T(4,128)(2,1)S(1)} %bitcast.6), custom_call_target="tpu_custom_call" | custom-call | tf_op jit(solution)/shard_map/pallas_call | solution.py:601
  143.8 0.0 copy-done
  143.8 2.3 %shard_map.68 = bf16[512,768]{1,0:T(8,128)(2,1)} custom-call(bf16[12,512,128]{2,1,0:T(8,128)(2,1)S(1)} %bitcast.5, bf16[1536,768]{1,0:T(8,128)(2,1)S(1)} %copy-done), custom_call_target="tpu_custom_call" | custom-call | tf_op jit(solution)/shard_map/pallas_call | solution.py:638
Async XLA Ops:
  3.5 52.6 %copy-start.1 = (s32[17,128]{1,0:T(8,128)S(1)}, s32[17,128]{1,0:T(8,128)}, u32[]{:S(2)}) copy-start(s32[17,128]{1,0:T(8,128)} %get-tuple-element.10.list_ref) | copy-start | bytes 26116
  56.1 87.7 %copy-start = (bf16[1536,768]{1,0:T(8,128)(2,1)S(1)}, bf16[1536,768]{1,0:T(8,128)(2,1)}, u32[]{:S(2)}) copy-start(bf16[1536,768]{1,0:T(8,128)(2,1)} %get-tuple-element.14.w_ref) | copy-start | bytes 7077892
